TPU v7x, 512 devices: a whole 4x4x16 slice. The times are simulated.
512 devices in a mesh: rows: 64 (over y, z), cols: 8 (over x, core).
Axes of the slice: x: 4, y: 4, z: 16, core: 2. Of those that a mesh axis runs over, the one named last changes fastest.
Arguments:
- queries: bfloat16 [9216, 768], P('rows', 'cols'), may hold values from -4 to 4
- passages: bfloat16 [9216, 768], P('cols', 'rows'), may hold values from -2 to 2
- positive: int32 [9216], P('rows'), may hold values from 0 to 9215, each once
Outputs:
- query_grad: float32 [9216, 768], P('rows', 'cols')
- passage_grad: float32 [9216, 768], P('cols', 'rows')
Inputs may be any that keep to these rules, and one draw needn't show every extreme that they name: Every passage is the positive of exactly one query.
All inputs are finite; a program needn't handle non-finite values.
Results may differ from a plain program's by a relative error of at most 0.002.
Values may be sent and summed in bfloat16 or wider, within the bound.
No kernel may reach another device: no remote copies, remote signals or barrier semaphores. Data moves between devices by JAX's collectives and lax.ppermute only.
A program may use at most 64 MiB of HBM per device.

v0:
```python
import jax
import jax.numpy as jnp
from jax import lax
from jax.sharding import PartitionSpec as P

logit_scale = 20.0


def body(queries, passages, positive):
    query_full = lax.all_gather(queries, "cols", axis=1, tiled=True)
    passage_full = lax.all_gather(passages, "rows", axis=1, tiled=True)
    pc_local = passage_full.shape[0]
    logit_tile = logit_scale * lax.dot_general(
        query_full, passage_full, (((1,), (1,)), ((), ())), preferred_element_type=jnp.float32
    )
    row_top = lax.pmax(jnp.max(logit_tile, axis=1), "cols")
    row_sum = lax.psum(jnp.sum(jnp.exp(logit_tile - row_top[:, None]), axis=1), "cols")
    col_top = lax.pmax(jnp.max(logit_tile, axis=0), "rows")
    col_sum = lax.psum(jnp.sum(jnp.exp(logit_tile - col_top[None, :]), axis=0), "rows")
    row_lse = row_top + jnp.log(row_sum)
    col_lse = col_top + jnp.log(col_sum)
    column_ids = lax.axis_index("cols") * pc_local + jnp.arange(pc_local, dtype=jnp.int32)
    hit = (positive[:, None] == column_ids[None, :]).astype(jnp.float32)
    dlogits = (
        jnp.exp(logit_tile - row_lse[:, None]) + jnp.exp(logit_tile - col_lse[None, :]) - 2.0 * hit
    ).astype(jnp.bfloat16)
    query_terms = logit_scale * jnp.dot(dlogits, passage_full, preferred_element_type=jnp.float32)
    query_grad = lax.psum_scatter(query_terms, "cols", scatter_dimension=1, tiled=True)
    passage_terms = logit_scale * lax.dot_general(
        dlogits, query_full, (((0,), (0,)), ((), ())), preferred_element_type=jnp.float32
    )
    passage_grad = lax.psum_scatter(passage_terms, "rows", scatter_dimension=1, tiled=True)
    return (query_grad, passage_grad)


def solution(mesh):
    return jax.shard_map(
        body,
        mesh=mesh,
        in_specs=(P("rows", "cols"), P("cols", "rows"), P("rows")),
        out_specs=(P("rows", "cols"), P("cols", "rows")),
        check_vma=False,
    )
```

profile of v0, /device:TPU:16, one launch (start us, length us, event | category | flops | bytes accessed | tf_op | source)
XLA Modules:
  0.0 731.4 jit_solution(16429631686562862104)
XLA Ops:
  7.9 13.4 %all-gather = bf16[8,96,144]{1,2,0:T(8,128)(2,1)S(1)} all-gather(bf16[1,96,144]{1,2,0:T(8,128)(2,1)} %bitcast.20), channel_id=1, replica_groups=mesh['rows'=64,'cols'=8] {'cols'}, dimensions={0}, use_global_device_ids=true | all-gather | bytes 248832 | tf_op jit(solution)/shard_map/all_gather | solution.py:10
  21.7 134.1 %all-gather.4.cloned.1.call-done = bf16[64,12,1152]{2,1,0:T(8,128)(2,1)} async-done(((bf16[1,12,1152]{2,1,0:T(8,128)(2,1)}), bf16[64,12,1152]{2,1,0:T(8,128)(2,1)}) %all-gather.4.cloned.1.call-update) | async-done | bytes 1769488 | tf_op jit(solution)/shard_map/all_gather | solution.py:11
  155.8 2.5 reshape.16
  158.9 122.9 %pmax.15 = f32[1152]{0:T(1024)S(1)} all-reduce(f32[1152]{0:T(1024)S(1)} %get-tuple-element.5), channel_id=1, replica_groups=mesh['rows'=64,'cols'=8] {'rows'}, use_global_device_ids=true, to_apply=%region_5.0 | all-reduce | flops 1152 | bytes 9216 | tf_op jit(solution)/shard_map/pmax | solution.py:18
  281.9 12.4 %pmax.14 = f32[144]{0:T(256)S(1)} all-reduce(f32[144]{0:T(256)S(1)} %get-tuple-element.4), channel_id=1, replica_groups=mesh['rows'=64,'cols'=8] {'cols'}, use_global_device_ids=true, to_apply=%region_1.0 | all-reduce | flops 144 | bytes 1152 | tf_op jit(solution)/shard_map/pmax | solution.py:16
  294.6 120.7 %psum.15 = f32[1152]{0:T(1024)S(1)} all-reduce(f32[1152]{0:T(1024)S(1)} %get-tuple-element.3), channel_id=1, replica_groups=mesh['rows'=64,'cols'=8] {'rows'}, use_global_device_ids=true, to_apply=%region_7.0 | all-reduce | flops 1152 | bytes 9216 | tf_op jit(solution)/shard_map/psum | solution.py:19
  415.3 12.4 %psum.14 = f32[144]{0:T(256)S(1)} all-reduce(f32[144]{0:T(256)S(1)} %get-tuple-element.2), channel_id=1, replica_groups=mesh['rows'=64,'cols'=8] {'cols'}, use_global_device_ids=true, to_apply=%region_3.0 | all-reduce | flops 144 | bytes 1152 | tf_op jit(solution)/shard_map/psum | solution.py:17
  427.7 1.5 convolution_multiply_fusion.2
  429.3 2.0 convolution_multiply_fusion
  431.3 2.2 copy.7
  433.5 162.1 %fusion = f32[1152,16]{0,1:T(8,128)} fusion(f32[1152,768]{0,1:T(8,128)S(1)} %convolution_multiply_fusion), kind=kCustom, calls=%all-reduce-scatter | all-reduce-scatter fusion | flops 1179649 | bytes 3614720
  595.6 0.9 slice
  596.5 24.1 %collective-permute-start.15 = (f32[1152,12]{0,1:T(8,128)S(1)}, f32[1152,12]{0,1:T(8,128)S(1)}, u32[]{:S(2)}, u32[]{:S(2)}) collective-permute-start(f32[1152,12]{0,1:T(8,128)S(1)} %slice), channel_id=1, source_target_pairs={{0,128},{8,136},{16,144},{24,152},{32,160},{40,168},{48,176},{56,1... | collective-permute-start | bytes 165896
  620.6 28.6 %collective-permute-start.14 = (f32[1152,16]{0,1:T(8,128)}, f32[1152,16]{0,1:T(8,128)S(1)}, u32[]{:S(2)}, u32[]{:S(2)}) collective-permute-start(f32[1152,16]{0,1:T(8,128)} %fusion), channel_id=1, source_target_pairs={{0,120},{8,128},{16,136},{24,144},{32,152},{40,160},{48,168},{56,1... | collective-permute-start | bytes 221192
  649.3 1.9 collective-permute-start.13
  651.2 1.9 collective-permute-start.12
  653.2 1.9 collective-permute-start.11
  655.1 1.9 collective-permute-start.10
  657.0 1.9 collective-permute-start.9
  659.0 9.6 %collective-permute-start.8 = (f32[1152,16]{0,1:T(8,128)}, f32[1152,16]{0,1:T(8,128)S(1)}, u32[]{:S(2)}, u32[]{:S(2)}) collective-permute-start(f32[1152,16]{0,1:T(8,128)} %fusion), channel_id=1, source_target_pairs={{0,72},{8,80},{16,88},{24,96},{32,104},{40,112},{48,120},{56,128},... | collective-permute-start | bytes 221192
  668.6 3.2 collective-permute-start.7
  671.8 1.9 collective-permute-start.6
  673.7 8.5 %collective-permute-start.5 = (f32[1152,16]{0,1:T(8,128)}, f32[1152,16]{0,1:T(8,128)S(1)}, u32[]{:S(2)}, u32[]{:S(2)}) collective-permute-start(f32[1152,16]{0,1:T(8,128)} %fusion), channel_id=1, source_target_pairs={{0,48},{8,56},{16,64},{24,72},{32,80},{40,88},{48,96},{56,104},{64... | collective-permute-start | bytes 221192
  682.2 1.9 collective-permute-start.4
  684.1 8.8 %collective-permute-start.3 = (f32[1152,16]{0,1:T(8,128)}, f32[1152,16]{0,1:T(8,128)S(1)}, u32[]{:S(2)}, u32[]{:S(2)}) collective-permute-start(f32[1152,16]{0,1:T(8,128)} %fusion), channel_id=1, source_target_pairs={{0,32},{8,40},{16,48},{24,56},{32,64},{40,72},{48,80},{56,88},{64,... | collective-permute-start | bytes 221192
  692.9 14.7 %collective-permute-start.2 = (f32[1152,16]{0,1:T(8,128)}, f32[1152,16]{0,1:T(8,128)S(1)}, u32[]{:S(2)}, u32[]{:S(2)}) collective-permute-start(f32[1152,16]{0,1:T(8,128)} %fusion), channel_id=1, source_target_pairs={{0,24},{8,32},{16,40},{24,48},{32,56},{40,64},{48,72},{56,80},{64,... | collective-permute-start | bytes 221192
  707.6 2.5 collective-permute-start.1
  710.1 2.5 collective-permute-start
  712.6 1.3 dynamic-slice.4
  714.5 4.1 collective-permute-done.1
  719.2 3.1 concatenate
  722.9 1.6 copy.8
  (34 shorter events, 3.2 us)
Async XLA Ops:
  7.2 148.6 %all-gather.4.cloned.1.call-start = ((), (), s32[]{:S(2)}) async-start(), calls=%async_computation.1 | async-start | bytes 2396160 | tf_op jit(solution)/shard_map/all_gather | solution.py:11
  7.9 715.0 %reduce-scatter.6.cloned.1.call-start = ((), (), s32[]{:S(2)}) async-start(), calls=%async_computation.2 | async-start | bytes 884736
  21.7 136.6 %copy-start.1 = (bf16[768,144]{0,1:T(8,128)(2,1)}, bf16[768,144]{0,1:T(8,128)(2,1)S(1)}, u32[]{:S(2)}) copy-start(bf16[768,144]{0,1:T(8,128)(2,1)S(1)} %reshape.14) | copy-start | bytes 663556
  158.3 269.4 %copy-start.2 = (s32[144]{0:T(256)S(1)}, s32[144]{0:T(256)}, u32[]{:S(2)}) copy-start(s32[144]{0:T(256)} %param.5) | copy-start | bytes 1732
  158.9 268.8 %copy-start = (f32[144,1152]{1,0:T(8,128)}, f32[144,1152]{1,0:T(8,128)S(1)}, u32[]{:S(2)}) copy-start(f32[144,1152]{1,0:T(8,128)S(1)} %get-tuple-element.6) | copy-start | bytes 1990660
  596.5 58.5 %collective-permute-start.15 = (f32[1152,12]{0,1:T(8,128)S(1)}, f32[1152,12]{0,1:T(8,128)S(1)}, u32[]{:S(2)}, u32[]{:S(2)}) collective-permute-start(f32[1152,12]{0,1:T(8,128)S(1)} %slice), channel_id=1, source_target_pairs={{0,128},{8,136},{16,144},{24,152},{32,160},{40,168},{48,176},{56,1... | collective-permute-start | bytes 165896
  620.6 36.4 %collective-permute-start.14 = (f32[1152,16]{0,1:T(8,128)}, f32[1152,16]{0,1:T(8,128)S(1)}, u32[]{:S(2)}, u32[]{:S(2)}) collective-permute-start(f32[1152,16]{0,1:T(8,128)} %fusion), channel_id=1, source_target_pairs={{0,120},{8,128},{16,136},{24,144},{32,152},{40,160},{48,168},{56,1... | collective-permute-start | bytes 221192
  649.3 9.7 %collective-permute-start.13 = (f32[1152,16]{0,1:T(8,128)}, f32[1152,16]{0,1:T(8,128)S(1)}, u32[]{:S(2)}, u32[]{:S(2)}) collective-permute-start(f32[1152,16]{0,1:T(8,128)} %fusion), channel_id=1, source_target_pairs={{0,112},{8,120},{16,128},{24,136},{32,144},{40,152},{48,160},{56,1... | collective-permute-start | bytes 221192
  651.2 17.3 %collective-permute-start.12 = (f32[1152,16]{0,1:T(8,128)}, f32[1152,16]{0,1:T(8,128)S(1)}, u32[]{:S(2)}, u32[]{:S(2)}) collective-permute-start(f32[1152,16]{0,1:T(8,128)} %fusion), channel_id=1, source_target_pairs={{0,104},{8,112},{16,120},{24,128},{32,136},{40,144},{48,152},{56,1... | collective-permute-start | bytes 221192
  653.2 18.6 %collective-permute-start.11 = (f32[1152,16]{0,1:T(8,128)}, f32[1152,16]{0,1:T(8,128)S(1)}, u32[]{:S(2)}, u32[]{:S(2)}) collective-permute-start(f32[1152,16]{0,1:T(8,128)} %fusion), channel_id=1, source_target_pairs={{0,96},{8,104},{16,112},{24,120},{32,128},{40,136},{48,144},{56,15... | collective-permute-start | bytes 221192
  655.1 18.6 %collective-permute-start.10 = (f32[1152,16]{0,1:T(8,128)}, f32[1152,16]{0,1:T(8,128)S(1)}, u32[]{:S(2)}, u32[]{:S(2)}) collective-permute-start(f32[1152,16]{0,1:T(8,128)} %fusion), channel_id=1, source_target_pairs={{0,88},{8,96},{16,104},{24,112},{32,120},{40,128},{48,136},{56,144... | collective-permute-start | bytes 221192
  657.0 25.2 %collective-permute-start.9 = (f32[1152,16]{0,1:T(8,128)}, f32[1152,16]{0,1:T(8,128)S(1)}, u32[]{:S(2)}, u32[]{:S(2)}) collective-permute-start(f32[1152,16]{0,1:T(8,128)} %fusion), channel_id=1, source_target_pairs={{0,80},{8,88},{16,96},{24,104},{32,112},{40,120},{48,128},{56,136}... | collective-permute-start | bytes 221192
  659.0 25.2 %collective-permute-start.8 = (f32[1152,16]{0,1:T(8,128)}, f32[1152,16]{0,1:T(8,128)S(1)}, u32[]{:S(2)}, u32[]{:S(2)}) collective-permute-start(f32[1152,16]{0,1:T(8,128)} %fusion), channel_id=1, source_target_pairs={{0,72},{8,80},{16,88},{24,96},{32,104},{40,112},{48,120},{56,128},... | collective-permute-start | bytes 221192
  668.6 24.4 %collective-permute-start.7 = (f32[1152,16]{0,1:T(8,128)}, f32[1152,16]{0,1:T(8,128)S(1)}, u32[]{:S(2)}, u32[]{:S(2)}) collective-permute-start(f32[1152,16]{0,1:T(8,128)} %fusion), channel_id=1, source_target_pairs={{0,64},{8,72},{16,80},{24,88},{32,96},{40,104},{48,112},{56,120},{... | collective-permute-start | bytes 221192
  671.8 35.9 %collective-permute-start.6 = (f32[1152,16]{0,1:T(8,128)}, f32[1152,16]{0,1:T(8,128)S(1)}, u32[]{:S(2)}, u32[]{:S(2)}) collective-permute-start(f32[1152,16]{0,1:T(8,128)} %fusion), channel_id=1, source_target_pairs={{0,56},{8,64},{16,72},{24,80},{32,88},{40,96},{48,104},{56,112},{6... | collective-permute-start | bytes 221192
  673.7 36.4 %collective-permute-start.5 = (f32[1152,16]{0,1:T(8,128)}, f32[1152,16]{0,1:T(8,128)S(1)}, u32[]{:S(2)}, u32[]{:S(2)}) collective-permute-start(f32[1152,16]{0,1:T(8,128)} %fusion), channel_id=1, source_target_pairs={{0,48},{8,56},{16,64},{24,72},{32,80},{40,88},{48,96},{56,104},{64... | collective-permute-start | bytes 221192
  682.2 32.3 %collective-permute-start.4 = (f32[1152,16]{0,1:T(8,128)}, f32[1152,16]{0,1:T(8,128)S(1)}, u32[]{:S(2)}, u32[]{:S(2)}) collective-permute-start(f32[1152,16]{0,1:T(8,128)} %fusion), channel_id=1, source_target_pairs={{0,40},{8,48},{16,56},{24,64},{32,72},{40,80},{48,88},{56,96},{64,... | collective-permute-start | bytes 221192
  684.1 30.4 %collective-permute-start.3 = (f32[1152,16]{0,1:T(8,128)}, f32[1152,16]{0,1:T(8,128)S(1)}, u32[]{:S(2)}, u32[]{:S(2)}) collective-permute-start(f32[1152,16]{0,1:T(8,128)} %fusion), channel_id=1, source_target_pairs={{0,32},{8,40},{16,48},{24,56},{32,64},{40,72},{48,80},{56,88},{64,... | collective-permute-start | bytes 221192
  692.9 21.6 %collective-permute-start.2 = (f32[1152,16]{0,1:T(8,128)}, f32[1152,16]{0,1:T(8,128)S(1)}, u32[]{:S(2)}, u32[]{:S(2)}) collective-permute-start(f32[1152,16]{0,1:T(8,128)} %fusion), channel_id=1, source_target_pairs={{0,24},{8,32},{16,40},{24,48},{32,56},{40,64},{48,72},{56,80},{64,... | collective-permute-start | bytes 221192
  707.6 11.0 %collective-permute-start.1 = (f32[1152,16]{0,1:T(8,128)}, f32[1152,16]{0,1:T(8,128)S(1)}, u32[]{:S(2)}, u32[]{:S(2)}) collective-permute-start(f32[1152,16]{0,1:T(8,128)} %fusion), channel_id=1, source_target_pairs={{0,16},{8,24},{16,32},{24,40},{32,48},{40,56},{48,64},{56,72},{64,... | collective-permute-start | bytes 221192
  710.1 9.1 %collective-permute-start = (f32[1152,16]{0,1:T(8,128)}, f32[1152,16]{0,1:T(8,128)S(1)}, u32[]{:S(2)}, u32[]{:S(2)}) collective-permute-start(f32[1152,16]{0,1:T(8,128)} %fusion), channel_id=1, source_target_pairs={{0,8},{8,16},{16,24},{24,32},{32,40},{40,48},{48,56},{56,64},{64,7... | collective-permute-start | bytes 221192
Sparse Core Ops, SparseCore 0:
  11.0 144.7 all-gather.3
  433.6 68.0 reduce-scatter.5
where the time goes:
time: 732 us; the launch traced here: 731 us
  blocking collectives  444 us (61%)
  waiting for transfers between devices  139 us (19%)
  starting transfers between devices  116 us (16%)
  between operations  15 us (2%)
  local copies, waits for them, and re-layouts  12.5 us (2%)
    unnamed x1, blocking collectives  162 us
    all_gather x1, waiting for transfers between devices, body(): passage_full = lax.all_gather(passages, 'rows', axis=1, tiled=True)  134 us
    pmax x1, blocking collectives, body(): col_top = lax.pmax(jnp.max(logit_tile, axis=0), 'rows')  123 us
    psum x1, blocking collectives, body(): lax.psum(jnp.sum(jnp.exp(logit_tile - col_top[None, :]), axis=0), 'rows')  121 us
    unnamed x17, starting transfers between devices  116 us
  transfers between devices with their start and end apart: 18, of which 3 were waited for; matrix products, arithmetic and copies ran while one was open for 23% of the time, Pallas kernels for 0%

commit v1 on v0

v1 whole, which is shorter than its diff:
```python
import jax
import jax.numpy as jnp
from jax import lax
from jax.sharding import Mesh, PartitionSpec as P

logit_scale = 20.0
f32 = jnp.float32
bf16 = jnp.bfloat16


def share(x, axes, n):
    return lax.all_to_all(jnp.broadcast_to(x[None], (n, *x.shape)), axes, 0, 0, tiled=True)


def merge(pairs):
    top = jnp.max(pairs[:, 0], axis=0)
    total = jnp.sum(pairs[:, 1] * jnp.exp(pairs[:, 0] - top[None]), axis=0)
    return jnp.stack([top, total])


def body(queries, passages, positive):
    rows, width = queries.shape
    cols, slice_width = passages.shape
    query_parts = share(queries, ("x", "core"), 8)
    query_full = query_parts.transpose(1, 0, 2).reshape(rows, 8 * width)
    part = lax.all_gather(passages.T, "z", axis=0, tiled=False).reshape(16 * slice_width, cols)
    passage_full = share(part, "y", 4).reshape(64 * slice_width, cols)

    logit_tile = logit_scale * jnp.dot(query_full, passage_full, preferred_element_type=f32)
    row_top = jnp.max(logit_tile, axis=1)
    row_sum = jnp.sum(jnp.exp(logit_tile - row_top[:, None]), axis=1)
    col_top = jnp.max(logit_tile, axis=0)
    col_sum = jnp.sum(jnp.exp(logit_tile - col_top[None, :]), axis=0)
    row_pair = merge(share(jnp.stack([row_top, row_sum]), ("x", "core"), 8))
    col_pair = merge(share(jnp.stack([col_top, col_sum]), "y", 4))
    col_pair = merge(share(col_pair, "z", 16))
    row_lse = row_pair[0] + jnp.log(row_pair[1])
    col_lse = col_pair[0] + jnp.log(col_pair[1])

    block = lax.axis_index("x") * 2 + lax.axis_index("core")
    column_ids = block * cols + jnp.arange(cols, dtype=jnp.int32)
    hit = (positive[:, None] == column_ids[None, :]).astype(f32)
    dlogits = (
        jnp.exp(logit_tile - row_lse[:, None]) + jnp.exp(logit_tile - col_lse[None, :]) - 2.0 * hit
    ).astype(bf16)

    passage_terms = logit_scale * lax.dot_general(
        query_full, dlogits, (((0,), (0,)), ((), ())), preferred_element_type=f32
    )
    passage_terms = passage_terms.astype(bf16).reshape(4, 16 * slice_width, cols)
    passage_terms = lax.all_to_all(passage_terms, "y", 0, 0, tiled=True)
    passage_terms = jnp.sum(passage_terms.astype(f32), axis=0)
    passage_terms = lax.all_to_all(passage_terms.reshape(16, slice_width, cols), "z", 0, 0, tiled=True)
    passage_grad = jnp.sum(passage_terms, axis=0).T

    query_terms = logit_scale * lax.dot_general(
        dlogits, passage_full, (((1,), (1,)), ((), ())), preferred_element_type=f32
    )
    query_terms = query_terms.astype(bf16).reshape(rows, 8, width).transpose(1, 0, 2)
    query_terms = lax.all_to_all(query_terms, ("x", "core"), 0, 0, tiled=True)
    query_grad = jnp.sum(query_terms.astype(f32), axis=0)
    return (query_grad, passage_grad)


def solution(mesh):
    chips = Mesh(mesh.devices.reshape(4, 16, 4, 2), ("y", "z", "x", "core"))
    yz, xc = ("y", "z"), ("x", "core")
    return jax.shard_map(
        body,
        mesh=chips,
        in_specs=(P(yz, xc), P(xc, yz), P(yz)),
        out_specs=(P(yz, xc), P(xc, yz)),
        check_vma=False,
    )
```

time: 732 us -> 212 us (0.29)
  the two profiles are of different devices: /device:TPU:16 before, /device:TPU:32 now
where the time goes in v1:
time: 212 us; the launch traced here: 211 us
  waiting for transfers between devices  119 us (56%)
  starting transfers between devices  38.5 us (18%)
  blocking collectives  36.7 us (17%)
  local copies, waits for them, and re-layouts  8.37 us (4%)
  matrix products  5.28 us (2%)
  other arithmetic  2.28 us (1%)
    all_to_all x1, waiting for transfers between devices, body(): lax.all_to_all(passage_terms.reshape(16, slice_width, cols), 'z', 0, 0, t...  53.8 us
    all_to_all x5, waiting for transfers between devices, share(): lax.all_to_all(jnp.broadcast_to(x[None], (n, *x.shape)), axes, 0, 0, tile...  41.5 us
    all_gather x1, blocking collectives, body(): lax.all_gather(passages.T, 'z', axis=0, tiled=False)  36.7 us
    all_to_all x5, starting transfers between devices, share(): lax.all_to_all(jnp.broadcast_to(x[None], (n, *x.shape)), axes, 0, 0, tile...  25.3 us
    all_to_all x1, waiting for transfers between devices, body(): passage_terms = lax.all_to_all(passage_terms, 'y', 0, 0, tiled=True)  16.9 us
    all_to_all x1, waiting for transfers between devices, body(): query_terms = lax.all_to_all(query_terms, ('x', 'core'), 0, 0, tiled=True)  6.44 us
    all_to_all x1, starting transfers between devices, body(): lax.all_to_all(passage_terms.reshape(16, slice_width, cols), 'z', 0, 0, t...  6.19 us
    broadcast_in_dim x5, local copies, waits for them, and re-layouts, share(): jnp.broadcast_to(x[None], (n, *x.shape))  4.79 us
  transfers between devices with their start and end apart: 8, of which 7 were waited for; matrix products, arithmetic and copies ran while one was open for 3% of the time, Pallas kernels for 0%

profile of v1, /device:TPU:32, one launch (start us, length us, event | category | flops | bytes accessed | tf_op | source)
XLA Modules:
  0.0 210.6 jit_solution(8311525645199727996)
XLA Ops:
  0.6 1.5 broadcast_in_dim.12
  2.1 4.3 %all-to-all-start = ((bf16[8,144,96]{2,1,0:T(8,128)(2,1)}), bf16[8,144,96]{2,1,0:T(8,128)(2,1)S(1)}, u32[]{:S(2)}, u32[]{:S(2)}) async-start(bf16[8,144,96]{2,1,0:T(8,128)(2,1)} %broadcast_in_dim.12), calls=%async_computation | async-start | bytes 589824 | tf_op jit(solution)/shard_map/all_to_all | solution.py:12
  6.4 36.7 %all-gather.1 = bf16[16,12,1152]{2,1,0:T(8,128)(2,1)S(1)} all-gather(bf16[1,12,1152]{2,1,0:T(8,128)(2,1)} %bitcast.59), channel_id=2, replica_groups=mesh['y'=4,'z'=16,'x'=4,'core'=2] {'z'}, dimensions={0}, use_global_device_ids=true | all-gather | bytes 470016 | tf_op jit(solution)/shard_map/all_gather | solution.py:26
  43.3 1.3 broadcast_in_dim.14
  44.6 4.5 %all-to-all-start.1 = ((bf16[4,192,1152]{2,1,0:T(8,128)(2,1)}), bf16[4,192,1152]{2,1,0:T(8,128)(2,1)S(1)}, u32[]{:S(2)}, u32[]{:S(2)}) async-start(bf16[4,192,1152]{2,1,0:T(8,128)(2,1)} %broadcast_in_dim.14), calls=%async_computation.1 | async-start | bytes 3538944 | tf_op jit(solution)/shard_map/all_to_all | solution.py:12
  49.1 0.2 reshape.46
  49.4 16.6 %all-to-all-done.1 = bf16[4,192,1152]{2,1,0:T(8,128)(2,1)S(1)} async-done(((bf16[4,192,1152]{2,1,0:T(8,128)(2,1)}), bf16[4,192,1152]{2,1,0:T(8,128)(2,1)S(1)}, u32[]{:S(2)}, u32[]{:S(2)}) %all-to-all-start.1) | async-done | bytes 1769504 | tf_op jit(solution)/shard_map/all_to_all | solution.py:12
  66.0 0.6 fusion.14
  66.6 0.3 exponential_reduce_fusion.1
  66.9 0.6 broadcast_in_dim.16
  67.5 3.3 %all-to-all-start.3 = ((f32[4,2,1152]{2,1,0:T(2,128)}), f32[4,2,1152]{2,1,0:T(2,128)S(1)}, u32[]{:S(2)}, u32[]{:S(2)}) async-start(f32[4,2,1152]{2,1,0:T(2,128)} %broadcast_in_dim.16), calls=%async_computation.3 | async-start | bytes 73728 | tf_op jit(solution)/shard_map/all_to_all | solution.py:12
  70.8 5.4 %all-to-all-done.3 = f32[4,2,1152]{2,1,0:T(2,128)S(1)} async-done(((f32[4,2,1152]{2,1,0:T(2,128)}), f32[4,2,1152]{2,1,0:T(2,128)S(1)}, u32[]{:S(2)}, u32[]{:S(2)}) %all-to-all-start.3) | async-done | bytes 36896 | tf_op jit(solution)/shard_map/all_to_all | solution.py:12
  76.2 0.6 broadcast_in_dim.15
  76.8 4.4 %all-to-all-start.2 = ((f32[8,2,144]{2,1,0:T(2,128)}), f32[8,2,144]{2,1,0:T(2,128)S(1)}, u32[]{:S(2)}, u32[]{:S(2)}) async-start(f32[8,2,144]{2,1,0:T(2,128)} %broadcast_in_dim.15), calls=%async_computation.2 | async-start | bytes 32768 | tf_op jit(solution)/shard_map/all_to_all | solution.py:12
  81.4 5.2 %all-to-all-done.2 = f32[8,2,144]{2,1,0:T(2,128)S(1)} async-done(((f32[8,2,144]{2,1,0:T(2,128)}), f32[8,2,144]{2,1,0:T(2,128)S(1)}, u32[]{:S(2)}, u32[]{:S(2)}) %all-to-all-start.2) | async-done | bytes 9248 | tf_op jit(solution)/shard_map/all_to_all | solution.py:12
  86.6 0.7 broadcast_in_dim.17
  87.3 8.9 %all-to-all-start.4 = ((f32[16,2,1152]{2,1,0:T(2,128)}), f32[16,2,1152]{2,1,0:T(2,128)S(1)}, u32[]{:S(2)}, u32[]{:S(2)}) async-start(f32[16,2,1152]{2,1,0:T(2,128)} %broadcast_in_dim.17), calls=%async_computation.4 | async-start | bytes 294912 | tf_op jit(solution)/shard_map/all_to_all | solution.py:12
  96.2 14.3 %all-to-all-done.4 = f32[16,2,1152]{2,1,0:T(2,128)S(1)} async-done(((f32[16,2,1152]{2,1,0:T(2,128)}), f32[16,2,1152]{2,1,0:T(2,128)S(1)}, u32[]{:S(2)}, u32[]{:S(2)}) %all-to-all-start.4) | async-done | bytes 147488 | tf_op jit(solution)/shard_map/all_to_all | solution.py:12
  110.7 2.1 %fusion = bf16[1152,768]{0,1:T(8,128)(2,1)} fusion(bf16[144,768]{1,0:T(8,128)(2,1)S(1)} %reshape.46, f32[144,1152]{1,0:T(8,128)S(1)} %get-tuple-element.15, s32[1152]{0:T(1024)S(1)} %iota_add_fusion, f32[1152]{0:T(1024)S(1)} %log_add_fusion, f32[144]{0:T(256)S(1)} %log_add_fusion.1, s32[144]{0:T(256)S(1)} %copy-done.2), kind=kOutput, calls=%fused_computation.2 | convolution fusion | flops 257734656 | bytes 2664576 | tf_op jit(solution)/shard_map/dot_general | solution.py:47
  112.9 3.6 %all-to-all-start.6 = ((bf16[4,192,1152]{2,1,0:T(8,128)(2,1)}), bf16[4,192,1152]{2,1,0:T(8,128)(2,1)S(1)}, u32[]{:S(2)}, u32[]{:S(2)}) async-start(bf16[4,192,1152]{2,1,0:T(8,128)(2,1)} %bitcast.56), calls=%async_computation.6 | async-start | bytes 3538944 | tf_op jit(solution)/shard_map/all_to_all | solution.py:51
  116.4 2.6 %fusion.1 = bf16[144,768]{1,0:T(8,128)(2,1)} fusion(bf16[768,1152]{1,0:T(8,128)(2,1)S(1)} %bitcast.55, f32[144,1152]{1,0:T(8,128)} %copy-done, s32[1152]{0:T(1024)S(1)} %iota_add_fusion, f32[1152]{0:T(1024)S(1)} %log_add_fusion, f32[144]{0:T(256)} %copy-done.1, s32[144]{0:T(256)} %param.5), kind=kOutput, calls=%fused_computation.5 | convolution fusion | flops 256186368 | bytes 2664576 | tf_op jit(solution)/shard_map/dot_general | solution.py:56
  119.0 1.3 reshape.48
  120.3 0.8 copy.63
  121.1 16.9 %all-to-all-done.6 = bf16[4,192,1152]{2,1,0:T(8,128)(2,1)S(1)} async-done(((bf16[4,192,1152]{2,1,0:T(8,128)(2,1)}), bf16[4,192,1152]{2,1,0:T(8,128)(2,1)S(1)}, u32[]{:S(2)}, u32[]{:S(2)}) %all-to-all-start.6) | async-done | bytes 1769504 | tf_op jit(solution)/shard_map/all_to_all | solution.py:51
  138.0 3.4 %all-to-all-start.5 = ((bf16[8,144,96]{2,1,0:T(8,128)(2,1)}), bf16[8,144,96]{2,1,0:T(8,128)(2,1)S(1)}, u32[]{:S(2)}, u32[]{:S(2)}) async-start(bf16[8,144,96]{2,1,0:T(8,128)(2,1)} %bitcast.53), calls=%async_computation.5 | async-start | bytes 589824 | tf_op jit(solution)/shard_map/all_to_all | solution.py:60
  141.4 0.3 convert_reduce_fusion
  141.7 1.1 reshape.50
  142.8 6.4 %all-to-all-done.5 = bf16[8,144,96]{2,1,0:T(8,128)(2,1)S(1)} async-done(((bf16[8,144,96]{2,1,0:T(8,128)(2,1)}), bf16[8,144,96]{2,1,0:T(8,128)(2,1)S(1)}, u32[]{:S(2)}, u32[]{:S(2)}) %all-to-all-start.5) | async-done | bytes 221216 | tf_op jit(solution)/shard_map/all_to_all | solution.py:60
  149.2 6.2 %all-to-all-start.7 = ((f32[16,12,1152]{2,1,0:T(8,128)}), f32[16,12,1152]{2,1,0:T(8,128)S(1)}, u32[]{:S(2)}, u32[]{:S(2)}) async-start(f32[16,12,1152]{2,1,0:T(8,128)} %reshape.50), calls=%async_computation.7 | async-start | bytes 2359296 | tf_op jit(solution)/shard_map/all_to_all | solution.py:53
  155.4 0.7 convert_reduce_fusion.1
  156.1 53.8 %all-to-all-done.7 = f32[16,12,1152]{2,1,0:T(8,128)S(1)} async-done(((f32[16,12,1152]{2,1,0:T(8,128)}), f32[16,12,1152]{2,1,0:T(8,128)S(1)}, u32[]{:S(2)}, u32[]{:S(2)}) %all-to-all-start.7) | async-done | bytes 884768 | tf_op jit(solution)/shard_map/all_to_all | solution.py:53
  209.9 0.7 reduce_sum.79
  (25 shorter events, 0.6 us)
Async XLA Ops:
  2.1 41.1 %all-to-all-start = ((bf16[8,144,96]{2,1,0:T(8,128)(2,1)}), bf16[8,144,96]{2,1,0:T(8,128)(2,1)S(1)}, u32[]{:S(2)}, u32[]{:S(2)}) async-start(bf16[8,144,96]{2,1,0:T(8,128)(2,1)} %broadcast_in_dim.12), calls=%async_computation | async-start | bytes 589824 | tf_op jit(solution)/shard_map/all_to_all | solution.py:12
  44.6 21.4 %all-to-all-start.1 = ((bf16[4,192,1152]{2,1,0:T(8,128)(2,1)}), bf16[4,192,1152]{2,1,0:T(8,128)(2,1)S(1)}, u32[]{:S(2)}, u32[]{:S(2)}) async-start(bf16[4,192,1152]{2,1,0:T(8,128)(2,1)} %broadcast_in_dim.14), calls=%async_computation.1 | async-start | bytes 3538944 | tf_op jit(solution)/shard_map/all_to_all | solution.py:12
  66.0 44.8 %copy-start.2 = (s32[144]{0:T(256)S(1)}, s32[144]{0:T(256)}, u32[]{:S(2)}) copy-start(s32[144]{0:T(256)} %param.5) | copy-start | bytes 1732
  66.6 46.3 %copy-start = (f32[144,1152]{1,0:T(8,128)}, f32[144,1152]{1,0:T(8,128)S(1)}, u32[]{:S(2)}) copy-start(f32[144,1152]{1,0:T(8,128)S(1)} %get-tuple-element.15) | copy-start | bytes 1990660
  67.5 8.7 %all-to-all-start.3 = ((f32[4,2,1152]{2,1,0:T(2,128)}), f32[4,2,1152]{2,1,0:T(2,128)S(1)}, u32[]{:S(2)}, u32[]{:S(2)}) async-start(f32[4,2,1152]{2,1,0:T(2,128)} %broadcast_in_dim.16), calls=%async_computation.3 | async-start | bytes 73728 | tf_op jit(solution)/shard_map/all_to_all | solution.py:12
  76.8 9.8 %all-to-all-start.2 = ((f32[8,2,144]{2,1,0:T(2,128)}), f32[8,2,144]{2,1,0:T(2,128)S(1)}, u32[]{:S(2)}, u32[]{:S(2)}) async-start(f32[8,2,144]{2,1,0:T(2,128)} %broadcast_in_dim.15), calls=%async_computation.2 | async-start | bytes 32768 | tf_op jit(solution)/shard_map/all_to_all | solution.py:12
  87.3 23.2 %all-to-all-start.4 = ((f32[16,2,1152]{2,1,0:T(2,128)}), f32[16,2,1152]{2,1,0:T(2,128)S(1)}, u32[]{:S(2)}, u32[]{:S(2)}) async-start(f32[16,2,1152]{2,1,0:T(2,128)} %broadcast_in_dim.17), calls=%async_computation.4 | async-start | bytes 294912 | tf_op jit(solution)/shard_map/all_to_all | solution.py:12
  96.2 16.6 %copy-start.1 = (f32[144]{0:T(256)}, f32[144]{0:T(256)S(1)}, u32[]{:S(2)}) copy-start(f32[144]{0:T(256)S(1)} %log_add_fusion.1) | copy-start | bytes 1732
  112.9 25.1 %all-to-all-start.6 = ((bf16[4,192,1152]{2,1,0:T(8,128)(2,1)}), bf16[4,192,1152]{2,1,0:T(8,128)(2,1)S(1)}, u32[]{:S(2)}, u32[]{:S(2)}) async-start(bf16[4,192,1152]{2,1,0:T(8,128)(2,1)} %bitcast.56), calls=%async_computation.6 | async-start | bytes 3538944 | tf_op jit(solution)/shard_map/all_to_all | solution.py:51
  138.0 11.2 %all-to-all-start.5 = ((bf16[8,144,96]{2,1,0:T(8,128)(2,1)}), bf16[8,144,96]{2,1,0:T(8,128)(2,1)S(1)}, u32[]{:S(2)}, u32[]{:S(2)}) async-start(bf16[8,144,96]{2,1,0:T(8,128)(2,1)} %bitcast.53), calls=%async_computation.5 | async-start | bytes 589824 | tf_op jit(solution)/shard_map/all_to_all | solution.py:60
  149.2 60.7 %all-to-all-start.7 = ((f32[16,12,1152]{2,1,0:T(8,128)}), f32[16,12,1152]{2,1,0:T(8,128)S(1)}, u32[]{:S(2)}, u32[]{:S(2)}) async-start(f32[16,12,1152]{2,1,0:T(8,128)} %reshape.50), calls=%async_computation.7 | async-start | bytes 2359296 | tf_op jit(solution)/shard_map/all_to_all | solution.py:53

commit v2 on v1

v2 whole, which is shorter than its diff:
```python
import jax
import jax.numpy as jnp
import numpy as np
from jax import lax
from jax.sharding import Mesh, PartitionSpec as P

logit_scale = 20.0
f32 = jnp.float32
bf16 = jnp.bfloat16
NY, NZ, NX, NC = 4, 16, 4, 2
SHORT = ("y", "x", "core")


def share(x, axes, n):
    return lax.all_to_all(jnp.broadcast_to(x[None], (n, *x.shape)), axes, 0, 0, tiled=True)


def merge(pairs):
    top = jnp.max(pairs[:, 0], axis=0)
    total = jnp.sum(pairs[:, 1] * jnp.exp(pairs[:, 0] - top[None]), axis=0)
    return top + jnp.log(total)


def placement(slice_width, width):
    table = np.zeros((NX * NC, 128, NZ, NY, slice_width), np.float32)
    for d in range(NX * NC * width):
        y, z, k = d // (NZ * slice_width), d // slice_width % NZ, d % slice_width
        table[d // width, d % width, z, y, k] = 1.0
    return table.reshape(NX * NC * 128, NZ * NY * slice_width)


def body(queries, passages, positive):
    rows, width = queries.shape
    cols, slice_width = passages.shape
    sub = cols // NY
    place = jnp.asarray(placement(slice_width, width), bf16)

    spare = jnp.stack([positive // 128, positive % 128], axis=1).astype(bf16)
    message = jnp.concatenate([queries, spare, jnp.zeros((rows, 126 - width), bf16)], axis=1)
    query_parts = share(message, SHORT, NY * NX * NC)
    query_full = (
        query_parts.reshape(NY, NX * NC, rows, 128).transpose(0, 2, 1, 3).reshape(NY * rows, NX * NC * 128)
    )

    part = passages.T.reshape(slice_width, NY, sub).transpose(1, 0, 2)
    part = lax.all_to_all(part, "y", 0, 0, tiled=True).reshape(NY * slice_width, sub)
    passage_part = lax.all_gather(part, "z", axis=0, tiled=True)
    passage_full = jnp.dot(place, passage_part, preferred_element_type=f32).astype(bf16)

    logit_tile = logit_scale * jnp.dot(query_full, passage_full, preferred_element_type=f32)
    row_top = jnp.max(logit_tile, axis=1)
    row_sum = jnp.sum(jnp.exp(logit_tile - row_top[:, None]), axis=1)
    col_top = jnp.max(logit_tile, axis=0)
    col_sum = jnp.sum(jnp.exp(logit_tile - col_top[None, :]), axis=0)
    col_lse = merge(share(jnp.stack([col_top, col_sum]), "z", NZ))
    row_lse = merge(share(jnp.stack([row_top, row_sum]), SHORT, NY * NX * NC))

    block = (lax.axis_index("x") * NC + lax.axis_index("core")) * NY + lax.axis_index("y")
    column_ids = (block * sub + jnp.arange(sub, dtype=jnp.int32)).astype(f32)
    target = query_full[:, width].astype(f32) * 128.0 + query_full[:, width + 1].astype(f32)
    hit = (target[:, None] == column_ids[None, :]).astype(f32)
    dlogits = (
        jnp.exp(logit_tile - row_lse[:, None]) + jnp.exp(logit_tile - col_lse[None, :]) - 2.0 * hit
    ).astype(bf16)

    query_placed = jnp.dot(query_full, place, preferred_element_type=f32).astype(bf16)
    passage_terms = logit_scale * lax.dot_general(
        query_placed, dlogits, (((0,), (0,)), ((), ())), preferred_element_type=f32
    )
    passage_terms = passage_terms.astype(bf16).reshape(NZ, NY * slice_width, sub)
    passage_terms = lax.all_to_all(passage_terms, "z", 0, 0, tiled=True)
    passage_terms = jnp.sum(passage_terms.astype(f32), axis=0).reshape(NY, slice_width, sub)
    passage_terms = lax.all_to_all(passage_terms, "y", 0, 0, tiled=True)
    passage_grad = passage_terms.transpose(1, 0, 2).reshape(slice_width, cols).T

    query_terms = logit_scale * lax.dot_general(
        dlogits, passage_full, (((1,), (1,)), ((), ())), preferred_element_type=f32
    )
    query_terms = query_terms.astype(bf16).reshape(NY, rows, NX * NC, 128).transpose(0, 2, 1, 3)
    query_terms = lax.all_to_all(query_terms.reshape(NY * NX * NC, rows, 128), SHORT, 0, 0, tiled=True)
    query_grad = jnp.sum(query_terms.astype(f32), axis=0)[:, :width]
    return (query_grad, passage_grad)


def solution(mesh):
    chips = Mesh(mesh.devices.reshape(NY, NZ, NX, NC), ("y", "z", "x", "core"))
    yz, xc = ("y", "z"), ("x", "core")
    return jax.shard_map(
        body,
        mesh=chips,
        in_specs=(P(yz, xc), P(xc, yz), P(yz)),
        out_specs=(P(yz, xc), P(xc, yz)),
        check_vma=False,
    )
```

time: 212 us -> 172 us (0.81)
  waiting for transfers between devices: 119 us -> 75.3 us
  matrix products: 5.28 us -> 7.79 us
    all_to_all x5 -> x3, waiting for transfers between devices: 41.5 us -> 18.9 us  [share(): lax.all_to_all(jnp.broadcast_to(x[None], (n, *x.shape)), axes, 0, 0, tile...]
    all_to_all x1, waiting for transfers between devices: 16.9 us -> 4.96 us  [body(): passage_terms = lax.all_to_all(passage_terms, 'y', 0, 0, tiled=True)]
    all_to_all x2 -> x3, waiting for transfers between devices: 60.2 us -> 51.5 us  [the longest x1 29.5 us: body(): passage_terms = lax.all_to_all(passage_terms, 'z', 0, 0, tiled=True)]
    dot_general x1 -> x2, matrix products: 2.12 us -> 6.01 us  [the longest x1 3.11 us: body(): lax.dot_general(query_placed, dlogits, (((0,), (0,)), ((), ())), preferre...]
    all_to_all x5 -> x3, starting transfers between devices: 25.3 us -> 21.6 us  [share(): lax.all_to_all(jnp.broadcast_to(x[None], (n, *x.shape)), axes, 0, 0, tile...]
    all_to_all x2 -> x3, starting transfers between devices: 9.62 us -> 12.9 us  [the longest x1 4.54 us: body(): passage_terms = lax.all_to_all(passage_terms, 'z', 0, 0, tiled=True)]
    broadcast_in_dim x5 -> x3, local copies, waits for them, and re-layouts: 4.79 us -> 2.51 us  [share(): jnp.broadcast_to(x[None], (n, *x.shape))]
  transfers between devices with their start and end apart: 8 -> 7, of which waited for: 7 -> 6; matrix products, arithmetic and copies ran while one was open for 3% -> 6% of each run, Pallas kernels for 0% -> 0%
where the time goes in v2:
time: 172 us; the launch traced here: 171 us
  waiting for transfers between devices  75.3 us (44%)
  starting transfers between devices  37.8 us (22%)
  blocking collectives  36.7 us (21%)
  local copies, waits for them, and re-layouts  9.66 us (6%)
  matrix products  7.79 us (5%)
  other arithmetic  3.36 us (2%)
    all_gather x1, blocking collectives, body(): passage_part = lax.all_gather(part, 'z', axis=0, tiled=True)  36.7 us
    all_to_all x1, waiting for transfers between devices, body(): passage_terms = lax.all_to_all(passage_terms, 'z', 0, 0, tiled=True)  29.5 us
    all_to_all x3, starting transfers between devices, share(): lax.all_to_all(jnp.broadcast_to(x[None], (n, *x.shape)), axes, 0, 0, tile...  21.6 us
    all_to_all x3, waiting for transfers between devices, share(): lax.all_to_all(jnp.broadcast_to(x[None], (n, *x.shape)), axes, 0, 0, tile...  18.9 us
    all_to_all x1, waiting for transfers between devices, body(): lax.all_to_all(query_terms.reshape(NY * NX * NC, rows, 128), SHORT, 0, 0,...  18.3 us
    all_to_all x1, waiting for transfers between devices, body(): passage_terms = lax.all_to_all(passage_terms, 'y', 0, 0, tiled=True)  4.96 us
    all_to_all x1, starting transfers between devices, body(): passage_terms = lax.all_to_all(passage_terms, 'z', 0, 0, tiled=True)  4.54 us
    all_to_all x1, starting transfers between devices, body(): lax.all_to_all(part, 'y', 0, 0, tiled=True).reshape(NY * slice_width, sub)  4.46 us
  transfers between devices with their start and end apart: 7, of which 6 were waited for; matrix products, arithmetic and copies ran while one was open for 6% of the time, Pallas kernels for 0%

profile of v2, /device:TPU:32, one launch (start us, length us, event | category | flops | bytes accessed | tf_op | source)
XLA Modules:
  0.0 171.4 jit_solution(5871348833316797554)
XLA Ops:
  0.6 0.9 reshape.57
  1.5 0.6 copy.76
  2.1 4.5 %all-to-all-start.1 = ((bf16[4,12,288]{2,1,0:T(8,128)(2,1)}), bf16[4,12,288]{2,1,0:T(8,128)(2,1)S(1)}, u32[]{:S(2)}, u32[]{:S(2)}) async-start(bf16[4,12,288]{2,1,0:T(8,128)(2,1)} %bitcast.55), calls=%async_computation.1 | async-start | bytes 98304 | tf_op jit(solution)/shard_map/all_to_all | solution.py:46
  6.6 0.7 fusion.11
  7.6 0.9 maximum_maximum_fusion
  8.4 3.7 %all-to-all-done.1 = bf16[4,12,288]{2,1,0:T(8,128)(2,1)S(1)} async-done(((bf16[4,12,288]{2,1,0:T(8,128)(2,1)}), bf16[4,12,288]{2,1,0:T(8,128)(2,1)S(1)}, u32[]{:S(2)}, u32[]{:S(2)}) %all-to-all-start.1) | async-done | bytes 27680 | tf_op jit(solution)/shard_map/all_to_all | solution.py:46
  12.1 1.2 broadcast_in_dim.9
  13.3 5.3 %all-to-all-start = ((bf16[32,144,128]{2,1,0:T(8,128)(2,1)}), bf16[32,144,128]{2,1,0:T(8,128)(2,1)S(1)}, u32[]{:S(2)}, u32[]{:S(2)}) async-start(bf16[32,144,128]{2,1,0:T(8,128)(2,1)} %broadcast_in_dim.9), calls=%async_computation | async-start | bytes 2359296 | tf_op jit(solution)/shard_map/all_to_all | solution.py:15
  18.7 36.7 %all_gather.3 = bf16[768,288]{1,0:T(8,128)(2,1)S(1)} all-gather(bf16[48,288]{1,0:T(8,128)(2,1)S(1)} %reshape.58), channel_id=1, replica_groups=mesh['y'=4,'z'=16,'x'=4,'core'=2] {'z'}, dimensions={0}, use_global_device_ids=true | all-gather | bytes 470016 | tf_op jit(solution)/shard_map/all_gather | solution.py:47
  55.3 2.9 %convolution_convert_fusion.1 = bf16[1024,288]{0,1:T(8,128)(2,1)} fusion(bf16[1024,768]{1,0:T(8,128)(2,1)} %constant.63.clone, bf16[768,288]{1,0:T(8,128)(2,1)S(1)} %all_gather.3), kind=kOutput, calls=%fused_computation.5 | convolution fusion | flops 453279744 | bytes 2605056 | tf_op jit(solution)/shard_map/dot_general | solution.py:48
  58.5 0.8 copy-done
  59.3 0.8 fusion.12
  60.1 0.3 exponential_reduce_fusion.1
  60.5 0.6 broadcast_in_dim.11
  61.1 8.7 %all-to-all-start.3 = ((f32[16,2,288]{2,1,0:T(2,128)}), f32[16,2,288]{2,1,0:T(2,128)S(1)}, u32[]{:S(2)}, u32[]{:S(2)}) async-start(f32[16,2,288]{2,1,0:T(2,128)} %broadcast_in_dim.11), calls=%async_computation.3 | async-start | bytes 98304 | tf_op jit(solution)/shard_map/all_to_all | solution.py:15
  70.4 11.0 %all-to-all-done.3 = f32[16,2,288]{2,1,0:T(2,128)S(1)} async-done(((f32[16,2,288]{2,1,0:T(2,128)}), f32[16,2,288]{2,1,0:T(2,128)S(1)}, u32[]{:S(2)}, u32[]{:S(2)}) %all-to-all-start.3) | async-done | bytes 36896 | tf_op jit(solution)/shard_map/all_to_all | solution.py:15
  81.4 0.7 broadcast_in_dim.10
  82.1 7.5 %all-to-all-start.2 = ((f32[32,2,576]{2,1,0:T(2,128)}), f32[32,2,576]{2,1,0:T(2,128)S(1)}, u32[]{:S(2)}, u32[]{:S(2)}) async-start(f32[32,2,576]{2,1,0:T(2,128)} %broadcast_in_dim.10), calls=%async_computation.2 | async-start | bytes 327680 | tf_op jit(solution)/shard_map/all_to_all | solution.py:15
  89.8 7.8 %all-to-all-done.2 = f32[32,2,576]{2,1,0:T(2,128)S(1)} async-done(((f32[32,2,576]{2,1,0:T(2,128)}), f32[32,2,576]{2,1,0:T(2,128)S(1)}, u32[]{:S(2)}, u32[]{:S(2)}) %all-to-all-start.2) | async-done | bytes 147488 | tf_op jit(solution)/shard_map/all_to_all | solution.py:15
  97.8 3.1 %fusion.1 = bf16[768,288]{0,1:T(8,128)(2,1)S(1)} fusion(bf16[1024,768]{1,0:T(8,128)(2,1)} %constant.63.clone, bf16[72,8,8,128]{3,2,1,0:T(8,128)(2,1)S(1)} %bitcast.59, f32[576,288]{0,1:T(8,128)S(1)} %get-tuple-element.14, f32[576]{0:T(1024)S(1)} %add_reduce_fusion, f32[288]{0:T(512)S(1)} %log_add_fusion.1, f32[576]{0:T(1024)S(1)} %log_add_fusion, ...), kind=kOutput, calls=%fused_computation.7 | convolution fusion | flops 1162819584 | bytes 3865344 | tf_op jit(solution)/shard_map/dot_general | solution.py:67
  101.0 1.1 copy.38
  102.0 4.5 %all-to-all-start.5 = ((bf16[16,48,288]{2,1,0:T(8,128)(2,1)}), bf16[16,48,288]{2,1,0:T(8,128)(2,1)S(1)}, u32[]{:S(2)}, u32[]{:S(2)}) async-start(bf16[16,48,288]{2,1,0:T(8,128)(2,1)} %bitcast.8), calls=%async_computation.5 | async-start | bytes 1179648 | tf_op jit(solution)/shard_map/all_to_all | solution.py:71
  106.6 1.0 fusion
  107.9 1.2 copy.37
  109.1 29.5 %all-to-all-done.5 = bf16[16,48,288]{2,1,0:T(8,128)(2,1)S(1)} async-done(((bf16[16,48,288]{2,1,0:T(8,128)(2,1)}), bf16[16,48,288]{2,1,0:T(8,128)(2,1)S(1)}, u32[]{:S(2)}, u32[]{:S(2)}) %all-to-all-start.5) | async-done | bytes 442400 | tf_op jit(solution)/shard_map/all_to_all | solution.py:71
  138.6 3.9 %all-to-all-start.4 = ((bf16[32,144,128]{2,1,0:T(8,128)(2,1)}), bf16[32,144,128]{2,1,0:T(8,128)(2,1)S(1)}, u32[]{:S(2)}, u32[]{:S(2)}) async-start(bf16[32,144,128]{2,1,0:T(8,128)(2,1)} %bitcast.7), calls=%async_computation.4 | async-start | bytes 2359296 | tf_op jit(solution)/shard_map/all_to_all | solution.py:80
  142.7 0.6 reshape.62
  143.3 18.3 %all-to-all-done.4 = bf16[32,144,128]{2,1,0:T(8,128)(2,1)S(1)} async-done(((bf16[32,144,128]{2,1,0:T(8,128)(2,1)}), bf16[32,144,128]{2,1,0:T(8,128)(2,1)S(1)}, u32[]{:S(2)}, u32[]{:S(2)}) %all-to-all-start.4) | async-done | bytes 1179680 | tf_op jit(solution)/shard_map/all_to_all | solution.py:80
  161.6 3.3 %all-to-all-start.6 = ((f32[4,12,288]{2,1,0:T(8,128)}), f32[4,12,288]{2,1,0:T(8,128)S(1)}, u32[]{:S(2)}, u32[]{:S(2)}) async-start(f32[4,12,288]{2,1,0:T(8,128)} %reshape.62), calls=%async_computation.6 | async-start | bytes 196608 | tf_op jit(solution)/shard_map/all_to_all | solution.py:73
  164.9 0.8 convert_reduce_fusion
  165.7 5.0 %all-to-all-done.6 = f32[4,12,288]{2,1,0:T(8,128)S(1)} async-done(((f32[4,12,288]{2,1,0:T(8,128)}), f32[4,12,288]{2,1,0:T(8,128)S(1)}, u32[]{:S(2)}, u32[]{:S(2)}) %all-to-all-start.6) | async-done | bytes 55328 | tf_op jit(solution)/shard_map/all_to_all | solution.py:73
  170.7 0.7 reshape.63
  (28 shorter events, 1.9 us)
Async XLA Ops:
  2.1 10.0 %all-to-all-start.1 = ((bf16[4,12,288]{2,1,0:T(8,128)(2,1)}), bf16[4,12,288]{2,1,0:T(8,128)(2,1)S(1)}, u32[]{:S(2)}, u32[]{:S(2)}) async-start(bf16[4,12,288]{2,1,0:T(8,128)(2,1)} %bitcast.55), calls=%async_computation.1 | async-start | bytes 98304 | tf_op jit(solution)/shard_map/all_to_all | solution.py:46
  13.3 44.9 %all-to-all-start = ((bf16[32,144,128]{2,1,0:T(8,128)(2,1)}), bf16[32,144,128]{2,1,0:T(8,128)(2,1)S(1)}, u32[]{:S(2)}, u32[]{:S(2)}) async-start(bf16[32,144,128]{2,1,0:T(8,128)(2,1)} %broadcast_in_dim.9), calls=%async_computation | async-start | bytes 2359296 | tf_op jit(solution)/shard_map/all_to_all | solution.py:15
  58.2 1.1 copy-start
  61.1 20.3 %all-to-all-start.3 = ((f32[16,2,288]{2,1,0:T(2,128)}), f32[16,2,288]{2,1,0:T(2,128)S(1)}, u32[]{:S(2)}, u32[]{:S(2)}) async-start(f32[16,2,288]{2,1,0:T(2,128)} %broadcast_in_dim.11), calls=%async_computation.3 | async-start | bytes 98304 | tf_op jit(solution)/shard_map/all_to_all | solution.py:15
  82.1 15.5 %all-to-all-start.2 = ((f32[32,2,576]{2,1,0:T(2,128)}), f32[32,2,576]{2,1,0:T(2,128)S(1)}, u32[]{:S(2)}, u32[]{:S(2)}) async-start(f32[32,2,576]{2,1,0:T(2,128)} %broadcast_in_dim.10), calls=%async_computation.2 | async-start | bytes 327680 | tf_op jit(solution)/shard_map/all_to_all | solution.py:15
  100.9 5.6 %copy-start.1 = (bf16[1024,288]{0,1:T(8,128)(2,1)S(1)}, bf16[1024,288]{0,1:T(8,128)(2,1)}, u32[]{:S(2)}) copy-start(bf16[1024,288]{0,1:T(8,128)(2,1)} %convolution_convert_fusion.1) | copy-start | bytes 1769476
  102.0 36.6 %all-to-all-start.5 = ((bf16[16,48,288]{2,1,0:T(8,128)(2,1)}), bf16[16,48,288]{2,1,0:T(8,128)(2,1)S(1)}, u32[]{:S(2)}, u32[]{:S(2)}) async-start(bf16[16,48,288]{2,1,0:T(8,128)(2,1)} %bitcast.8), calls=%async_computation.5 | async-start | bytes 1179648 | tf_op jit(solution)/shard_map/all_to_all | solution.py:71
  138.6 23.0 %all-to-all-start.4 = ((bf16[32,144,128]{2,1,0:T(8,128)(2,1)}), bf16[32,144,128]{2,1,0:T(8,128)(2,1)S(1)}, u32[]{:S(2)}, u32[]{:S(2)}) async-start(bf16[32,144,128]{2,1,0:T(8,128)(2,1)} %bitcast.7), calls=%async_computation.4 | async-start | bytes 2359296 | tf_op jit(solution)/shard_map/all_to_all | solution.py:80
  161.6 9.1 %all-to-all-start.6 = ((f32[4,12,288]{2,1,0:T(8,128)}), f32[4,12,288]{2,1,0:T(8,128)S(1)}, u32[]{:S(2)}, u32[]{:S(2)}) async-start(f32[4,12,288]{2,1,0:T(8,128)} %reshape.62), calls=%async_computation.6 | async-start | bytes 196608 | tf_op jit(solution)/shard_map/all_to_all | solution.py:73

commit v3 on v2

--- a/solution.py
+++ b/solution.py
@@ -8,7 +8,7 @@
 f32 = jnp.float32
 bf16 = jnp.bfloat16
 NY, NZ, NX, NC = 4, 16, 4, 2
-SHORT = ("y", "x", "core")
+SHORT = ("y", "core", "x")
 
 
 def share(x, axes, n):
@@ -18,14 +18,26 @@
 def merge(pairs):
     top = jnp.max(pairs[:, 0], axis=0)
     total = jnp.sum(pairs[:, 1] * jnp.exp(pairs[:, 0] - top[None]), axis=0)
-    return top + jnp.log(total)
+    return jnp.stack([top, total])
+
+
+def lse(pair):
+    return pair[0] + jnp.log(pair[1])
+
+
+def around(x, axis, n, step):
+    return lax.ppermute(x, axis, [(i, (i + step) % n) for i in range(n)])
+
+
+def pick(blocks, axis, n, step):
+    return lax.dynamic_index_in_dim(blocks, (lax.axis_index(axis) + step) % n, 0, keepdims=False)
 
 
 def placement(slice_width, width):
-    table = np.zeros((NX * NC, 128, NZ, NY, slice_width), np.float32)
+    table = np.zeros((NC, NX, 128, NZ, NY, slice_width), np.float32)
     for d in range(NX * NC * width):
         y, z, k = d // (NZ * slice_width), d // slice_width % NZ, d % slice_width
-        table[d // width, d % width, z, y, k] = 1.0
+        table[d // width % NC, d // width // NC, d % width, z, y, k] = 1.0
     return table.reshape(NX * NC * 128, NZ * NY * slice_width)
 
 
@@ -38,9 +50,8 @@
     spare = jnp.stack([positive // 128, positive % 128], axis=1).astype(bf16)
     message = jnp.concatenate([queries, spare, jnp.zeros((rows, 126 - width), bf16)], axis=1)
     query_parts = share(message, SHORT, NY * NX * NC)
-    query_full = (
-        query_parts.reshape(NY, NX * NC, rows, 128).transpose(0, 2, 1, 3).reshape(NY * rows, NX * NC * 128)
-    )
+    query_full = query_parts.reshape(NY, NC * NX, rows, 128).transpose(0, 2, 1, 3)
+    query_full = query_full.reshape(NY * rows, NC * NX * 128)
 
     part = passages.T.reshape(slice_width, NY, sub).transpose(1, 0, 2)
     part = lax.all_to_all(part, "y", 0, 0, tiled=True).reshape(NY * slice_width, sub)
@@ -52,8 +63,11 @@
     row_sum = jnp.sum(jnp.exp(logit_tile - row_top[:, None]), axis=1)
     col_top = jnp.max(logit_tile, axis=0)
     col_sum = jnp.sum(jnp.exp(logit_tile - col_top[None, :]), axis=0)
-    col_lse = merge(share(jnp.stack([col_top, col_sum]), "z", NZ))
-    row_lse = merge(share(jnp.stack([row_top, row_sum]), SHORT, NY * NX * NC))
+    col_lse = lse(merge(share(jnp.stack([col_top, col_sum]), "z", NZ)))
+    row_pair = merge(lax.all_gather(jnp.stack([row_top, row_sum]), "core"))
+    for axis, n in (("x", NX), ("y", NY)):
+        row_pair = merge(jnp.stack([row_pair] + [around(row_pair, axis, n, step) for step in range(1, n)]))
+    row_lse = lse(row_pair)
 
     block = (lax.axis_index("x") * NC + lax.axis_index("core")) * NY + lax.axis_index("y")
     column_ids = (block * sub + jnp.arange(sub, dtype=jnp.int32)).astype(f32)
@@ -73,12 +87,23 @@
     passage_terms = lax.all_to_all(passage_terms, "y", 0, 0, tiled=True)
     passage_grad = passage_terms.transpose(1, 0, 2).reshape(slice_width, cols).T
 
-    query_terms = logit_scale * lax.dot_general(
-        dlogits, passage_full, (((1,), (1,)), ((), ())), preferred_element_type=f32
+    halves = passage_full.reshape(NC, NX * 128, sub)
+    ours, theirs = (
+        logit_scale
+        * lax.dot_general(
+            dlogits, pick(halves, "core", NC, step), (((1,), (1,)), ((), ())), preferred_element_type=f32
+        )
+        for step in range(NC)
     )
-    query_terms = query_terms.astype(bf16).reshape(NY, rows, NX * NC, 128).transpose(0, 2, 1, 3)
-    query_terms = lax.all_to_all(query_terms.reshape(NY * NX * NC, rows, 128), SHORT, 0, 0, tiled=True)
-    query_grad = jnp.sum(query_terms.astype(f32), axis=0)[:, :width]
+    blocks = (ours + around(theirs, "core", NC, 1)).reshape(NY * rows, NX, 128).transpose(1, 0, 2)
+    terms = pick(blocks, "x", NX, 0)
+    for step in range(1, NX):
+        terms += around(pick(blocks, "x", NX, step).astype(bf16), "x", NX, step).astype(f32)
+    blocks = terms.reshape(NY, rows, 128)
+    terms = pick(blocks, "y", NY, 0)
+    for step in range(1, NY):
+        terms += around(pick(blocks, "y", NY, step), "y", NY, step)
+    query_grad = terms[:, :width]
     return (query_grad, passage_grad)
 
 

time: 172 us -> 166 us (0.965)
  the two profiles are of different devices: /device:TPU:32 before, /device:TPU:2 now
where the time goes in v3:
time: 166 us; the launch traced here: 165 us
  starting transfers between devices  78.1 us (47%)
  blocking collectives  37.9 us (23%)
  waiting for transfers between devices  19.9 us (12%)
  local copies, waits for them, and re-layouts  12.6 us (8%)
  matrix products  10.7 us (6%)
  other arithmetic  4.4 us (3%)
    ppermute x13, starting transfers between devices, around(): return lax.ppermute(x, axis, [(i, (i + step) % n) for i in range(n)])  42.7 us
    all_gather x1, blocking collectives, body(): passage_part = lax.all_gather(part, 'z', axis=0, tiled=True)  36.1 us
    all_to_all x2, starting transfers between devices, share(): lax.all_to_all(jnp.broadcast_to(x[None], (n, *x.shape)), axes, 0, 0, tile...  15 us
    all_to_all x1, starting transfers between devices, body(): passage_terms = lax.all_to_all(passage_terms, 'z', 0, 0, tiled=True)  12.1 us
    ppermute x13, waiting for transfers between devices, around(): return lax.ppermute(x, axis, [(i, (i + step) % n) for i in range(n)])  7.22 us
    all_to_all x1, waiting for transfers between devices, body(): passage_terms = lax.all_to_all(passage_terms, 'y', 0, 0, tiled=True)  5.13 us
    dot_general x2, matrix products, body(): lax.dot_general(dlogits, pick(halves, 'core', NC, step), (((1,), (1,)), (...  4.73 us
    all_to_all x1, starting transfers between devices, body(): lax.all_to_all(part, 'y', 0, 0, tiled=True).reshape(NY * slice_width, sub)  4.46 us
  transfers between devices with their start and end apart: 18, of which 6 were waited for; matrix products, arithmetic and copies ran while one was open for 11% of the time, Pallas kernels for 0%

profile of v3, /device:TPU:2, one launch (start us, length us, event | category | flops | bytes accessed | tf_op | source)
XLA Modules:
  0.0 165.0 jit_solution(10059825417966255345)
XLA Ops:
  2.1 4.5 %all-to-all-start.1 = ((bf16[4,12,288]{2,1,0:T(8,128)(2,1)}), bf16[4,12,288]{2,1,0:T(8,128)(2,1)S(1)}, u32[]{:S(2)}, u32[]{:S(2)}) async-start(bf16[4,12,288]{2,1,0:T(8,128)(2,1)} %bitcast.108), calls=%async_computation.1 | async-start | bytes 98304 | tf_op jit(solution)/shard_map/all_to_all | solution.py:57
  8.4 3.7 %all-to-all-done.1 = bf16[4,12,288]{2,1,0:T(8,128)(2,1)S(1)} async-done(((bf16[4,12,288]{2,1,0:T(8,128)(2,1)}), bf16[4,12,288]{2,1,0:T(8,128)(2,1)S(1)}, u32[]{:S(2)}, u32[]{:S(2)}) %all-to-all-start.1) | async-done | bytes 27680 | tf_op jit(solution)/shard_map/all_to_all | solution.py:57
  13.3 8.3 %all-to-all-start = ((bf16[32,144,128]{2,1,0:T(8,128)(2,1)}), bf16[32,144,128]{2,1,0:T(8,128)(2,1)S(1)}, u32[]{:S(2)}, u32[]{:S(2)}) async-start(bf16[32,144,128]{2,1,0:T(8,128)(2,1)} %broadcast_in_dim.7), calls=%async_computation | async-start | bytes 2359296 | tf_op jit(solution)/shard_map/all_to_all | solution.py:15
  21.7 36.1 %all_gather.9 = bf16[768,288]{1,0:T(8,128)(2,1)S(1)} all-gather(bf16[48,288]{1,0:T(8,128)(2,1)S(1)} %reshape.73), channel_id=1, replica_groups=mesh['y'=4,'z'=16,'x'=4,'core'=2] {'z'}, dimensions={0}, use_global_device_ids=true | all-gather | bytes 470016 | tf_op jit(solution)/shard_map/all_gather | solution.py:58
  57.7 2.1 %convolution_convert_fusion.1 = bf16[1024,288]{0,1:T(8,128)(2,1)S(1)} fusion(bf16[1024,768]{1,0:T(8,128)(2,1)} %constant.140.clone, bf16[768,288]{1,0:T(8,128)(2,1)S(1)} %all_gather.9), kind=kOutput, calls=%fused_computation.5 | convolution fusion | flops 453279744 | bytes 2605056 | tf_op jit(solution)/shard_map/dot_general | solution.py:59
  60.3 2.3 %constant_dynamic-slice_fusion.5 = (bf16[1,512,288]{1,0,2:T(2,128)(2,1)}, bf16[1,512,288]{1,0,2:T(2,128)(2,1)}) fusion(bf16[2,512,288]{1,0,2:T(2,128)(2,1)S(1)} %reshape.74, s32[]{:T(128)S(6)} %select_n.90, s32[]{:T(128)S(6)} %select_n.92), kind=kLoop, calls=%fused_computation.63 | loop fusion | bytes 1179656 | tf_op jit(solution)/shard_map/jit(dynamic_index_in_dim)/dynamic_slice | solution.py:33
  64.7 1.8 %all-gather.1 = f32[2,2,576]{2,1,0:T(2,128)S(1)} all-gather(f32[1,2,576]{2,1,0:T(2,128)S(1)} %maximum_bitcast_fusion), channel_id=2, replica_groups=mesh['y'=4,'z'=16,'x'=4,'core'=2] {'core'}, dimensions={0}, use_global_device_ids=true | all-gather | bytes 13824 | tf_op jit(solution)/shard_map/all_gather | solution.py:67
  66.6 3.4 %collective-permute-start = (f32[2,576]{1,0:T(2,128)S(1)}, f32[2,576]{1,0:T(2,128)S(1)}, u32[]{:S(2)}, u32[]{:S(2)}) collective-permute-start(f32[2,576]{1,0:T(2,128)S(1)} %get-tuple-element.25), channel_id=1, source_target_pairs={{0,2},{2,4},{4,6},{6,0},{1,3},{3,5},{5,7},{7,1},{8,10},{10,12},{12... | collective-permute-start | bytes 13832 | tf_op jit(solution)/shard_map/ppermute | solution.py:29
  70.0 2.9 %collective-permute-start.1 = (f32[2,576]{1,0:T(2,128)S(1)}, f32[2,576]{1,0:T(2,128)S(1)}, u32[]{:S(2)}, u32[]{:S(2)}) collective-permute-start(f32[2,576]{1,0:T(2,128)S(1)} %get-tuple-element.25), channel_id=1, source_target_pairs={{0,4},{2,6},{4,0},{6,2},{1,5},{3,7},{5,1},{7,3},{8,12},{10,14},{12... | collective-permute-start | bytes 13832 | tf_op jit(solution)/shard_map/ppermute | solution.py:29
  72.9 4.2 %collective-permute-start.2 = (f32[2,576]{1,0:T(2,128)S(1)}, f32[2,576]{1,0:T(2,128)S(1)}, u32[]{:S(2)}, u32[]{:S(2)}) collective-permute-start(f32[2,576]{1,0:T(2,128)S(1)} %get-tuple-element.25), channel_id=1, source_target_pairs={{0,6},{2,0},{4,2},{6,4},{1,7},{3,1},{5,3},{7,5},{8,14},{10,8},{12,... | collective-permute-start | bytes 13832 | tf_op jit(solution)/shard_map/ppermute | solution.py:29
  78.1 6.7 %all-to-all-start.2 = ((f32[16,2,288]{2,1,0:T(2,128)}), f32[16,2,288]{2,1,0:T(2,128)S(1)}, u32[]{:S(2)}, u32[]{:S(2)}) async-start(f32[16,2,288]{2,1,0:T(2,128)} %broadcast_in_dim.8), calls=%async_computation.2 | async-start | bytes 98304 | tf_op jit(solution)/shard_map/all_to_all | solution.py:15
  85.0 3.4 %collective-permute-start.3 = (f32[2,576]{1,0:T(2,128)S(1)}, f32[2,576]{1,0:T(2,128)S(1)}, u32[]{:S(2)}, u32[]{:S(2)}) collective-permute-start(f32[2,576]{1,0:T(2,128)S(1)} %get-tuple-element.23), channel_id=1, source_target_pairs={{0,128},{128,256},{256,384},{384,0},{1,129},{129,257},{257,385},{3... | collective-permute-start | bytes 13832 | tf_op jit(solution)/shard_map/ppermute | solution.py:29
  88.4 4.7 %collective-permute-start.4 = (f32[2,576]{1,0:T(2,128)S(1)}, f32[2,576]{1,0:T(2,128)S(1)}, u32[]{:S(2)}, u32[]{:S(2)}) collective-permute-start(f32[2,576]{1,0:T(2,128)S(1)} %get-tuple-element.23), channel_id=1, source_target_pairs={{0,256},{128,384},{256,0},{384,128},{1,257},{129,385},{257,1},{385... | collective-permute-start | bytes 13832 | tf_op jit(solution)/shard_map/ppermute | solution.py:29
  93.1 3.3 %collective-permute-start.5 = (f32[2,576]{1,0:T(2,128)S(1)}, f32[2,576]{1,0:T(2,128)S(1)}, u32[]{:S(2)}, u32[]{:S(2)}) collective-permute-start(f32[2,576]{1,0:T(2,128)S(1)} %get-tuple-element.23), channel_id=1, source_target_pairs={{0,384},{128,0},{256,128},{384,256},{1,385},{129,1},{257,129},{385... | collective-permute-start | bytes 13832 | tf_op jit(solution)/shard_map/ppermute | solution.py:29
  96.8 1.8 %collective-permute-done.5 = f32[2,576]{1,0:T(2,128)S(1)} collective-permute-done((f32[2,576]{1,0:T(2,128)S(1)}, f32[2,576]{1,0:T(2,128)S(1)}, u32[]{:S(2)}, u32[]{:S(2)}) %collective-permute-start.5) | collective-permute-done | bytes 4640 | tf_op jit(solution)/shard_map/ppermute | solution.py:29
  98.8 2.8 %convolution_multiply_fusion = f32[576,512]{1,0:T(8,128)} fusion(bf16[1,512,288]{1,0,2:T(2,128)(2,1)} %get-tuple-element.11, f32[576,288]{0,1:T(8,128)S(1)} %get-tuple-element.28, f32[576]{0:T(1024)S(1)} %add_reduce_fusion, f32[288]{0:T(512)S(1)} %log_add_fusion.1, f32[576]{0:T(1024)S(1)} %log_add_fusion, f32[288]{0:T(512)S(1)} %add_convert_fusion), kind=kOutput, calls=%fused_computation.1 | convolution fusion | flops 171325440 | bytes 2145024 | tf_op jit(solution)/shard_map/dot_general | solution.py:93
  101.6 1.9 %collective-permute-start.6 = (f32[576,512]{1,0:T(8,128)}, f32[576,512]{1,0:T(8,128)S(1)}, u32[]{:S(2)}, u32[]{:S(2)}) collective-permute-start(f32[576,512]{1,0:T(8,128)} %convolution_multiply_fusion), channel_id=1, source_target_pairs={{0,1},{1,0},{2,3},{3,2},{4,5},{5,4},{6,7},{7,6},{8,9},{9,8},{10,11... | collective-permute-start | bytes 3538952 | tf_op jit(solution)/shard_map/ppermute | solution.py:29
  103.6 3.1 %fusion.1 = bf16[768,288]{0,1:T(8,128)(2,1)S(1)} fusion(bf16[1024,768]{1,0:T(8,128)(2,1)} %constant.140.clone, bf16[72,8,8,128]{3,2,1,0:T(8,128)(2,1)S(1)} %bitcast.111, f32[576,288]{0,1:T(8,128)S(1)} %get-tuple-element.28, f32[576]{0:T(1024)S(1)} %add_reduce_fusion, f32[288]{0:T(512)S(1)} %log_add_fusion.1, f32[576]{0:T(1024)S(1)} %log_add_fusion, ...), kind=kOutput, calls=%fused_computation.7 | convolution fusion | flops 1162819584 | bytes 3865344 | tf_op jit(solution)/shard_map/dot_general | solution.py:81
  107.8 12.1 %all-to-all-start.3 = ((bf16[16,48,288]{2,1,0:T(8,128)(2,1)}), bf16[16,48,288]{2,1,0:T(8,128)(2,1)}, u32[]{:S(2)}, u32[]{:S(2)}) async-start(bf16[16,48,288]{2,1,0:T(8,128)(2,1)} %bitcast.28), calls=%async_computation.3 | async-start | bytes 1179648 | tf_op jit(solution)/shard_map/all_to_all | solution.py:85
  120.9 2.0 %fusion = f32[576,512]{1,0:T(8,128)S(1)} fusion(f32[576,512]{1,0:T(8,128)} %copy-done.1, bf16[1,512,288]{1,0,2:T(2,128)(2,1)S(1)} %copy-done, f32[576,288]{0,1:T(8,128)S(1)} %get-tuple-element.28, f32[576]{0:T(1024)S(1)} %add_reduce_fusion, f32[288]{0:T(512)S(1)} %log_add_fusion.1, f32[576]{0:T(1024)S(1)} %log_add_fusion, f32[288]{0:T(512)S(1)} %add_convert_fusion), kind=kOutput, calls=%fused_computation.3 | convolution fusion | flops 171620352 | bytes 3324672 | tf_op jit(solution)/shard_map/dot_general | solution.py:93
  124.3 1.9 %collective-permute-start.7 = (bf16[576,128]{1,0:T(8,128)(2,1)S(1)}, bf16[576,128]{1,0:T(8,128)(2,1)S(1)}, u32[]{:S(2)}, u32[]{:S(2)}) collective-permute-start(bf16[576,128]{1,0:T(8,128)(2,1)S(1)} %convert_bitcast_fusion.2), channel_id=1, source_target_pairs={{0,2},{2,4},{4,6},{6,0},{1,3},{3,5},{5,7},{7,1},{8,10},{10,12},{12... | collective-permute-start | bytes 442376 | tf_op jit(solution)/shard_map/ppermute | solution.py:29
  126.2 5.4 %collective-permute-start.8 = (bf16[576,128]{1,0:T(8,128)(2,1)S(1)}, bf16[576,128]{1,0:T(8,128)(2,1)S(1)}, u32[]{:S(2)}, u32[]{:S(2)}) collective-permute-start(bf16[576,128]{1,0:T(8,128)(2,1)S(1)} %convert_bitcast_fusion.1), channel_id=1, source_target_pairs={{0,4},{2,6},{4,0},{6,2},{1,5},{3,7},{5,1},{7,3},{8,12},{10,14},{12... | collective-permute-start | bytes 442376 | tf_op jit(solution)/shard_map/ppermute | solution.py:29
  131.7 1.9 %collective-permute-start.9 = (bf16[576,128]{1,0:T(8,128)(2,1)S(1)}, bf16[576,128]{1,0:T(8,128)(2,1)S(1)}, u32[]{:S(2)}, u32[]{:S(2)}) collective-permute-start(bf16[576,128]{1,0:T(8,128)(2,1)S(1)} %convert_bitcast_fusion), channel_id=1, source_target_pairs={{0,6},{2,0},{4,2},{6,4},{1,7},{3,1},{5,3},{7,5},{8,14},{10,8},{12,... | collective-permute-start | bytes 442376 | tf_op jit(solution)/shard_map/ppermute | solution.py:29
  133.7 2.2 %collective-permute-done.8 = bf16[576,128]{1,0:T(8,128)(2,1)S(1)} collective-permute-done((bf16[576,128]{1,0:T(8,128)(2,1)S(1)}, bf16[576,128]{1,0:T(8,128)(2,1)S(1)}, u32[]{:S(2)}, u32[]{:S(2)}) %collective-permute-start.8) | collective-permute-done | bytes 147488 | tf_op jit(solution)/shard_map/ppermute | solution.py:29
  135.9 3.1 %collective-permute-done.9 = bf16[576,128]{1,0:T(8,128)(2,1)S(1)} collective-permute-done((bf16[576,128]{1,0:T(8,128)(2,1)S(1)}, bf16[576,128]{1,0:T(8,128)(2,1)S(1)}, u32[]{:S(2)}, u32[]{:S(2)}) %collective-permute-start.9) | collective-permute-done | bytes 147488 | tf_op jit(solution)/shard_map/ppermute | solution.py:29
  139.1 1.9 %collective-permute-start.10 = (f32[144,128]{1,0:T(8,128)S(1)}, f32[144,128]{1,0:T(8,128)S(1)}, u32[]{:S(2)}, u32[]{:S(2)}) collective-permute-start(f32[144,128]{1,0:T(8,128)S(1)} %get-tuple-element.15), channel_id=1, source_target_pairs={{0,128},{128,256},{256,384},{384,0},{1,129},{129,257},{257,385},{3... | collective-permute-start | bytes 221192 | tf_op jit(solution)/shard_map/ppermute | solution.py:29
  141.1 5.9 %collective-permute-start.11 = (f32[144,128]{1,0:T(8,128)S(1)}, f32[144,128]{1,0:T(8,128)S(1)}, u32[]{:S(2)}, u32[]{:S(2)}) collective-permute-start(f32[144,128]{1,0:T(8,128)S(1)} %get-tuple-element.14), channel_id=1, source_target_pairs={{0,256},{128,384},{256,0},{384,128},{1,257},{129,385},{257,1},{385... | collective-permute-start | bytes 221192 | tf_op jit(solution)/shard_map/ppermute | solution.py:29
  146.9 1.9 %collective-permute-start.12 = (f32[144,128]{1,0:T(8,128)S(1)}, f32[144,128]{1,0:T(8,128)S(1)}, u32[]{:S(2)}, u32[]{:S(2)}) collective-permute-start(f32[144,128]{1,0:T(8,128)S(1)} %get-tuple-element.13), channel_id=1, source_target_pairs={{0,384},{128,0},{256,128},{384,256},{1,385},{129,1},{257,129},{385... | collective-permute-start | bytes 221192 | tf_op jit(solution)/shard_map/ppermute | solution.py:29
  148.9 3.8 %all-to-all-done.3 = bf16[16,48,288]{2,1,0:T(8,128)(2,1)} async-done(((bf16[16,48,288]{2,1,0:T(8,128)(2,1)}), bf16[16,48,288]{2,1,0:T(8,128)(2,1)}, u32[]{:S(2)}, u32[]{:S(2)}) %all-to-all-start.3) | async-done | bytes 442400 | tf_op jit(solution)/shard_map/all_to_all | solution.py:85
  152.7 1.2 convert_reduce_fusion
  154.5 3.9 %all-to-all-start.4 = ((f32[4,12,288]{2,1,0:T(8,128)}), f32[4,12,288]{2,1,0:T(8,128)S(1)}, u32[]{:S(2)}, u32[]{:S(2)}) async-start(f32[4,12,288]{2,1,0:T(8,128)} %reshape.78), calls=%async_computation.4 | async-start | bytes 196608 | tf_op jit(solution)/shard_map/all_to_all | solution.py:87
  159.1 5.1 %all-to-all-done.4 = f32[4,12,288]{2,1,0:T(8,128)S(1)} async-done(((f32[4,12,288]{2,1,0:T(8,128)}), f32[4,12,288]{2,1,0:T(8,128)S(1)}, u32[]{:S(2)}, u32[]{:S(2)}) %all-to-all-start.4) | async-done | bytes 55328 | tf_op jit(solution)/shard_map/all_to_all | solution.py:87
  (82 shorter events, 14.4 us)
Async XLA Ops:
  2.1 10.0 %all-to-all-start.1 = ((bf16[4,12,288]{2,1,0:T(8,128)(2,1)}), bf16[4,12,288]{2,1,0:T(8,128)(2,1)S(1)}, u32[]{:S(2)}, u32[]{:S(2)}) async-start(bf16[4,12,288]{2,1,0:T(8,128)(2,1)} %bitcast.108), calls=%async_computation.1 | async-start | bytes 98304 | tf_op jit(solution)/shard_map/all_to_all | solution.py:57
  13.3 49.2 %all-to-all-start = ((bf16[32,144,128]{2,1,0:T(8,128)(2,1)}), bf16[32,144,128]{2,1,0:T(8,128)(2,1)S(1)}, u32[]{:S(2)}, u32[]{:S(2)}) async-start(bf16[32,144,128]{2,1,0:T(8,128)(2,1)} %broadcast_in_dim.7), calls=%async_computation | async-start | bytes 2359296 | tf_op jit(solution)/shard_map/all_to_all | solution.py:15
  59.8 2.7 %copy-start.2 = (bf16[1024,288]{0,1:T(8,128)(2,1)}, bf16[1024,288]{0,1:T(8,128)(2,1)S(1)}, u32[]{:S(2)}) copy-start(bf16[1024,288]{0,1:T(8,128)(2,1)S(1)} %convolution_convert_fusion.1) | copy-start | bytes 1769476
  62.5 1.1 copy-start.3
  66.6 18.2 %collective-permute-start = (f32[2,576]{1,0:T(2,128)S(1)}, f32[2,576]{1,0:T(2,128)S(1)}, u32[]{:S(2)}, u32[]{:S(2)}) collective-permute-start(f32[2,576]{1,0:T(2,128)S(1)} %get-tuple-element.25), channel_id=1, source_target_pairs={{0,2},{2,4},{4,6},{6,0},{1,3},{3,5},{5,7},{7,1},{8,10},{10,12},{12... | collective-permute-start | bytes 13832 | tf_op jit(solution)/shard_map/ppermute | solution.py:29
  70.0 14.8 %collective-permute-start.1 = (f32[2,576]{1,0:T(2,128)S(1)}, f32[2,576]{1,0:T(2,128)S(1)}, u32[]{:S(2)}, u32[]{:S(2)}) collective-permute-start(f32[2,576]{1,0:T(2,128)S(1)} %get-tuple-element.25), channel_id=1, source_target_pairs={{0,4},{2,6},{4,0},{6,2},{1,5},{3,7},{5,1},{7,3},{8,12},{10,14},{12... | collective-permute-start | bytes 13832 | tf_op jit(solution)/shard_map/ppermute | solution.py:29
  72.9 12.0 %collective-permute-start.2 = (f32[2,576]{1,0:T(2,128)S(1)}, f32[2,576]{1,0:T(2,128)S(1)}, u32[]{:S(2)}, u32[]{:S(2)}) collective-permute-start(f32[2,576]{1,0:T(2,128)S(1)} %get-tuple-element.25), channel_id=1, source_target_pairs={{0,6},{2,0},{4,2},{6,4},{1,7},{3,1},{5,3},{7,5},{8,14},{10,8},{12,... | collective-permute-start | bytes 13832 | tf_op jit(solution)/shard_map/ppermute | solution.py:29
  78.1 20.6 %all-to-all-start.2 = ((f32[16,2,288]{2,1,0:T(2,128)}), f32[16,2,288]{2,1,0:T(2,128)S(1)}, u32[]{:S(2)}, u32[]{:S(2)}) async-start(f32[16,2,288]{2,1,0:T(2,128)} %broadcast_in_dim.8), calls=%async_computation.2 | async-start | bytes 98304 | tf_op jit(solution)/shard_map/all_to_all | solution.py:15
  85.0 11.7 %collective-permute-start.3 = (f32[2,576]{1,0:T(2,128)S(1)}, f32[2,576]{1,0:T(2,128)S(1)}, u32[]{:S(2)}, u32[]{:S(2)}) collective-permute-start(f32[2,576]{1,0:T(2,128)S(1)} %get-tuple-element.23), channel_id=1, source_target_pairs={{0,128},{128,256},{256,384},{384,0},{1,129},{129,257},{257,385},{3... | collective-permute-start | bytes 13832 | tf_op jit(solution)/shard_map/ppermute | solution.py:29
  88.4 8.3 %collective-permute-start.4 = (f32[2,576]{1,0:T(2,128)S(1)}, f32[2,576]{1,0:T(2,128)S(1)}, u32[]{:S(2)}, u32[]{:S(2)}) collective-permute-start(f32[2,576]{1,0:T(2,128)S(1)} %get-tuple-element.23), channel_id=1, source_target_pairs={{0,256},{128,384},{256,0},{384,128},{1,257},{129,385},{257,1},{385... | collective-permute-start | bytes 13832 | tf_op jit(solution)/shard_map/ppermute | solution.py:29
  93.1 5.5 %collective-permute-start.5 = (f32[2,576]{1,0:T(2,128)S(1)}, f32[2,576]{1,0:T(2,128)S(1)}, u32[]{:S(2)}, u32[]{:S(2)}) collective-permute-start(f32[2,576]{1,0:T(2,128)S(1)} %get-tuple-element.23), channel_id=1, source_target_pairs={{0,384},{128,0},{256,128},{384,256},{1,385},{129,1},{257,129},{385... | collective-permute-start | bytes 13832 | tf_op jit(solution)/shard_map/ppermute | solution.py:29
  101.6 18.2 %collective-permute-start.6 = (f32[576,512]{1,0:T(8,128)}, f32[576,512]{1,0:T(8,128)S(1)}, u32[]{:S(2)}, u32[]{:S(2)}) collective-permute-start(f32[576,512]{1,0:T(8,128)} %convolution_multiply_fusion), channel_id=1, source_target_pairs={{0,1},{1,0},{2,3},{3,2},{4,5},{5,4},{6,7},{7,6},{8,9},{9,8},{10,11... | collective-permute-start | bytes 3538952 | tf_op jit(solution)/shard_map/ppermute | solution.py:29
  106.7 14.2 %copy-start = (bf16[1,512,288]{1,0,2:T(2,128)(2,1)S(1)}, bf16[1,512,288]{1,0,2:T(2,128)(2,1)}, u32[]{:S(2)}) copy-start(bf16[1,512,288]{1,0,2:T(2,128)(2,1)} %get-tuple-element.10) | copy-start | bytes 884740
  107.8 45.0 %all-to-all-start.3 = ((bf16[16,48,288]{2,1,0:T(8,128)(2,1)}), bf16[16,48,288]{2,1,0:T(8,128)(2,1)}, u32[]{:S(2)}, u32[]{:S(2)}) async-start(bf16[16,48,288]{2,1,0:T(8,128)(2,1)} %bitcast.28), calls=%async_computation.3 | async-start | bytes 1179648 | tf_op jit(solution)/shard_map/all_to_all | solution.py:85
  119.8 1.0 copy-start.1
  124.3 9.4 %collective-permute-start.7 = (bf16[576,128]{1,0:T(8,128)(2,1)S(1)}, bf16[576,128]{1,0:T(8,128)(2,1)S(1)}, u32[]{:S(2)}, u32[]{:S(2)}) collective-permute-start(bf16[576,128]{1,0:T(8,128)(2,1)S(1)} %convert_bitcast_fusion.2), channel_id=1, source_target_pairs={{0,2},{2,4},{4,6},{6,0},{1,3},{3,5},{5,7},{7,1},{8,10},{10,12},{12... | collective-permute-start | bytes 442376 | tf_op jit(solution)/shard_map/ppermute | solution.py:29
  126.2 9.7 %collective-permute-start.8 = (bf16[576,128]{1,0:T(8,128)(2,1)S(1)}, bf16[576,128]{1,0:T(8,128)(2,1)S(1)}, u32[]{:S(2)}, u32[]{:S(2)}) collective-permute-start(bf16[576,128]{1,0:T(8,128)(2,1)S(1)} %convert_bitcast_fusion.1), channel_id=1, source_target_pairs={{0,4},{2,6},{4,0},{6,2},{1,5},{3,7},{5,1},{7,3},{8,12},{10,14},{12... | collective-permute-start | bytes 442376 | tf_op jit(solution)/shard_map/ppermute | solution.py:29
  131.7 7.3 %collective-permute-start.9 = (bf16[576,128]{1,0:T(8,128)(2,1)S(1)}, bf16[576,128]{1,0:T(8,128)(2,1)S(1)}, u32[]{:S(2)}, u32[]{:S(2)}) collective-permute-start(bf16[576,128]{1,0:T(8,128)(2,1)S(1)} %convert_bitcast_fusion), channel_id=1, source_target_pairs={{0,6},{2,0},{4,2},{6,4},{1,7},{3,1},{5,3},{7,5},{8,14},{10,8},{12,... | collective-permute-start | bytes 442376 | tf_op jit(solution)/shard_map/ppermute | solution.py:29
  139.1 19.3 %collective-permute-start.10 = (f32[144,128]{1,0:T(8,128)S(1)}, f32[144,128]{1,0:T(8,128)S(1)}, u32[]{:S(2)}, u32[]{:S(2)}) collective-permute-start(f32[144,128]{1,0:T(8,128)S(1)} %get-tuple-element.15), channel_id=1, source_target_pairs={{0,128},{128,256},{256,384},{384,0},{1,129},{129,257},{257,385},{3... | collective-permute-start | bytes 221192 | tf_op jit(solution)/shard_map/ppermute | solution.py:29
  141.1 17.3 %collective-permute-start.11 = (f32[144,128]{1,0:T(8,128)S(1)}, f32[144,128]{1,0:T(8,128)S(1)}, u32[]{:S(2)}, u32[]{:S(2)}) collective-permute-start(f32[144,128]{1,0:T(8,128)S(1)} %get-tuple-element.14), channel_id=1, source_target_pairs={{0,256},{128,384},{256,0},{384,128},{1,257},{129,385},{257,1},{385... | collective-permute-start | bytes 221192 | tf_op jit(solution)/shard_map/ppermute | solution.py:29
  146.9 11.5 %collective-permute-start.12 = (f32[144,128]{1,0:T(8,128)S(1)}, f32[144,128]{1,0:T(8,128)S(1)}, u32[]{:S(2)}, u32[]{:S(2)}) collective-permute-start(f32[144,128]{1,0:T(8,128)S(1)} %get-tuple-element.13), channel_id=1, source_target_pairs={{0,384},{128,0},{256,128},{384,256},{1,385},{129,1},{257,129},{385... | collective-permute-start | bytes 221192 | tf_op jit(solution)/shard_map/ppermute | solution.py:29
  154.5 9.7 %all-to-all-start.4 = ((f32[4,12,288]{2,1,0:T(8,128)}), f32[4,12,288]{2,1,0:T(8,128)S(1)}, u32[]{:S(2)}, u32[]{:S(2)}) async-start(f32[4,12,288]{2,1,0:T(8,128)} %reshape.78), calls=%async_computation.4 | async-start | bytes 196608 | tf_op jit(solution)/shard_map/all_to_all | solution.py:87

commit v4 on v0

v4 whole, which is shorter than its diff:
```python
import jax
import jax.numpy as jnp
import numpy as np
from jax import lax
from jax.experimental import pallas as pl
from jax.experimental.pallas import tpu as pltpu
from jax.sharding import Mesh, PartitionSpec as P

logit_scale = 20.0
f32 = jnp.float32
bf16 = jnp.bfloat16
NY, NZ, NX, NC = 4, 16, 4, 2
ROWS, WIDTH = 144, 96
COLS, SLICE = 1152, 12
TALL, SUB = NY * ROWS, COLS // NY
HALF = NX * 128
THIRD = NZ * NY * SLICE // NC
BLOCKS = [(0, 128), (128, 128), (256, 128), (384, 128), (512, 64)]
MSG = ROWS + 48
NT = (((1,), (1,)), ((), ()))


def call(kernel, outs, *args, scratch=(), flops=0):
    bytes_accessed = sum(int(np.prod(a.shape)) * a.dtype.itemsize for a in (*args, *outs))
    vmem = pl.BlockSpec(memory_space=pltpu.VMEM)
    smem = pl.BlockSpec(memory_space=pltpu.SMEM)
    return pl.pallas_call(
        kernel,
        out_shape=outs,
        in_specs=[smem if a.ndim == 1 else vmem for a in args],
        out_specs=[vmem] * len(outs),
        scratch_shapes=list(scratch),
        compiler_params=pltpu.CompilerParams(vmem_limit_bytes=32 << 20),
        cost_estimate=pl.CostEstimate(flops=flops, bytes_accessed=bytes_accessed, transcendentals=0),
    )(*args)


def shape(dtype, *dims):
    return jax.ShapeDtypeStruct(dims, dtype)


def placement():
    table = np.zeros((NX, 128, NZ // NC, NY, SLICE), np.float32)
    for x in range(NX):
        for lane in range(WIDTH):
            table[x, lane, lane // SLICE, x, lane % SLICE] = 1.0
    return table.reshape(HALF, THIRD)


def tile_kernel(parts, passages, place, logits, row_pairs, col_pairs, query_full, passage_full):
    for y in range(NY):
        for b in range(NC * NX):
            query_full[y * ROWS : (y + 1) * ROWS, b * 128 : (b + 1) * 128] = parts[y * NC * NX + b]
    for c in range(NC):
        placed = jnp.dot(place[...], passages[c * THIRD : (c + 1) * THIRD], preferred_element_type=f32)
        passage_full[c * HALF : (c + 1) * HALF] = placed.astype(bf16)
    lane = lax.broadcasted_iota(jnp.int32, (128, 128), 1)
    packed = jnp.ones((128, 128), f32)
    col_top = None
    for j, (start, size) in enumerate(BLOCKS):
        scores = logit_scale * jnp.dot(
            query_full[start : start + size], passage_full[...], preferred_element_type=f32
        )
        logits[start : start + size] = scores
        top = jnp.max(scores, axis=1, keepdims=True)
        total = jnp.sum(jnp.exp(scores - top), axis=1, keepdims=True)
        if size < 128:
            fill = jnp.ones((128 - size, 1), f32)
            top, total = jnp.concatenate([top, fill], axis=0), jnp.concatenate([total, fill], axis=0)
        packed = jnp.where(lane == j, top, jnp.where(lane == j + 8, total, packed))
        peak = jnp.max(scores, axis=0, keepdims=True)
        col_top = peak if col_top is None else jnp.maximum(col_top, peak)
    turned = packed.T[:16]
    for i in range(NX * NC):
        row_pairs[i] = turned
    col_sum = jnp.zeros((1, SUB), f32)
    for start, size in BLOCKS:
        col_sum += jnp.sum(jnp.exp(logits[start : start + size] - col_top), axis=0, keepdims=True)
    fill = jnp.ones((1, 384 - SUB), f32)
    both = [jnp.concatenate([v, fill], axis=1) for v in (col_top, col_sum)]
    lines = [v[:, b * 128 : (b + 1) * 128] for v in both for b in range(3)]
    lines = jnp.concatenate(lines + [jnp.ones((2, 128), f32)], axis=0)
    for i in range(NZ):
        col_pairs[i] = lines


def turn_kernel(query_full, place, ids, placed, hits):
    for c in range(NC):
        half = query_full[:, c * HALF : (c + 1) * HALF]
        placed[c * THIRD : (c + 1) * THIRD] = lax.dot_general(
            place[...], half, NT, preferred_element_type=f32
        ).astype(bf16)
    spare = query_full[:, :128].astype(f32)
    target = spare[:, WIDTH : WIDTH + 1] * 128.0 + spare[:, WIDTH + 1 : WIDTH + 2]
    hits[...] = jnp.where(target == ids[...], 2.0, 0.0)


def passage_kernel(logits, hits, placed, row_pairs, col_pairs, dlogits, terms):
    top, total = row_pairs[:, :8], row_pairs[:, 8:]
    peak = jnp.max(top, axis=0)
    row_lse = peak + jnp.log(jnp.sum(total * jnp.exp(top - peak[None]), axis=0))
    row_lse = jnp.concatenate([row_lse, jnp.zeros((120, 128), f32)], axis=0).T
    pairs = col_pairs[...]
    top, total = pairs[:, 0:3], pairs[:, 3:6]
    peak = jnp.max(top, axis=0)
    col_lse = peak + jnp.log(jnp.sum(total * jnp.exp(top - peak[None]), axis=0))
    col_lse = jnp.concatenate([col_lse[b : b + 1] for b in range(3)], axis=1)[:, :SUB]
    for j, (start, size) in enumerate(BLOCKS):
        scores = logits[start : start + size]
        slope = jnp.exp(scores - row_lse[:size, j : j + 1]) + jnp.exp(scores - col_lse)
        dlogits[start : start + size] = (slope - hits[start : start + size]).astype(bf16)
    for start in range(0, NC * THIRD, 192):
        part = jnp.dot(placed[start : start + 192], dlogits[...], preferred_element_type=f32)
        terms[start : start + 192] = (logit_scale * part).astype(bf16)


def theirs_kernel(place, dlogits, passage_full, theirs):
    core = place[0]
    half = passage_full[pl.ds(pl.multiple_of((1 - core) * HALF, HALF), HALF)]
    theirs[...] = logit_scale * lax.dot_general(dlogits[...], half, NT, preferred_element_type=f32)


def ours_kernel(place, dlogits, passage_full, theirs, own, *rest):
    outs, total = rest[:-1], rest[-1]
    core, x = place[0], place[1]
    half = passage_full[pl.ds(pl.multiple_of(core * HALF, HALF), HALF)]
    total[...] = theirs[...] + logit_scale * lax.dot_general(
        dlogits[...], half, NT, preferred_element_type=f32
    )
    own[...] = total[:, pl.ds(pl.multiple_of(x * 128, 128), 128)]
    for step, out in enumerate(outs, 1):
        lanes = pl.ds(pl.multiple_of(lax.rem(x + step, NX) * 128, 128), 128)
        out[...] = total[:, lanes].astype(bf16)


def fold_kernel(terms, own, *rest):
    came, message, total = rest[:-2], rest[-2], rest[-1]
    total[:, :SUB] = jnp.sum(terms[...].astype(f32), axis=0)
    total[:, SUB:] = jnp.zeros((48, 384 - SUB), f32)
    for y in range(NY):
        rows = slice(y * ROWS, (y + 1) * ROWS)
        message[y, :ROWS] = own[rows] + sum(c[rows].astype(f32) for c in came)
        for b in range(3):
            piece = total[y * SLICE : (y + 1) * SLICE, b * 128 : (b + 1) * 128]
            message[y, ROWS + b * 16 : ROWS + b * 16 + SLICE] = piece
            message[y, ROWS + b * 16 + SLICE : ROWS + b * 16 + 16] = jnp.zeros((16 - SLICE, 128), f32)


def share(x, axes, n):
    return lax.all_to_all(jnp.broadcast_to(x[None], (n, *x.shape)), axes, 0, 0, tiled=True)


def merge(pairs):
    top, total = pairs[:, :8], pairs[:, 8:]
    peak = jnp.max(top, axis=0)
    return jnp.concatenate([peak, jnp.sum(total * jnp.exp(top - peak[None]), axis=0)])


def around(x, axis, n, step):
    return lax.ppermute(x, axis, [(i, (i + step) % n) for i in range(n)])


def body(queries, passages, positive):
    table = placement()
    place, place_t = jnp.asarray(table, bf16), jnp.asarray(table.T, bf16)
    where = jnp.stack([lax.axis_index("core"), lax.axis_index("x")]).astype(jnp.int32)

    spare = jnp.stack([positive // 128, positive % 128], axis=1).astype(bf16)
    message = jnp.concatenate([queries, spare, jnp.zeros((ROWS, 126 - WIDTH), bf16)], axis=1)
    parts = share(message, ("y", "core", "x"), NY * NC * NX)

    part = passages.T.reshape(SLICE, NY, SUB).transpose(1, 0, 2)
    part = lax.all_to_all(part, "y", 0, 0, tiled=True).reshape(NY * SLICE, SUB)
    passage_part = lax.all_gather(part, "z", axis=0, tiled=True)

    logits, row_pairs, col_pairs, query_full, passage_full = call(
        tile_kernel,
        [
            shape(f32, TALL, SUB),
            shape(f32, NX * NC, 16, 128),
            shape(f32, NZ, 8, 128),
            shape(bf16, TALL, NC * HALF),
            shape(bf16, NC * HALF, SUB),
        ],
        parts,
        passage_part,
        place,
        flops=2 * TALL * SUB * NC * HALF,
    )
    row_pairs = lax.all_to_all(row_pairs, ("x", "core"), 0, 0, tiled=True)
    col_pairs = lax.all_to_all(col_pairs, "z", 0, 0, tiled=True)
    row_pairs = lax.all_gather(merge(row_pairs), "y")

    block = (lax.axis_index("x") * NC + lax.axis_index("core")) * NY + lax.axis_index("y")
    ids = (block * SUB + jnp.arange(SUB, dtype=jnp.int32)).astype(f32)[None]
    placed, hits = call(
        turn_kernel,
        [shape(bf16, NC * THIRD, TALL), shape(f32, TALL, SUB)],
        query_full,
        place_t,
        ids,
        flops=2 * TALL * HALF * THIRD * NC,
    )
    dlogits, terms = call(
        passage_kernel,
        [shape(bf16, TALL, SUB), shape(bf16, NC * THIRD, SUB)],
        logits,
        hits,
        placed,
        row_pairs,
        col_pairs,
        flops=2 * TALL * SUB * NC * THIRD,
    )
    terms = lax.all_to_all(terms.reshape(NZ, NY * SLICE, SUB), "z", 0, 0, tiled=True)

    (theirs,) = call(
        theirs_kernel, [shape(f32, TALL, HALF)], where, dlogits, passage_full, flops=2 * TALL * SUB * HALF
    )
    theirs = around(theirs, "core", NC, 1)
    own, *others = call(
        ours_kernel,
        [shape(f32, TALL, 128)] + [shape(bf16, TALL, 128)] * (NX - 1),
        where,
        dlogits,
        passage_full,
        theirs,
        scratch=[pltpu.VMEM((TALL, HALF), f32)],
        flops=2 * TALL * SUB * HALF,
    )
    came = [around(other, "x", NX, step) for step, other in enumerate(others, 1)]

    (message,) = call(fold_kernel, [shape(f32, NY, MSG, 128)], terms, own, *came, scratch=[pltpu.VMEM((48, 384), f32)])
    message = lax.all_to_all(message, "y", 0, 0, tiled=True)
    query_grad = jnp.sum(message[:, :ROWS, :WIDTH], axis=0)
    blocks = message[:, ROWS:].reshape(NY, 3, 16, 128)[:, :, :SLICE].transpose(2, 0, 1, 3)
    passage_grad = blocks.reshape(SLICE, NY, 384)[:, :, :SUB].reshape(SLICE, COLS).T
    return (query_grad, passage_grad)


def solution(mesh):
    chips = Mesh(mesh.devices.reshape(NY, NZ, NX, NC), ("y", "z", "x", "core"))
    yz, xc = ("y", "z"), ("x", "core")
    return jax.shard_map(
        body,
        mesh=chips,
        in_specs=(P(yz, xc), P(xc, yz), P(yz)),
        out_specs=(P(yz, xc), P(xc, yz)),
        check_vma=False,
    )
```

time: 732 us -> 148 us (0.20)
  the two profiles are of different devices: /device:TPU:16 before, /device:TPU:2 now
where the time goes in v4:
time: 148 us; the launch traced here: 147 us
  blocking collectives  59.3 us (40%)
  starting transfers between devices  47.5 us (32%)
  waiting for transfers between devices  19.7 us (13%)
  local copies, waits for them, and re-layouts  10.3 us (7%)
  Pallas kernels  7.59 us (5%)
  other arithmetic  2.32 us (2%)
    all_gather x1, blocking collectives, body(): passage_part = lax.all_gather(part, 'z', axis=0, tiled=True)  36.1 us
    all_gather x1, blocking collectives, body(): row_pairs = lax.all_gather(merge(row_pairs), 'y')  12 us
    ppermute x4, starting transfers between devices, around(): return lax.ppermute(x, axis, [(i, (i + step) % n) for i in range(n)])  11.7 us
    all_to_all x1, starting transfers between devices, body(): lax.all_to_all(terms.reshape(NZ, NY * SLICE, SUB), 'z', 0, 0, tiled=True)  11.3 us
    all_to_all x1, blocking collectives, body(): message = lax.all_to_all(message, 'y', 0, 0, tiled=True)  11.2 us
    all_to_all x1, starting transfers between devices, share(): lax.all_to_all(jnp.broadcast_to(x[None], (n, *x.shape)), axes, 0, 0, tile...  8.42 us
    ppermute x4, waiting for transfers between devices, around(): return lax.ppermute(x, axis, [(i, (i + step) % n) for i in range(n)])  7.73 us
    pallas_call x6, Pallas kernels, call(): pl.pallas_call(kernel, out_shape=outs, in_specs=[smem if a.ndim == 1 else...  7.59 us
  transfers between devices with their start and end apart: 9, of which 7 were waited for; matrix products, arithmetic and copies ran while one was open for 1% of the time, Pallas kernels for 2%

profile of v4, /device:TPU:2, one launch (start us, length us, event | category | flops | bytes accessed | tf_op | source)
XLA Modules:
  0.0 147.5 jit_solution(15021499003032511506)
XLA Ops:
  0.6 0.9 reshape.34
  2.1 4.5 %all-to-all-start.1 = ((bf16[4,12,288]{2,1,0:T(8,128)(2,1)}), bf16[4,12,288]{2,1,0:T(8,128)(2,1)S(1)}, u32[]{:S(2)}, u32[]{:S(2)}) async-start(bf16[4,12,288]{2,1,0:T(8,128)(2,1)} %bitcast.12), calls=%async_computation.1 | async-start | bytes 98304 | tf_op jit(solution)/shard_map/all_to_all | solution.py:173
  7.6 0.9 maximum_maximum_fusion
  8.4 3.7 %all-to-all-done.1 = bf16[4,12,288]{2,1,0:T(8,128)(2,1)S(1)} async-done(((bf16[4,12,288]{2,1,0:T(8,128)(2,1)}), bf16[4,12,288]{2,1,0:T(8,128)(2,1)S(1)}, u32[]{:S(2)}, u32[]{:S(2)}) %all-to-all-start.1) | async-done | bytes 27680 | tf_op jit(solution)/shard_map/all_to_all | solution.py:173
  12.1 1.2 broadcast_in_dim.5
  13.4 8.4 %all-to-all-start = ((bf16[32,144,128]{2,1,0:T(8,128)(2,1)}), bf16[32,144,128]{2,1,0:T(8,128)(2,1)S(1)}, u32[]{:S(2)}, u32[]{:S(2)}) async-start(bf16[32,144,128]{2,1,0:T(8,128)(2,1)} %broadcast_in_dim.5), calls=%async_computation | async-start | bytes 2359296 | tf_op jit(solution)/shard_map/all_to_all | solution.py:150
  21.8 36.1 %all_gather.9.passages = bf16[768,288]{1,0:T(8,128)(2,1)S(1)} all-gather(bf16[48,288]{1,0:T(8,128)(2,1)S(1)} %reshape.35), channel_id=1, replica_groups=mesh['y'=4,'z'=16,'x'=4,'core'=2] {'z'}, dimensions={0}, use_global_device_ids=true | all-gather | bytes 470016 | tf_op jit(solution)/shard_map/all_gather | solution.py:174
  57.9 2.4 %shard_map.68 = (f32[576,288]{1,0:T(8,128)S(1)}, f32[8,16,128]{2,1,0:T(8,128)}, f32[16,8,128]{2,1,0:T(8,128)}, bf16[576,1024]{1,0:T(8,128)(2,1)S(1)}, bf16[1024,288]{1,0:T(8,128)(2,1)S(1)}) custom-call(bf16[32,144,128]{2,1,0:T(8,128)(2,1)S(1)} %all-to-all-done.parts, bf16[768,288]{1,0:T(8,128)(2,1)S(1)} %all_gather.9.passages, bf16[512,384]{1,0:T(8,128)(2,1)S(1)} %copy-done.4), custom_call_target="tpu_custom_call" | custom-call | flops 339738624 | bytes 4579328 | tf_op jit(solution)/shard_map/pallas_call | solution.py:27
  60.3 0.9 copy-done
  61.3 1.1 copy-done.5
  62.3 4.8 %all-to-all-start.2 = ((f32[8,16,128]{2,1,0:T(8,128)}), f32[8,16,128]{2,1,0:T(8,128)S(1)}, u32[]{:S(2)}, u32[]{:S(2)}) async-start(f32[8,16,128]{2,1,0:T(8,128)} %get-tuple-element.19), calls=%async_computation.2 | async-start | bytes 131072 | tf_op jit(solution)/shard_map/all_to_all | solution.py:190
  67.1 1.3 copy-done.6
  68.4 0.8 shard_map.69
  69.2 0.9 copy-done.2
  70.1 1.1 all-to-all-done.2
  71.3 6.7 %all-to-all-start.3 = ((f32[16,8,128]{2,1,0:T(8,128)}), f32[16,8,128]{2,1,0:T(8,128)S(1)}, u32[]{:S(2)}, u32[]{:S(2)}) async-start(f32[16,8,128]{2,1,0:T(8,128)} %get-tuple-element.20), calls=%async_computation.3 | async-start | bytes 131072 | tf_op jit(solution)/shard_map/all_to_all | solution.py:191
  78.1 12.0 %all-gather = f32[64,128]{1,0:T(8,128)S(1)} all-gather(f32[16,128]{1,0:T(8,128)S(1)} %pad_maximum_fusion), channel_id=2, replica_groups=mesh['y'=4,'z'=16,'x'=4,'core'=2] {'y'}, dimensions={0}, use_global_device_ids=true | all-gather | bytes 40960 | tf_op jit(solution)/shard_map/all_gather | solution.py:192
  90.8 1.2 copy-done.1
  91.9 1.2 copy-done.3
  93.1 1.9 %shard_map.70 = (bf16[576,288]{1,0:T(8,128)(2,1)S(1)}, bf16[768,288]{1,0:T(8,128)(2,1)}) custom-call(f32[576,288]{1,0:T(8,128)S(1)} %copy-done.1, f32[576,288]{1,0:T(8,128)S(1)} %copy-done.3, bf16[768,576]{1,0:T(8,128)(2,1)S(1)} %get-tuple-element.18.placed, f32[4,16,128]{2,1,0:T(8,128)S(1)} %bitcast.15, f32[16,8,128]{2,1,0:T(8,128)S(1)} %all-to-all-done.3.col_pairs), custom_call_target="tpu_custom_call" | custom-call | flops 254803968 | bytes 3084288 | tf_op jit(solution)/shard_map/pallas_call | solution.py:27
  95.0 11.3 %all-to-all-start.4 = ((bf16[16,48,288]{2,1,0:T(8,128)(2,1)}), bf16[16,48,288]{2,1,0:T(8,128)(2,1)S(1)}, u32[]{:S(2)}, u32[]{:S(2)}) async-start(bf16[16,48,288]{2,1,0:T(8,128)(2,1)} %bitcast.3), calls=%async_computation.4 | async-start | bytes 1179648 | tf_op jit(solution)/shard_map/all_to_all | solution.py:214
  106.4 1.0 shard_map.71
  107.5 1.9 %collective-permute-start = (f32[576,512]{1,0:T(8,128)S(1)}, f32[576,512]{1,0:T(8,128)S(1)}, u32[]{:S(2)}, u32[]{:S(2)}) collective-permute-start(f32[576,512]{1,0:T(8,128)S(1)} %shard_map.71), channel_id=1, source_target_pairs={{0,1},{1,0},{2,3},{3,2},{4,5},{5,4},{6,7},{7,6},{8,9},{9,8},{10,11... | collective-permute-start | bytes 3538952 | tf_op jit(solution)/shard_map/ppermute | solution.py:160
  109.4 2.8 %collective-permute-done.theirs = f32[576,512]{1,0:T(8,128)S(1)} collective-permute-done((f32[576,512]{1,0:T(8,128)S(1)}, f32[576,512]{1,0:T(8,128)S(1)}, u32[]{:S(2)}, u32[]{:S(2)}) %collective-permute-start) | collective-permute-done | bytes 1179680 | tf_op jit(solution)/shard_map/ppermute | solution.py:160
  112.2 1.2 shard_map.72
  113.4 2.3 %collective-permute-start.1 = (bf16[576,128]{1,0:T(8,128)(2,1)S(1)}, bf16[576,128]{1,0:T(8,128)(2,1)S(1)}, u32[]{:S(2)}, u32[]{:S(2)}) collective-permute-start(bf16[576,128]{1,0:T(8,128)(2,1)S(1)} %get-tuple-element.25), channel_id=1, source_target_pairs={{0,2},{2,4},{4,6},{6,0},{1,3},{3,5},{5,7},{7,1},{8,10},{10,12},{12... | collective-permute-start | bytes 442376 | tf_op jit(solution)/shard_map/ppermute | solution.py:160
  115.7 5.1 %collective-permute-start.2 = (bf16[576,128]{1,0:T(8,128)(2,1)S(1)}, bf16[576,128]{1,0:T(8,128)(2,1)S(1)}, u32[]{:S(2)}, u32[]{:S(2)}) collective-permute-start(bf16[576,128]{1,0:T(8,128)(2,1)S(1)} %get-tuple-element.26), channel_id=1, source_target_pairs={{0,4},{2,6},{4,0},{6,2},{1,5},{3,7},{5,1},{7,3},{8,12},{10,14},{12... | collective-permute-start | bytes 442376 | tf_op jit(solution)/shard_map/ppermute | solution.py:160
  120.8 2.5 %collective-permute-start.3 = (bf16[576,128]{1,0:T(8,128)(2,1)S(1)}, bf16[576,128]{1,0:T(8,128)(2,1)S(1)}, u32[]{:S(2)}, u32[]{:S(2)}) collective-permute-start(bf16[576,128]{1,0:T(8,128)(2,1)S(1)} %get-tuple-element.27), channel_id=1, source_target_pairs={{0,6},{2,0},{4,2},{6,4},{1,7},{3,1},{5,3},{7,5},{8,14},{10,8},{12,... | collective-permute-start | bytes 442376 | tf_op jit(solution)/shard_map/ppermute | solution.py:160
  123.3 1.9 %collective-permute-done.2.rest_1_ = bf16[576,128]{1,0:T(8,128)(2,1)S(1)} collective-permute-done((bf16[576,128]{1,0:T(8,128)(2,1)S(1)}, bf16[576,128]{1,0:T(8,128)(2,1)S(1)}, u32[]{:S(2)}, u32[]{:S(2)}) %collective-permute-start.2) | collective-permute-done | bytes 147488 | tf_op jit(solution)/shard_map/ppermute | solution.py:160
  125.2 3.0 %collective-permute-done.3.rest_2_ = bf16[576,128]{1,0:T(8,128)(2,1)S(1)} collective-permute-done((bf16[576,128]{1,0:T(8,128)(2,1)S(1)}, bf16[576,128]{1,0:T(8,128)(2,1)S(1)}, u32[]{:S(2)}, u32[]{:S(2)}) %collective-permute-start.3) | collective-permute-done | bytes 147488 | tf_op jit(solution)/shard_map/ppermute | solution.py:160
  128.2 6.4 %all-to-all-done.4.terms = bf16[16,48,288]{2,1,0:T(8,128)(2,1)S(1)} async-done(((bf16[16,48,288]{2,1,0:T(8,128)(2,1)}), bf16[16,48,288]{2,1,0:T(8,128)(2,1)S(1)}, u32[]{:S(2)}, u32[]{:S(2)}) %all-to-all-start.4) | async-done | bytes 442400 | tf_op jit(solution)/shard_map/all_to_all | solution.py:214
  134.8 11.2 %all_to_all.30 = f32[4,192,128]{2,1,0:T(8,128)S(1)} all-to-all(f32[4,192,128]{2,1,0:T(8,128)S(1)} %shard_map.73), channel_id=1, replica_groups=mesh['y'=4,'z'=16,'x'=4,'core'=2] {'y'}, dimensions={0} | all-to-all | bytes 786432 | tf_op jit(solution)/shard_map/all_to_all | solution.py:233
  (31 shorter events, 4.1 us)
Async XLA Ops:
  2.1 10.0 %all-to-all-start.1 = ((bf16[4,12,288]{2,1,0:T(8,128)(2,1)}), bf16[4,12,288]{2,1,0:T(8,128)(2,1)S(1)}, u32[]{:S(2)}, u32[]{:S(2)}) async-start(bf16[4,12,288]{2,1,0:T(8,128)(2,1)} %bitcast.12), calls=%async_computation.1 | async-start | bytes 98304 | tf_op jit(solution)/shard_map/all_to_all | solution.py:173
  13.4 44.5 %copy-start.4 = (bf16[512,384]{1,0:T(8,128)(2,1)S(1)}, bf16[512,384]{1,0:T(8,128)(2,1)}, u32[]{:S(2)}) copy-start(bf16[512,384]{1,0:T(8,128)(2,1)} %constant.56.clone.place) | copy-start | bytes 1179652
  13.4 44.5 %all-to-all-start = ((bf16[32,144,128]{2,1,0:T(8,128)(2,1)}), bf16[32,144,128]{2,1,0:T(8,128)(2,1)S(1)}, u32[]{:S(2)}, u32[]{:S(2)}) async-start(bf16[32,144,128]{2,1,0:T(8,128)(2,1)} %broadcast_in_dim.5), calls=%async_computation | async-start | bytes 2359296 | tf_op jit(solution)/shard_map/all_to_all | solution.py:150
  57.9 9.3 %copy-start.7 = (bf16[384,512]{1,0:T(8,128)(2,1)S(1)}, bf16[384,512]{1,0:T(8,128)(2,1)}, u32[]{:S(2)}) copy-start(bf16[384,512]{1,0:T(8,128)(2,1)} %constant.57.clone.place) | copy-start | bytes 1179652
  60.3 0.9 copy-start
  61.3 1.1 copy-start.5
  62.3 9.0 %all-to-all-start.2 = ((f32[8,16,128]{2,1,0:T(8,128)}), f32[8,16,128]{2,1,0:T(8,128)S(1)}, u32[]{:S(2)}, u32[]{:S(2)}) async-start(f32[8,16,128]{2,1,0:T(8,128)} %get-tuple-element.19), calls=%async_computation.2 | async-start | bytes 131072 | tf_op jit(solution)/shard_map/all_to_all | solution.py:190
  67.1 1.3 copy-start.6
  69.2 0.9 copy-start.2
  71.3 19.5 %all-to-all-start.3 = ((f32[16,8,128]{2,1,0:T(8,128)}), f32[16,8,128]{2,1,0:T(8,128)S(1)}, u32[]{:S(2)}, u32[]{:S(2)}) async-start(f32[16,8,128]{2,1,0:T(8,128)} %get-tuple-element.20), calls=%async_computation.3 | async-start | bytes 131072 | tf_op jit(solution)/shard_map/all_to_all | solution.py:191
  90.8 1.2 copy-start.1
  91.9 1.2 copy-start.3
  95.0 39.5 %all-to-all-start.4 = ((bf16[16,48,288]{2,1,0:T(8,128)(2,1)}), bf16[16,48,288]{2,1,0:T(8,128)(2,1)S(1)}, u32[]{:S(2)}, u32[]{:S(2)}) async-start(bf16[16,48,288]{2,1,0:T(8,128)(2,1)} %bitcast.3), calls=%async_computation.4 | async-start | bytes 1179648 | tf_op jit(solution)/shard_map/all_to_all | solution.py:214
  107.5 4.7 %collective-permute-start = (f32[576,512]{1,0:T(8,128)S(1)}, f32[576,512]{1,0:T(8,128)S(1)}, u32[]{:S(2)}, u32[]{:S(2)}) collective-permute-start(f32[576,512]{1,0:T(8,128)S(1)} %shard_map.71), channel_id=1, source_target_pairs={{0,1},{1,0},{2,3},{3,2},{4,5},{5,4},{6,7},{7,6},{8,9},{9,8},{10,11... | collective-permute-start | bytes 3538952 | tf_op jit(solution)/shard_map/ppermute | solution.py:160
  113.4 9.8 %collective-permute-start.1 = (bf16[576,128]{1,0:T(8,128)(2,1)S(1)}, bf16[576,128]{1,0:T(8,128)(2,1)S(1)}, u32[]{:S(2)}, u32[]{:S(2)}) collective-permute-start(bf16[576,128]{1,0:T(8,128)(2,1)S(1)} %get-tuple-element.25), channel_id=1, source_target_pairs={{0,2},{2,4},{4,6},{6,0},{1,3},{3,5},{5,7},{7,1},{8,10},{10,12},{12... | collective-permute-start | bytes 442376 | tf_op jit(solution)/shard_map/ppermute | solution.py:160
  115.7 9.4 %collective-permute-start.2 = (bf16[576,128]{1,0:T(8,128)(2,1)S(1)}, bf16[576,128]{1,0:T(8,128)(2,1)S(1)}, u32[]{:S(2)}, u32[]{:S(2)}) collective-permute-start(bf16[576,128]{1,0:T(8,128)(2,1)S(1)} %get-tuple-element.26), channel_id=1, source_target_pairs={{0,4},{2,6},{4,0},{6,2},{1,5},{3,7},{5,1},{7,3},{8,12},{10,14},{12... | collective-permute-start | bytes 442376 | tf_op jit(solution)/shard_map/ppermute | solution.py:160
  120.8 7.4 %collective-permute-start.3 = (bf16[576,128]{1,0:T(8,128)(2,1)S(1)}, bf16[576,128]{1,0:T(8,128)(2,1)S(1)}, u32[]{:S(2)}, u32[]{:S(2)}) collective-permute-start(bf16[576,128]{1,0:T(8,128)(2,1)S(1)} %get-tuple-element.27), channel_id=1, source_target_pairs={{0,6},{2,0},{4,2},{6,4},{1,7},{3,1},{5,3},{7,5},{8,14},{10,8},{12,... | collective-permute-start | bytes 442376 | tf_op jit(solution)/shard_map/ppermute | solution.py:160

commit v5 on v4

v5 whole, which is shorter than its diff:
```python
import jax
import jax.numpy as jnp
import numpy as np
from jax import lax
from jax.experimental import pallas as pl
from jax.experimental.pallas import tpu as pltpu
from jax.sharding import Mesh, PartitionSpec as P

logit_scale = 20.0
f32 = jnp.float32
bf16 = jnp.bfloat16
NY, NZ, NX, NC = 4, 16, 4, 2
ROWS, WIDTH = 144, 96
COLS, SLICE = 1152, 12
TALL, SUB = NY * ROWS, COLS // NY
HALF = NX * 128
THIRD = NZ * NY * SLICE // NC
BLOCKS = [(0, 128), (128, 128), (256, 128), (384, 128), (512, 64)]
MSG = ROWS + 48
NT = (((1,), (1,)), ((), ()))


def call(kernel, outs, *args, far=(), far_outs=(), scratch=(), flops=0):
    bytes_accessed = sum(int(np.prod(a.shape)) * a.dtype.itemsize for a in (*args, *outs))
    vmem, smem, hbm = (pl.BlockSpec(memory_space=m) for m in (pltpu.VMEM, pltpu.SMEM, pltpu.HBM))
    return pl.pallas_call(
        kernel,
        out_shape=outs,
        in_specs=[hbm if i in far else smem if a.ndim == 1 else vmem for i, a in enumerate(args)],
        out_specs=[hbm if i in far_outs else vmem for i in range(len(outs))],
        scratch_shapes=list(scratch),
        compiler_params=pltpu.CompilerParams(vmem_limit_bytes=32 << 20),
        cost_estimate=pl.CostEstimate(flops=flops, bytes_accessed=bytes_accessed, transcendentals=0),
    )(*args)


def shape(dtype, *dims):
    return jax.ShapeDtypeStruct(dims, dtype)


def placement():
    table = np.zeros((NX, 128, NZ // NC, NY, SLICE), np.float32)
    for x in range(NX):
        for lane in range(WIDTH):
            table[x, lane, lane // SLICE, x, lane % SLICE] = 1.0
    return table.reshape(HALF, THIRD)


def columns(wide, width):
    lane = lax.broadcasted_iota(jnp.int32, (128, 128), 1)
    packed = jnp.ones((128, 128), f32)
    for j, group in enumerate(wide):
        for g, column in enumerate(group):
            if column.shape[0] < 128:
                column = jnp.concatenate([column, jnp.ones((128 - column.shape[0], 1), f32)], axis=0)
            packed = jnp.where(lane == 8 * g + j, column, packed)
    return packed.T[:width]


def upright(lines):
    return jnp.concatenate([lines, jnp.zeros((120, 128), f32)], axis=0).T


def prep_kernel(queries, positive, passages, message, wide, tall):
    index = positive[...].astype(f32)
    index = jnp.concatenate(
        [index[:, :128], jnp.concatenate([index[:, 128:], jnp.zeros((1, 256 - ROWS), f32)], axis=1)], axis=0
    )
    index = upright(jnp.concatenate([index, jnp.zeros((6, 128), f32)], axis=0))
    index = jnp.concatenate([index[:, 0:1], index[: ROWS - 128, 1:2]], axis=0)
    high = jnp.floor(index * (1.0 / 128.0))
    low = index - 128.0 * high
    wide[...] = jnp.zeros((ROWS, 128), f32)
    wide[:, :WIDTH] = queries[...].astype(f32)
    lane = lax.broadcasted_iota(jnp.int32, (ROWS, 128), 1)
    own = jnp.where(lane == WIDTH, high, jnp.where(lane == WIDTH + 1, low, wide[...])).astype(bf16)
    tall[...] = jnp.zeros((16, COLS), f32)
    tall[:SLICE] = passages[...].astype(f32)
    for y in range(NY):
        message[y, :ROWS] = own
        piece = pltpu.roll(tall[...], (COLS - y * SUB) % COLS, 1)
        for b in range(3):
            message[y, ROWS + 16 * b : ROWS + 16 * b + 16] = piece[:, b * 128 : (b + 1) * 128].astype(bf16)


def split_kernel(came, queries, part, total):
    for y in range(NY):
        for b in range(3):
            piece = came[y, ROWS + 16 * b : ROWS + 16 * b + 16].astype(f32)
            total[y * SLICE : (y + 1) * SLICE, b * 128 : (b + 1) * 128] = piece[:SLICE]
        for i in range(NX * NC):
            queries[i, y * ROWS : (y + 1) * ROWS] = came[y, :ROWS]
    part[...] = total[:, :SUB].astype(bf16)


def gather_parts(parts, query_full, sems):
    copies = [
        pltpu.make_async_copy(parts.at[b], query_full.at[:, pl.ds(b * 128, 128)], sems.at[b])
        for b in range(NC * NX)
    ]
    for copy in copies:
        copy.start()
    return copies


def tile_kernel(parts, passages, place, logits, row_pairs, col_pairs, passage_full, query_full, kept, sems, out_sems):
    copies = gather_parts(parts, query_full, sems)
    for c in range(NC):
        placed = jnp.dot(place[...], passages[c * THIRD : (c + 1) * THIRD], preferred_element_type=f32)
        passage_full[c * HALF : (c + 1) * HALF] = placed.astype(bf16)
    for copy in copies:
        copy.wait()
    pairs, col_top, out = [], None, []
    for j, (start, size) in enumerate(BLOCKS):
        rows = pl.ds(start, size)
        scores = logit_scale * jnp.dot(query_full[rows], passage_full[...], preferred_element_type=f32)
        kept[rows] = scores
        out.append(pltpu.make_async_copy(kept.at[rows], logits.at[rows], out_sems.at[j]))
        out[-1].start()
        top = jnp.max(scores, axis=1, keepdims=True)
        pairs.append((top, jnp.sum(jnp.exp(scores - top), axis=1, keepdims=True)))
        peak = jnp.max(scores, axis=0, keepdims=True)
        col_top = peak if col_top is None else jnp.maximum(col_top, peak)
    turned = columns(pairs, 16)
    for i in range(NX * NC):
        row_pairs[i] = turned
    col_sum = jnp.zeros((1, SUB), f32)
    for start, size in BLOCKS:
        col_sum += jnp.sum(jnp.exp(kept[start : start + size] - col_top), axis=0, keepdims=True)
    fill = jnp.ones((1, 384 - SUB), f32)
    both = [jnp.concatenate([v, fill], axis=1) for v in (col_top, col_sum)]
    lines = [v[:, b * 128 : (b + 1) * 128] for v in both for b in range(3)]
    lines = jnp.concatenate(lines + [jnp.ones((2, 128), f32)], axis=0)
    for i in range(NZ):
        col_pairs[i] = lines
    for copy in out:
        copy.wait()


def turn_kernel(parts, place, placed, targets, query_full, sems):
    for copy in gather_parts(parts, query_full, sems):
        copy.wait()
    for c in range(NC):
        half = query_full[:, c * HALF : (c + 1) * HALF]
        placed[c * THIRD : (c + 1) * THIRD] = lax.dot_general(
            place[...], half, NT, preferred_element_type=f32
        ).astype(bf16)
    spare = query_full[:, :128].astype(f32)
    target = spare[:, WIDTH : WIDTH + 1] * 128.0 + spare[:, WIDTH + 1 : WIDTH + 2]
    targets[...] = columns([(target[start : start + size],) for start, size in BLOCKS], 8)


def passage_kernel(
    logits, targets, ids, placed, row_pairs, col_pairs, dlogits, terms, kept, tails, sems
):
    copies = [
        pltpu.make_async_copy(logits.at[pl.ds(start, size)], kept.at[pl.ds(start, size)], sems.at[j])
        for j, (start, size) in enumerate(BLOCKS)
    ]
    for copy in copies:
        copy.start()
    top, total = row_pairs[:, :8], row_pairs[:, 8:]
    peak = jnp.max(top, axis=0)
    row_lse = upright(peak + jnp.log(jnp.sum(total * jnp.exp(top - peak[None]), axis=0)))
    target = upright(targets[...])
    pairs = col_pairs[...]
    top, total = pairs[:, 0:3], pairs[:, 3:6]
    peak = jnp.max(top, axis=0)
    col_lse = peak + jnp.log(jnp.sum(total * jnp.exp(top - peak[None]), axis=0))
    col_lse = jnp.concatenate([col_lse[b : b + 1] for b in range(3)], axis=1)[:, :SUB]
    dlogits[:, 256:] = jnp.zeros((TALL, 128), bf16)
    for j, (start, size) in enumerate(BLOCKS):
        copies[j].wait()
        scores = kept[start : start + size]
        slope = jnp.exp(scores - row_lse[:size, j : j + 1]) + jnp.exp(scores - col_lse)
        hit = jnp.where(target[:size, j : j + 1] == ids[...], 2.0, 0.0)
        dlogits[start : start + size, :SUB] = (slope - hit).astype(bf16)
    high = NY * SLICE
    for first in range(0, NZ, 4):
        part = logit_scale * jnp.dot(
            placed[first * high : (first + 4) * high], dlogits[...], preferred_element_type=f32
        )
        for a in range(NY):
            tails[a] = part[:, 256:] if a == 0 else pltpu.roll(part[:, 256:], 32 * a, 1)
        for i in range(4):
            for b in range(2):
                piece = part[i * high : (i + 1) * high, b * 128 : (b + 1) * 128]
                terms[first + i, b * high : (b + 1) * high] = piece.astype(bf16)
            tail = sum(tails[a, i * high + a * SLICE : i * high + (a + 1) * SLICE] for a in range(NY))
            tail = jnp.concatenate([tail, jnp.zeros((16 - SLICE, 128), f32)], axis=0)
            terms[first + i, 2 * high : 2 * high + 16] = tail.astype(bf16)


def theirs_kernel(place, dlogits, passage_full, theirs):
    core = place[0]
    half = passage_full[pl.ds(pl.multiple_of((1 - core) * HALF, HALF), HALF)]
    theirs[...] = logit_scale * lax.dot_general(dlogits[:, :SUB], half, NT, preferred_element_type=f32)


def ours_kernel(place, dlogits, passage_full, theirs, own, *rest):
    outs, total = rest[:-1], rest[-1]
    core, x = place[0], place[1]
    half = passage_full[pl.ds(pl.multiple_of(core * HALF, HALF), HALF)]
    total[...] = theirs[...] + logit_scale * lax.dot_general(
        dlogits[:, :SUB], half, NT, preferred_element_type=f32
    )
    own[...] = total[:, pl.ds(pl.multiple_of(x * 128, 128), 128)]
    for step, out in enumerate(outs, 1):
        lanes = pl.ds(pl.multiple_of(lax.rem(x + step, NX) * 128, 128), 128)
        out[...] = total[:, lanes].astype(bf16)


def fold_kernel(terms, own, *rest):
    came, message, total = rest[:-2], rest[-2], rest[-1]
    high = NY * SLICE
    total[...] = jnp.sum(terms[...].astype(f32), axis=0)
    for y in range(NY):
        rows = slice(y * ROWS, (y + 1) * ROWS)
        message[y, :ROWS] = own[rows] + sum(c[rows].astype(f32) for c in came)
        tail = total[2 * high :]
        tail = tail if y == 0 else pltpu.roll(tail, 128 - 32 * y, 1)
        for b in range(3):
            piece = tail[:SLICE] if b == 2 else total[b * high + y * SLICE : b * high + (y + 1) * SLICE]
            message[y, ROWS + b * 16 : ROWS + b * 16 + SLICE] = piece
            message[y, ROWS + b * 16 + SLICE : ROWS + b * 16 + 16] = jnp.zeros((16 - SLICE, 128), f32)


def final_kernel(came, query_grad, passage_grad):
    query_grad[...] = jnp.sum(came[:, :ROWS], axis=0)[:, :WIDTH]
    lane = lax.broadcasted_iota(jnp.int32, (16, 128), 1)
    total = None
    for y in range(NY):
        blocks = [came[y, ROWS + b * 16 : ROWS + b * 16 + 16] for b in range(3)]
        blocks[2] = jnp.where(lane < SUB - 256, blocks[2], 0.0)
        wide = jnp.concatenate(blocks + [jnp.zeros((16, COLS - 384), f32)], axis=1)
        wide = wide if y == 0 else pltpu.roll(wide, y * SUB, 1)
        total = wide if total is None else total + wide
    passage_grad[...] = total[:SLICE]


def merge(pairs):
    top, total = pairs[:, :8], pairs[:, 8:]
    peak = jnp.max(top, axis=0)
    return jnp.concatenate([peak, jnp.sum(total * jnp.exp(top - peak[None]), axis=0)])


def around(x, axis, n, step):
    return lax.ppermute(x, axis, [(i, (i + step) % n) for i in range(n)])


def body(queries, passages, positive):
    table = placement()
    place, place_t = jnp.asarray(table, bf16), jnp.asarray(table.T, bf16)
    where = jnp.stack([lax.axis_index("core"), lax.axis_index("x")]).astype(jnp.int32)

    (message,) = call(
        prep_kernel,
        [shape(bf16, NY, MSG, 128)],
        queries,
        positive[None],
        passages.T,
        scratch=[pltpu.VMEM((ROWS, 128), f32), pltpu.VMEM((16, COLS), f32)],
    )
    message = lax.all_to_all(message, "y", 0, 0, tiled=True)
    parts, passage_part = call(
        split_kernel,
        [shape(bf16, NX * NC, TALL, 128), shape(bf16, NY * SLICE, SUB)],
        message,
        scratch=[pltpu.VMEM((NY * SLICE, 384), f32)],
    )
    parts = lax.all_to_all(parts, ("core", "x"), 0, 0, tiled=True)
    passage_part = lax.all_gather(passage_part, "z", axis=0, tiled=True)

    assembly = [pltpu.VMEM((TALL, NC * HALF), bf16), pltpu.SemaphoreType.DMA((NC * NX,))]
    kept = pltpu.VMEM((TALL, SUB), f32)
    logits, row_pairs, col_pairs, passage_full = call(
        tile_kernel,
        [
            shape(f32, TALL, SUB),
            shape(f32, NX * NC, 16, 128),
            shape(f32, NZ, 8, 128),
            shape(bf16, NC * HALF, SUB),
        ],
        parts,
        passage_part,
        place,
        far=(0,),
        far_outs=(0,),
        scratch=[assembly[0], kept, assembly[1], pltpu.SemaphoreType.DMA((len(BLOCKS),))],
        flops=2 * TALL * SUB * NC * HALF,
    )
    placed, targets = call(
        turn_kernel,
        [shape(bf16, NC * THIRD, TALL), shape(f32, 8, 128)],
        parts,
        place_t,
        far=(0,),
        scratch=assembly,
        flops=2 * TALL * HALF * THIRD * NC,
    )
    row_pairs = lax.all_to_all(row_pairs, ("x", "core"), 0, 0, tiled=True)
    col_pairs = lax.all_to_all(col_pairs, "z", 0, 0, tiled=True)
    row_pairs = lax.all_gather(merge(row_pairs), "y")

    block = (lax.axis_index("x") * NC + lax.axis_index("core")) * NY + lax.axis_index("y")
    ids = (block * SUB + jnp.arange(SUB, dtype=jnp.int32)).astype(f32)[None]
    dlogits, terms = call(
        passage_kernel,
        [shape(bf16, TALL, 384), shape(bf16, NZ, 112, 128)],
        logits,
        targets,
        ids,
        placed,
        row_pairs,
        col_pairs,
        far=(0,),
        scratch=[kept, pltpu.VMEM((NY, 4 * NY * SLICE, 128), f32), pltpu.SemaphoreType.DMA((len(BLOCKS),))],
        flops=2 * TALL * SUB * NC * THIRD,
    )
    terms = lax.all_to_all(terms, "z", 0, 0, tiled=True)

    (theirs,) = call(
        theirs_kernel, [shape(f32, TALL, HALF)], where, dlogits, passage_full, flops=2 * TALL * SUB * HALF
    )
    theirs = around(theirs, "core", NC, 1)
    own, *others = call(
        ours_kernel,
        [shape(f32, TALL, 128)] + [shape(bf16, TALL, 128)] * (NX - 1),
        where,
        dlogits,
        passage_full,
        theirs,
        scratch=[pltpu.VMEM((TALL, HALF), f32)],
        flops=2 * TALL * SUB * HALF,
    )
    came = [around(other, "x", NX, step) for step, other in enumerate(others, 1)]

    (message,) = call(fold_kernel, [shape(f32, NY, MSG, 128)], terms, own, *came, scratch=[pltpu.VMEM((112, 128), f32)])
    message = lax.all_to_all(message, "y", 0, 0, tiled=True)
    query_grad, passage_grad = call(final_kernel, [shape(f32, ROWS, WIDTH), shape(f32, SLICE, COLS)], message)
    return (query_grad, passage_grad.T)


def solution(mesh):
    chips = Mesh(mesh.devices.reshape(NY, NZ, NX, NC), ("y", "z", "x", "core"))
    yz, xc = ("y", "z"), ("x", "core")
    return jax.shard_map(
        body,
        mesh=chips,
        in_specs=(P(yz, xc), P(xc, yz), P(yz)),
        out_specs=(P(yz, xc), P(xc, yz)),
        check_vma=False,
    )
```

time: 148 us -> 144 us (0.973)
  the two profiles are of different devices: /device:TPU:2 before, /device:TPU:64 now
where the time goes in v5:
time: 144 us; the launch traced here: 143 us
  blocking collectives  68.1 us (47%)
  starting transfers between devices  41.9 us (29%)
  Pallas kernels  14.1 us (10%)
  waiting for transfers between devices  13.6 us (9%)
  local copies, waits for them, and re-layouts  4.28 us (3%)
    all_gather x1, blocking collectives, body(): passage_part = lax.all_gather(passage_part, 'z', axis=0, tiled=True)  35.7 us
    all_to_all x2, blocking collectives, body(): message = lax.all_to_all(message, 'y', 0, 0, tiled=True)  20.5 us
    pallas_call x9, Pallas kernels, call(): pl.pallas_call(kernel, out_shape=outs, in_specs=[hbm if i in far else sme...  14.1 us
    all_to_all x1, starting transfers between devices, body(): terms = lax.all_to_all(terms, 'z', 0, 0, tiled=True)  12 us
    all_gather x1, blocking collectives, body(): row_pairs = lax.all_gather(merge(row_pairs), 'y')  11.9 us
    ppermute x4, starting transfers between devices, around(): return lax.ppermute(x, axis, [(i, (i + step) % n) for i in range(n)])  11.3 us
    all_to_all x1, starting transfers between devices, body(): col_pairs = lax.all_to_all(col_pairs, 'z', 0, 0, tiled=True)  9.5 us
    ppermute x4, waiting for transfers between devices, around(): return lax.ppermute(x, axis, [(i, (i + step) % n) for i in range(n)])  8.09 us
  transfers between devices with their start and end apart: 8, of which 5 were waited for; matrix products, arithmetic and copies ran while one was open for 0% of the time, Pallas kernels for 2%

profile of v5, /device:TPU:64, one launch (start us, length us, event | category | flops | bytes accessed | tf_op | source)
XLA Modules:
  0.0 142.8 jit_solution(4001377985020378608)
XLA Ops:
  0.6 0.8 copy-done.3
  1.4 0.8 copy-done.4
  2.2 0.7 copy-done.5
  2.8 0.2 shard_map.68
  3.1 10.6 %all_to_all.30.came = bf16[4,192,128]{2,1,0:T(8,128)(2,1)S(1)} all-to-all(bf16[4,192,128]{2,1,0:T(8,128)(2,1)S(1)} %shard_map.68), channel_id=1, replica_groups=mesh['y'=4,'z'=16,'x'=4,'core'=2] {'y'}, dimensions={0} | all-to-all | bytes 393216 | tf_op jit(solution)/shard_map/all_to_all | solution.py:264
  13.7 1.2 shard_map.69
  14.9 4.4 %all-to-all-start.1 = ((bf16[8,576,128]{2,1,0:T(8,128)(2,1)}), bf16[8,576,128]{2,1,0:T(8,128)(2,1)S(1)}, u32[]{:S(2)}, u32[]{:S(2)}) async-start(bf16[8,576,128]{2,1,0:T(8,128)(2,1)} %get-tuple-element.18), calls=%async_computation.1 | async-start | bytes 2359296 | tf_op jit(solution)/shard_map/all_to_all | solution.py:271
  19.3 35.7 %all_gather.9.passages = bf16[768,288]{1,0:T(8,128)(2,1)S(1)} all-gather(bf16[48,288]{1,0:T(8,128)(2,1)S(1)} %get-tuple-element.19), channel_id=1, replica_groups=mesh['y'=4,'z'=16,'x'=4,'core'=2] {'z'}, dimensions={0}, use_global_device_ids=true | all-gather | bytes 470016 | tf_op jit(solution)/shard_map/all_gather | solution.py:272
  55.1 4.8 %shard_map.70 = (f32[576,288]{1,0:T(8,128)S(1)}, f32[8,16,128]{2,1,0:T(8,128)}, f32[16,8,128]{2,1,0:T(8,128)}, bf16[1024,288]{1,0:T(8,128)(2,1)S(1)}) custom-call(bf16[8,576,128]{2,1,0:T(8,128)(2,1)S(1)} %all-to-all-done.1.parts, bf16[768,288]{1,0:T(8,128)(2,1)S(1)} %all_gather.9.passages, bf16[512,384]{1,0:T(8,128)(2,1)S(1)} %copy-done.2), custom_call_target="tpu_custom_call" | custom-call | flops 339738624 | bytes 3399680 | tf_op jit(solution)/shard_map/pallas_call | solution.py:26
  59.9 0.9 copy-done
  60.8 4.6 %all-to-all-start.2 = ((f32[8,16,128]{2,1,0:T(8,128)}), f32[8,16,128]{2,1,0:T(8,128)S(1)}, u32[]{:S(2)}, u32[]{:S(2)}) async-start(f32[8,16,128]{2,1,0:T(8,128)} %get-tuple-element.23), calls=%async_computation.2 | async-start | bytes 131072 | tf_op jit(solution)/shard_map/all_to_all | solution.py:301
  65.4 1.2 shard_map.71
  66.7 4.4 %all-to-all-done.2 = f32[8,16,128]{2,1,0:T(8,128)S(1)} async-done(((f32[8,16,128]{2,1,0:T(8,128)}), f32[8,16,128]{2,1,0:T(8,128)S(1)}, u32[]{:S(2)}, u32[]{:S(2)}) %all-to-all-start.2) | async-done | bytes 65568 | tf_op jit(solution)/shard_map/all_to_all | solution.py:301
  71.0 9.5 %all-to-all-start.3 = ((f32[16,8,128]{2,1,0:T(8,128)}), f32[16,8,128]{2,1,0:T(8,128)S(1)}, u32[]{:S(2)}, u32[]{:S(2)}) async-start(f32[16,8,128]{2,1,0:T(8,128)} %get-tuple-element.24), calls=%async_computation.3 | async-start | bytes 131072 | tf_op jit(solution)/shard_map/all_to_all | solution.py:302
  80.6 11.9 %all-gather = f32[64,128]{1,0:T(8,128)S(1)} all-gather(f32[16,128]{1,0:T(8,128)S(1)} %pad_maximum_fusion), channel_id=2, replica_groups=mesh['y'=4,'z'=16,'x'=4,'core'=2] {'y'}, dimensions={0}, use_global_device_ids=true | all-gather | bytes 40960 | tf_op jit(solution)/shard_map/all_gather | solution.py:303
  92.5 1.2 copy-done.1
  93.7 3.4 %shard_map.72 = (bf16[576,384]{1,0:T(8,128)(2,1)S(1)}, bf16[16,112,128]{2,1,0:T(8,128)(2,1)}) custom-call(f32[576,288]{1,0:T(8,128)S(1)} %copy-done.1, f32[8,128]{1,0:T(8,128)S(1)} %get-tuple-element.21.targets, f32[1,288]{1,0:T(1,128)S(1)} %add_convert_fusion.ids, bf16[768,576]{1,0:T(8,128)(2,1)S(1)} %get-tuple-element.22.placed, ...), custom_call_target="tpu_custom_call" | custom-call | flops 254803968 | bytes 2552960 | tf_op jit(solution)/shard_map/pallas_call | solution.py:26
  97.1 12.0 %all-to-all-start.4 = ((bf16[16,112,128]{2,1,0:T(8,128)(2,1)}), bf16[16,112,128]{2,1,0:T(8,128)(2,1)S(1)}, u32[]{:S(2)}, u32[]{:S(2)}) async-start(bf16[16,112,128]{2,1,0:T(8,128)(2,1)} %get-tuple-element.25), calls=%async_computation.4 | async-start | bytes 917504 | tf_op jit(solution)/shard_map/all_to_all | solution.py:320
  109.2 0.1 pad_add_fusion.place
  109.3 1.0 shard_map.73
  110.3 1.9 %collective-permute-start = (f32[576,512]{1,0:T(8,128)S(1)}, f32[576,512]{1,0:T(8,128)S(1)}, u32[]{:S(2)}, u32[]{:S(2)}) collective-permute-start(f32[576,512]{1,0:T(8,128)S(1)} %shard_map.73), channel_id=1, source_target_pairs={{0,1},{1,0},{2,3},{3,2},{4,5},{5,4},{6,7},{7,6},{8,9},{9,8},{10,11... | collective-permute-start | bytes 3538952 | tf_op jit(solution)/shard_map/ppermute | solution.py:248
  112.2 2.8 %collective-permute-done.theirs = f32[576,512]{1,0:T(8,128)S(1)} collective-permute-done((f32[576,512]{1,0:T(8,128)S(1)}, f32[576,512]{1,0:T(8,128)S(1)}, u32[]{:S(2)}, u32[]{:S(2)}) %collective-permute-start) | collective-permute-done | bytes 1179680 | tf_op jit(solution)/shard_map/ppermute | solution.py:248
  115.0 1.2 shard_map.74
  116.3 2.5 %collective-permute-start.1 = (bf16[576,128]{1,0:T(8,128)(2,1)S(1)}, bf16[576,128]{1,0:T(8,128)(2,1)S(1)}, u32[]{:S(2)}, u32[]{:S(2)}) collective-permute-start(bf16[576,128]{1,0:T(8,128)(2,1)S(1)} %get-tuple-element.29), channel_id=1, source_target_pairs={{0,2},{2,4},{4,6},{6,0},{1,3},{3,5},{5,7},{7,1},{8,10},{10,12},{12... | collective-permute-start | bytes 442376 | tf_op jit(solution)/shard_map/ppermute | solution.py:248
  118.7 4.0 %collective-permute-start.2 = (bf16[576,128]{1,0:T(8,128)(2,1)S(1)}, bf16[576,128]{1,0:T(8,128)(2,1)S(1)}, u32[]{:S(2)}, u32[]{:S(2)}) collective-permute-start(bf16[576,128]{1,0:T(8,128)(2,1)S(1)} %get-tuple-element.30), channel_id=1, source_target_pairs={{0,4},{2,6},{4,0},{6,2},{1,5},{3,7},{5,1},{7,3},{8,12},{10,14},{12... | collective-permute-start | bytes 442376 | tf_op jit(solution)/shard_map/ppermute | solution.py:248
  122.7 2.9 %collective-permute-start.3 = (bf16[576,128]{1,0:T(8,128)(2,1)S(1)}, bf16[576,128]{1,0:T(8,128)(2,1)S(1)}, u32[]{:S(2)}, u32[]{:S(2)}) collective-permute-start(bf16[576,128]{1,0:T(8,128)(2,1)S(1)} %get-tuple-element.31), channel_id=1, source_target_pairs={{0,6},{2,0},{4,2},{6,4},{1,7},{3,1},{5,3},{7,5},{8,14},{10,8},{12,... | collective-permute-start | bytes 442376 | tf_op jit(solution)/shard_map/ppermute | solution.py:248
  125.6 2.8 %collective-permute-done.1.rest_0_ = bf16[576,128]{1,0:T(8,128)(2,1)S(1)} collective-permute-done((bf16[576,128]{1,0:T(8,128)(2,1)S(1)}, bf16[576,128]{1,0:T(8,128)(2,1)S(1)}, u32[]{:S(2)}, u32[]{:S(2)}) %collective-permute-start.1) | collective-permute-done | bytes 147488 | tf_op jit(solution)/shard_map/ppermute | solution.py:248
  128.4 2.5 %collective-permute-done.3.rest_2_ = bf16[576,128]{1,0:T(8,128)(2,1)S(1)} collective-permute-done((bf16[576,128]{1,0:T(8,128)(2,1)S(1)}, bf16[576,128]{1,0:T(8,128)(2,1)S(1)}, u32[]{:S(2)}, u32[]{:S(2)}) %collective-permute-start.3) | collective-permute-done | bytes 147488 | tf_op jit(solution)/shard_map/ppermute | solution.py:248
  130.9 1.1 all-to-all-done.4.terms
  132.0 0.1 shard_map.75
  132.2 9.9 %all_to_all.31.came = f32[4,192,128]{2,1,0:T(8,128)S(1)} all-to-all(f32[4,192,128]{2,1,0:T(8,128)S(1)} %shard_map.75), channel_id=1, replica_groups=mesh['y'=4,'z'=16,'x'=4,'core'=2] {'y'}, dimensions={0} | all-to-all | bytes 786432 | tf_op jit(solution)/shard_map/all_to_all | solution.py:339
  142.1 0.7 shard_map.76
  (16 shorter events, 0.1 us)
Async XLA Ops:
  0.6 0.8 copy-start.3
  1.4 0.8 copy-start.4
  2.2 0.7 copy-start.5
  14.9 40.2 %copy-start.2 = (bf16[512,384]{1,0:T(8,128)(2,1)S(1)}, bf16[512,384]{1,0:T(8,128)(2,1)}, u32[]{:S(2)}) copy-start(bf16[512,384]{1,0:T(8,128)(2,1)} %constant.26.clone.place) | copy-start | bytes 1179652
  14.9 40.2 %all-to-all-start.1 = ((bf16[8,576,128]{2,1,0:T(8,128)(2,1)}), bf16[8,576,128]{2,1,0:T(8,128)(2,1)S(1)}, u32[]{:S(2)}, u32[]{:S(2)}) async-start(bf16[8,576,128]{2,1,0:T(8,128)(2,1)} %get-tuple-element.18), calls=%async_computation.1 | async-start | bytes 2359296 | tf_op jit(solution)/shard_map/all_to_all | solution.py:271
  55.0 10.4 %copy-start.6 = (bf16[384,512]{1,0:T(8,128)(2,1)S(1)}, bf16[384,512]{1,0:T(8,128)(2,1)}, u32[]{:S(2)}) copy-start(bf16[384,512]{1,0:T(8,128)(2,1)} %constant.27.clone.place) | copy-start | bytes 1179652
  59.9 0.9 copy-start
  60.8 10.3 %all-to-all-start.2 = ((f32[8,16,128]{2,1,0:T(8,128)}), f32[8,16,128]{2,1,0:T(8,128)S(1)}, u32[]{:S(2)}, u32[]{:S(2)}) async-start(f32[8,16,128]{2,1,0:T(8,128)} %get-tuple-element.23), calls=%async_computation.2 | async-start | bytes 131072 | tf_op jit(solution)/shard_map/all_to_all | solution.py:301
  71.0 21.5 %all-to-all-start.3 = ((f32[16,8,128]{2,1,0:T(8,128)}), f32[16,8,128]{2,1,0:T(8,128)S(1)}, u32[]{:S(2)}, u32[]{:S(2)}) async-start(f32[16,8,128]{2,1,0:T(8,128)} %get-tuple-element.24), calls=%async_computation.3 | async-start | bytes 131072 | tf_op jit(solution)/shard_map/all_to_all | solution.py:302
  92.5 1.2 copy-start.1
  97.1 34.9 %all-to-all-start.4 = ((bf16[16,112,128]{2,1,0:T(8,128)(2,1)}), bf16[16,112,128]{2,1,0:T(8,128)(2,1)S(1)}, u32[]{:S(2)}, u32[]{:S(2)}) async-start(bf16[16,112,128]{2,1,0:T(8,128)(2,1)} %get-tuple-element.25), calls=%async_computation.4 | async-start | bytes 917504 | tf_op jit(solution)/shard_map/all_to_all | solution.py:320
  110.3 4.7 %collective-permute-start = (f32[576,512]{1,0:T(8,128)S(1)}, f32[576,512]{1,0:T(8,128)S(1)}, u32[]{:S(2)}, u32[]{:S(2)}) collective-permute-start(f32[576,512]{1,0:T(8,128)S(1)} %shard_map.73), channel_id=1, source_target_pairs={{0,1},{1,0},{2,3},{3,2},{4,5},{5,4},{6,7},{7,6},{8,9},{9,8},{10,11... | collective-permute-start | bytes 3538952 | tf_op jit(solution)/shard_map/ppermute | solution.py:248
  116.3 12.2 %collective-permute-start.1 = (bf16[576,128]{1,0:T(8,128)(2,1)S(1)}, bf16[576,128]{1,0:T(8,128)(2,1)S(1)}, u32[]{:S(2)}, u32[]{:S(2)}) collective-permute-start(bf16[576,128]{1,0:T(8,128)(2,1)S(1)} %get-tuple-element.29), channel_id=1, source_target_pairs={{0,2},{2,4},{4,6},{6,0},{1,3},{3,5},{5,7},{7,1},{8,10},{10,12},{12... | collective-permute-start | bytes 442376 | tf_op jit(solution)/shard_map/ppermute | solution.py:248
  118.7 9.7 %collective-permute-start.2 = (bf16[576,128]{1,0:T(8,128)(2,1)S(1)}, bf16[576,128]{1,0:T(8,128)(2,1)S(1)}, u32[]{:S(2)}, u32[]{:S(2)}) collective-permute-start(bf16[576,128]{1,0:T(8,128)(2,1)S(1)} %get-tuple-element.30), channel_id=1, source_target_pairs={{0,4},{2,6},{4,0},{6,2},{1,5},{3,7},{5,1},{7,3},{8,12},{10,14},{12... | collective-permute-start | bytes 442376 | tf_op jit(solution)/shard_map/ppermute | solution.py:248
  122.7 8.2 %collective-permute-start.3 = (bf16[576,128]{1,0:T(8,128)(2,1)S(1)}, bf16[576,128]{1,0:T(8,128)(2,1)S(1)}, u32[]{:S(2)}, u32[]{:S(2)}) collective-permute-start(bf16[576,128]{1,0:T(8,128)(2,1)S(1)} %get-tuple-element.31), channel_id=1, source_target_pairs={{0,6},{2,0},{4,2},{6,4},{1,7},{3,1},{5,3},{7,5},{8,14},{10,8},{12,... | collective-permute-start | bytes 442376 | tf_op jit(solution)/shard_map/ppermute | solution.py:248

commit v6 on v5

--- a/solution.py
+++ b/solution.py
@@ -17,21 +17,23 @@
 THIRD = NZ * NY * SLICE // NC
 BLOCKS = [(0, 128), (128, 128), (256, 128), (384, 128), (512, 64)]
 MSG = ROWS + 48
+GROUP = 384
 NT = (((1,), (1,)), ((), ()))
-
-
-def call(kernel, outs, *args, far=(), far_outs=(), scratch=(), flops=0):
+TN = (((0,), (0,)), ((), ()))
+
+
+def call(kernel, outs, *args, far=(), scratch=(), flops=0):
     bytes_accessed = sum(int(np.prod(a.shape)) * a.dtype.itemsize for a in (*args, *outs))
     vmem, smem, hbm = (pl.BlockSpec(memory_space=m) for m in (pltpu.VMEM, pltpu.SMEM, pltpu.HBM))
     return pl.pallas_call(
         kernel,
         out_shape=outs,
         in_specs=[hbm if i in far else smem if a.ndim == 1 else vmem for i, a in enumerate(args)],
-        out_specs=[hbm if i in far_outs else vmem for i in range(len(outs))],
+        out_specs=[vmem] * len(outs),
         scratch_shapes=list(scratch),
         compiler_params=pltpu.CompilerParams(vmem_limit_bytes=32 << 20),
         cost_estimate=pl.CostEstimate(flops=flops, bytes_accessed=bytes_accessed, transcendentals=0),
-    )(*args)
+    )(*(pltpu.with_memory_space_constraint(a, pltpu.HBM) if i in far else a for i, a in enumerate(args)))
 
 
 def shape(dtype, *dims):
@@ -61,7 +63,13 @@
     return jnp.concatenate([lines, jnp.zeros((120, 128), f32)], axis=0).T
 
 
-def prep_kernel(queries, positive, passages, message, wide, tall):
+def prep_kernel(queries_in, positive_in, passages_in, message, queries, positive, passages, wide, tall, sems):
+    pairs = ((queries_in, queries), (positive_in, positive), (passages_in, passages))
+    copies = [pltpu.make_async_copy(a, b, sems.at[i]) for i, (a, b) in enumerate(pairs)]
+    for copy in copies:
+        copy.start()
+    for copy in copies:
+        copy.wait()
     index = positive[...].astype(f32)
     index = jnp.concatenate(
         [index[:, :128], jnp.concatenate([index[:, 128:], jnp.zeros((1, 256 - ROWS), f32)], axis=1)], axis=0
@@ -93,30 +101,19 @@
     part[...] = total[:, :SUB].astype(bf16)
 
 
-def gather_parts(parts, query_full, sems):
-    copies = [
-        pltpu.make_async_copy(parts.at[b], query_full.at[:, pl.ds(b * 128, 128)], sems.at[b])
-        for b in range(NC * NX)
-    ]
-    for copy in copies:
-        copy.start()
-    return copies
-
-
-def tile_kernel(parts, passages, place, logits, row_pairs, col_pairs, passage_full, query_full, kept, sems, out_sems):
-    copies = gather_parts(parts, query_full, sems)
+def tile_kernel(parts, passages, place, row_pairs, col_pairs, placed, targets, query_half, logits):
     for c in range(NC):
-        placed = jnp.dot(place[...], passages[c * THIRD : (c + 1) * THIRD], preferred_element_type=f32)
-        passage_full[c * HALF : (c + 1) * HALF] = placed.astype(bf16)
-    for copy in copies:
-        copy.wait()
-    pairs, col_top, out = [], None, []
-    for j, (start, size) in enumerate(BLOCKS):
-        rows = pl.ds(start, size)
-        scores = logit_scale * jnp.dot(query_full[rows], passage_full[...], preferred_element_type=f32)
-        kept[rows] = scores
-        out.append(pltpu.make_async_copy(kept.at[rows], logits.at[rows], out_sems.at[j]))
-        out[-1].start()
+        for x in range(NX):
+            query_half[:, x * 128 : (x + 1) * 128] = parts[c * NX + x]
+        placed[:, c * THIRD : (c + 1) * THIRD] = jnp.dot(
+            query_half[...], place[...], preferred_element_type=f32
+        ).astype(bf16)
+    pairs, col_top = [], None
+    for start, size in BLOCKS:
+        scores = logit_scale * jnp.dot(
+            placed[start : start + size], passages[...], preferred_element_type=f32
+        )
+        logits[start : start + size] = scores
         top = jnp.max(scores, axis=1, keepdims=True)
         pairs.append((top, jnp.sum(jnp.exp(scores - top), axis=1, keepdims=True)))
         peak = jnp.max(scores, axis=0, keepdims=True)
@@ -126,39 +123,25 @@
         row_pairs[i] = turned
     col_sum = jnp.zeros((1, SUB), f32)
     for start, size in BLOCKS:
-        col_sum += jnp.sum(jnp.exp(kept[start : start + size] - col_top), axis=0, keepdims=True)
+        col_sum += jnp.sum(jnp.exp(logits[start : start + size] - col_top), axis=0, keepdims=True)
     fill = jnp.ones((1, 384 - SUB), f32)
     both = [jnp.concatenate([v, fill], axis=1) for v in (col_top, col_sum)]
     lines = [v[:, b * 128 : (b + 1) * 128] for v in both for b in range(3)]
     lines = jnp.concatenate(lines + [jnp.ones((2, 128), f32)], axis=0)
     for i in range(NZ):
         col_pairs[i] = lines
-    for copy in out:
-        copy.wait()
-
-
-def turn_kernel(parts, place, placed, targets, query_full, sems):
-    for copy in gather_parts(parts, query_full, sems):
-        copy.wait()
-    for c in range(NC):
-        half = query_full[:, c * HALF : (c + 1) * HALF]
-        placed[c * THIRD : (c + 1) * THIRD] = lax.dot_general(
-            place[...], half, NT, preferred_element_type=f32
-        ).astype(bf16)
-    spare = query_full[:, :128].astype(f32)
+    spare = parts[0].astype(f32)
     target = spare[:, WIDTH : WIDTH + 1] * 128.0 + spare[:, WIDTH + 1 : WIDTH + 2]
     targets[...] = columns([(target[start : start + size],) for start, size in BLOCKS], 8)
 
 
-def passage_kernel(
-    logits, targets, ids, placed, row_pairs, col_pairs, dlogits, terms, kept, tails, sems
-):
-    copies = [
-        pltpu.make_async_copy(logits.at[pl.ds(start, size)], kept.at[pl.ds(start, size)], sems.at[j])
-        for j, (start, size) in enumerate(BLOCKS)
-    ]
-    for copy in copies:
-        copy.start()
+def spread_kernel(passages, place, passage_full):
+    for c in range(NC):
+        turned = jnp.dot(place[...], passages[c * THIRD : (c + 1) * THIRD], preferred_element_type=f32)
+        passage_full[c * HALF : (c + 1) * HALF] = turned.astype(bf16)
+
+
+def passage_kernel(placed, passages, targets, ids, row_pairs, col_pairs, dlogits, terms, tails):
     top, total = row_pairs[:, :8], row_pairs[:, 8:]
     peak = jnp.max(top, axis=0)
     row_lse = upright(peak + jnp.log(jnp.sum(total * jnp.exp(top - peak[None]), axis=0)))
@@ -170,16 +153,18 @@
     col_lse = jnp.concatenate([col_lse[b : b + 1] for b in range(3)], axis=1)[:, :SUB]
     dlogits[:, 256:] = jnp.zeros((TALL, 128), bf16)
     for j, (start, size) in enumerate(BLOCKS):
-        copies[j].wait()
-        scores = kept[start : start + size]
+        scores = logit_scale * jnp.dot(placed[start : start + size], passages[...], preferred_element_type=f32)
         slope = jnp.exp(scores - row_lse[:size, j : j + 1]) + jnp.exp(scores - col_lse)
         hit = jnp.where(target[:size, j : j + 1] == ids[...], 2.0, 0.0)
         dlogits[start : start + size, :SUB] = (slope - hit).astype(bf16)
     high = NY * SLICE
     for first in range(0, NZ, 4):
-        part = logit_scale * jnp.dot(
-            placed[first * high : (first + 4) * high], dlogits[...], preferred_element_type=f32
-        )
+        if first * high % GROUP == 0:
+            whole = logit_scale * lax.dot_general(
+                placed[:, first * high : first * high + GROUP], dlogits[...], TN, preferred_element_type=f32
+            )
+        offset = first * high % GROUP
+        part = whole[offset : offset + 4 * high]
         for a in range(NY):
             tails[a] = part[:, 256:] if a == 0 else pltpu.roll(part[:, 256:], 32 * a, 1)
         for i in range(4):
@@ -249,8 +234,7 @@
 
 
 def body(queries, passages, positive):
-    table = placement()
-    place, place_t = jnp.asarray(table, bf16), jnp.asarray(table.T, bf16)
+    place = jnp.asarray(placement(), bf16)
     where = jnp.stack([lax.axis_index("core"), lax.axis_index("x")]).astype(jnp.int32)
 
     (message,) = call(
@@ -259,7 +243,15 @@
         queries,
         positive[None],
         passages.T,
-        scratch=[pltpu.VMEM((ROWS, 128), f32), pltpu.VMEM((16, COLS), f32)],
+        far=(0, 1, 2),
+        scratch=[
+            pltpu.VMEM((ROWS, WIDTH), bf16),
+            pltpu.VMEM((1, ROWS), jnp.int32),
+            pltpu.VMEM((SLICE, COLS), bf16),
+            pltpu.VMEM((ROWS, 128), f32),
+            pltpu.VMEM((16, COLS), f32),
+            pltpu.SemaphoreType.DMA((3,)),
+        ],
     )
     message = lax.all_to_all(message, "y", 0, 0, tiled=True)
     parts, passage_part = call(
@@ -271,33 +263,29 @@
     parts = lax.all_to_all(parts, ("core", "x"), 0, 0, tiled=True)
     passage_part = lax.all_gather(passage_part, "z", axis=0, tiled=True)
 
-    assembly = [pltpu.VMEM((TALL, NC * HALF), bf16), pltpu.SemaphoreType.DMA((NC * NX,))]
-    kept = pltpu.VMEM((TALL, SUB), f32)
-    logits, row_pairs, col_pairs, passage_full = call(
+    row_pairs, col_pairs, placed, targets = call(
         tile_kernel,
         [
-            shape(f32, TALL, SUB),
             shape(f32, NX * NC, 16, 128),
             shape(f32, NZ, 8, 128),
-            shape(bf16, NC * HALF, SUB),
+            shape(bf16, TALL, NC * THIRD),
+            shape(f32, 8, 128),
         ],
         parts,
         passage_part,
         place,
-        far=(0,),
-        far_outs=(0,),
-        scratch=[assembly[0], kept, assembly[1], pltpu.SemaphoreType.DMA((len(BLOCKS),))],
+        scratch=[pltpu.VMEM((TALL, HALF), bf16), pltpu.VMEM((TALL, SUB), f32)],
         flops=2 * TALL * SUB * NC * HALF,
     )
-    placed, targets = call(
-        turn_kernel,
-        [shape(bf16, NC * THIRD, TALL), shape(f32, 8, 128)],
-        parts,
-        place_t,
-        far=(0,),
-        scratch=assembly,
-        flops=2 * TALL * HALF * THIRD * NC,
-    )
+    passage_part, targets = lax.optimization_barrier((passage_part, targets))
+    (passage_full,) = call(
+        spread_kernel,
+        [shape(bf16, NC * HALF, SUB)],
+        passage_part,
+        place,
+        flops=2 * NC * HALF * THIRD * SUB,
+    )
+    col_pairs, passage_full = lax.optimization_barrier((col_pairs, passage_full))
     row_pairs = lax.all_to_all(row_pairs, ("x", "core"), 0, 0, tiled=True)
     col_pairs = lax.all_to_all(col_pairs, "z", 0, 0, tiled=True)
     row_pairs = lax.all_gather(merge(row_pairs), "y")
@@ -307,14 +295,13 @@
     dlogits, terms = call(
         passage_kernel,
         [shape(bf16, TALL, 384), shape(bf16, NZ, 112, 128)],
-        logits,
+        placed,
+        passage_part,
         targets,
         ids,
-        placed,
         row_pairs,
         col_pairs,
-        far=(0,),
-        scratch=[kept, pltpu.VMEM((NY, 4 * NY * SLICE, 128), f32), pltpu.SemaphoreType.DMA((len(BLOCKS),))],
+        scratch=[pltpu.VMEM((NY, 4 * NY * SLICE, 128), f32)],
         flops=2 * TALL * SUB * NC * THIRD,
     )
     terms = lax.all_to_all(terms, "z", 0, 0, tiled=True)

time: 144 us -> 137 us (0.951)
  local copies, waits for them, and re-layouts: 4.28 us -> 0.01 us
  Pallas kernels: 14.1 us -> 10.8 us
    unnamed x14 -> x2, local copies, waits for them, and re-layouts: 4.28 us -> 0.01 us
    pallas_call x9, Pallas kernels: 14.1 us -> 10.8 us  [call(): pl.pallas_call(kernel, out_shape=outs, in_specs=[hbm if i in far else sme...]
where the time goes in v6:
time: 137 us; the launch traced here: 136 us
  blocking collectives  68.1 us (50%)
  starting transfers between devices  41.9 us (31%)
  waiting for transfers between devices  14.2 us (10%)
  Pallas kernels  10.8 us (8%)
    all_gather x1, blocking collectives, body(): passage_part = lax.all_gather(passage_part, 'z', axis=0, tiled=True)  35.7 us
    all_to_all x2, blocking collectives, body(): message = lax.all_to_all(message, 'y', 0, 0, tiled=True)  20.5 us
    all_to_all x1, starting transfers between devices, body(): terms = lax.all_to_all(terms, 'z', 0, 0, tiled=True)  12 us
    all_gather x1, blocking collectives, body(): row_pairs = lax.all_gather(merge(row_pairs), 'y')  11.9 us
    ppermute x4, starting transfers between devices, around(): return lax.ppermute(x, axis, [(i, (i + step) % n) for i in range(n)])  11.3 us
    pallas_call x9, Pallas kernels, call(): pl.pallas_call(kernel, out_shape=outs, in_specs=[hbm if i in far else sme...  10.8 us
    all_to_all x1, starting transfers between devices, body(): col_pairs = lax.all_to_all(col_pairs, 'z', 0, 0, tiled=True)  9.5 us
    ppermute x4, waiting for transfers between devices, around(): return lax.ppermute(x, axis, [(i, (i + step) % n) for i in range(n)])  8.09 us
  transfers between devices with their start and end apart: 8, of which 5 were waited for; matrix products, arithmetic and copies ran while one was open for 0% of the time, Pallas kernels for 2%

profile of v6, /device:TPU:64, one launch (start us, length us, event | category | flops | bytes accessed | tf_op | source)
XLA Modules:
  0.0 135.8 jit_solution(5029678441692571790)
XLA Ops:
  0.6 1.1 shard_map.59
  1.7 10.6 %all_to_all.30.came = bf16[4,192,128]{2,1,0:T(8,128)(2,1)S(1)} all-to-all(bf16[4,192,128]{2,1,0:T(8,128)(2,1)S(1)} %shard_map.59), channel_id=1, replica_groups=mesh['y'=4,'z'=16,'x'=4,'core'=2] {'y'}, dimensions={0} | all-to-all | bytes 393216 | tf_op jit(solution)/shard_map/all_to_all | solution.py:256
  12.3 1.2 shard_map.60
  13.5 0.0 copy-start
  13.5 4.4 %all-to-all-start.1 = ((bf16[8,576,128]{2,1,0:T(8,128)(2,1)}), bf16[8,576,128]{2,1,0:T(8,128)(2,1)S(1)}, u32[]{:S(2)}, u32[]{:S(2)}) async-start(bf16[8,576,128]{2,1,0:T(8,128)(2,1)} %get-tuple-element.20), calls=%async_computation.1 | async-start | bytes 2359296 | tf_op jit(solution)/shard_map/all_to_all | solution.py:263
  17.9 35.7 %all_gather.9.passages = bf16[768,288]{1,0:T(8,128)(2,1)S(1)} all-gather(bf16[48,288]{1,0:T(8,128)(2,1)S(1)} %get-tuple-element.21), channel_id=1, replica_groups=mesh['y'=4,'z'=16,'x'=4,'core'=2] {'z'}, dimensions={0}, use_global_device_ids=true | all-gather | bytes 470016 | tf_op jit(solution)/shard_map/all_gather | solution.py:264
  53.6 0.0 all-to-all-done.1.parts
  53.6 0.0 copy-done
  53.6 2.5 %shard_map.61 = (f32[8,16,128]{2,1,0:T(8,128)}, f32[16,8,128]{2,1,0:T(8,128)}, bf16[576,768]{1,0:T(8,128)(2,1)S(1)}, f32[8,128]{1,0:T(8,128)S(1)}) custom-call(bf16[8,576,128]{2,1,0:T(8,128)(2,1)S(1)} %all-to-all-done.1.parts, bf16[768,288]{1,0:T(8,128)(2,1)S(1)} %all_gather.9.passages, bf16[512,384]{1,0:T(8,128)(2,1)S(1)} %copy-done), custom_call_target="tpu_custom_call" | custom-call | flops 339738624 | bytes 3035136 | tf_op jit(solution)/shard_map/pallas_call | solution.py:28
  56.1 4.6 %all-to-all-start.2 = ((f32[8,16,128]{2,1,0:T(8,128)}), f32[8,16,128]{2,1,0:T(8,128)S(1)}, u32[]{:S(2)}, u32[]{:S(2)}) async-start(f32[8,16,128]{2,1,0:T(8,128)} %get-tuple-element.26), calls=%async_computation.2 | async-start | bytes 131072 | tf_op jit(solution)/shard_map/all_to_all | solution.py:289
  60.8 0.6 shard_map.62.passage_full
  61.4 5.0 %all-to-all-done.2 = f32[8,16,128]{2,1,0:T(8,128)S(1)} async-done(((f32[8,16,128]{2,1,0:T(8,128)}), f32[8,16,128]{2,1,0:T(8,128)S(1)}, u32[]{:S(2)}, u32[]{:S(2)}) %all-to-all-start.2) | async-done | bytes 65568 | tf_op jit(solution)/shard_map/all_to_all | solution.py:289
  66.4 9.5 %all-to-all-start.3 = ((f32[16,8,128]{2,1,0:T(8,128)}), f32[16,8,128]{2,1,0:T(8,128)S(1)}, u32[]{:S(2)}, u32[]{:S(2)}) async-start(f32[16,8,128]{2,1,0:T(8,128)} %get-tuple-element.28), calls=%async_computation.3 | async-start | bytes 131072 | tf_op jit(solution)/shard_map/all_to_all | solution.py:290
  75.9 11.9 %all-gather = f32[64,128]{1,0:T(8,128)S(1)} all-gather(f32[16,128]{1,0:T(8,128)S(1)} %pad_maximum_fusion), channel_id=2, replica_groups=mesh['y'=4,'z'=16,'x'=4,'core'=2] {'y'}, dimensions={0}, use_global_device_ids=true | all-gather | bytes 40960 | tf_op jit(solution)/shard_map/all_gather | solution.py:291
  87.9 0.0 all-to-all-done.3.col_pairs
  87.9 2.3 %shard_map.63 = (bf16[576,384]{1,0:T(8,128)(2,1)S(1)}, bf16[16,112,128]{2,1,0:T(8,128)(2,1)}) custom-call(bf16[576,768]{1,0:T(8,128)(2,1)S(1)} %get-tuple-element.22.placed, bf16[768,288]{1,0:T(8,128)(2,1)S(1)} %all_gather.9.passages, f32[8,128]{1,0:T(8,128)S(1)} %get-tuple-element.25.targets, f32[1,288]{1,0:T(1,128)S(1)} %add_convert_fusion.ids, ...), custom_call_target="tpu_custom_call" | custom-call | flops 254803968 | bytes 2331776 | tf_op jit(solution)/shard_map/pallas_call | solution.py:28
  90.2 12.0 %all-to-all-start.4 = ((bf16[16,112,128]{2,1,0:T(8,128)(2,1)}), bf16[16,112,128]{2,1,0:T(8,128)(2,1)S(1)}, u32[]{:S(2)}, u32[]{:S(2)}) async-start(bf16[16,112,128]{2,1,0:T(8,128)(2,1)} %get-tuple-element.29), calls=%async_computation.4 | async-start | bytes 917504 | tf_op jit(solution)/shard_map/all_to_all | solution.py:307
  102.2 0.1 pad_add_fusion.place
  102.3 1.0 shard_map.64
  103.4 1.9 %collective-permute-start = (f32[576,512]{1,0:T(8,128)S(1)}, f32[576,512]{1,0:T(8,128)S(1)}, u32[]{:S(2)}, u32[]{:S(2)}) collective-permute-start(f32[576,512]{1,0:T(8,128)S(1)} %shard_map.64), channel_id=1, source_target_pairs={{0,1},{1,0},{2,3},{3,2},{4,5},{5,4},{6,7},{7,6},{8,9},{9,8},{10,11... | collective-permute-start | bytes 3538952 | tf_op jit(solution)/shard_map/ppermute | solution.py:233
  105.3 2.8 %collective-permute-done.theirs = f32[576,512]{1,0:T(8,128)S(1)} collective-permute-done((f32[576,512]{1,0:T(8,128)S(1)}, f32[576,512]{1,0:T(8,128)S(1)}, u32[]{:S(2)}, u32[]{:S(2)}) %collective-permute-start) | collective-permute-done | bytes 1179680 | tf_op jit(solution)/shard_map/ppermute | solution.py:233
  108.1 1.2 shard_map.65
  109.3 2.5 %collective-permute-start.1 = (bf16[576,128]{1,0:T(8,128)(2,1)S(1)}, bf16[576,128]{1,0:T(8,128)(2,1)S(1)}, u32[]{:S(2)}, u32[]{:S(2)}) collective-permute-start(bf16[576,128]{1,0:T(8,128)(2,1)S(1)} %get-tuple-element.33), channel_id=1, source_target_pairs={{0,2},{2,4},{4,6},{6,0},{1,3},{3,5},{5,7},{7,1},{8,10},{10,12},{12... | collective-permute-start | bytes 442376 | tf_op jit(solution)/shard_map/ppermute | solution.py:233
  111.8 4.0 %collective-permute-start.2 = (bf16[576,128]{1,0:T(8,128)(2,1)S(1)}, bf16[576,128]{1,0:T(8,128)(2,1)S(1)}, u32[]{:S(2)}, u32[]{:S(2)}) collective-permute-start(bf16[576,128]{1,0:T(8,128)(2,1)S(1)} %get-tuple-element.34), channel_id=1, source_target_pairs={{0,4},{2,6},{4,0},{6,2},{1,5},{3,7},{5,1},{7,3},{8,12},{10,14},{12... | collective-permute-start | bytes 442376 | tf_op jit(solution)/shard_map/ppermute | solution.py:233
  115.8 2.9 %collective-permute-start.3 = (bf16[576,128]{1,0:T(8,128)(2,1)S(1)}, bf16[576,128]{1,0:T(8,128)(2,1)S(1)}, u32[]{:S(2)}, u32[]{:S(2)}) collective-permute-start(bf16[576,128]{1,0:T(8,128)(2,1)S(1)} %get-tuple-element.35), channel_id=1, source_target_pairs={{0,6},{2,0},{4,2},{6,4},{1,7},{3,1},{5,3},{7,5},{8,14},{10,8},{12,... | collective-permute-start | bytes 442376 | tf_op jit(solution)/shard_map/ppermute | solution.py:233
  118.7 2.8 %collective-permute-done.1.rest_0_ = bf16[576,128]{1,0:T(8,128)(2,1)S(1)} collective-permute-done((bf16[576,128]{1,0:T(8,128)(2,1)S(1)}, bf16[576,128]{1,0:T(8,128)(2,1)S(1)}, u32[]{:S(2)}, u32[]{:S(2)}) %collective-permute-start.1) | collective-permute-done | bytes 147488 | tf_op jit(solution)/shard_map/ppermute | solution.py:233
  121.5 0.0 collective-permute-done.2.rest_1_
  121.5 2.5 %collective-permute-done.3.rest_2_ = bf16[576,128]{1,0:T(8,128)(2,1)S(1)} collective-permute-done((bf16[576,128]{1,0:T(8,128)(2,1)S(1)}, bf16[576,128]{1,0:T(8,128)(2,1)S(1)}, u32[]{:S(2)}, u32[]{:S(2)}) %collective-permute-start.3) | collective-permute-done | bytes 147488 | tf_op jit(solution)/shard_map/ppermute | solution.py:233
  124.0 1.1 all-to-all-done.4.terms
  125.1 0.1 shard_map.66
  125.2 9.9 %all_to_all.31.came = f32[4,192,128]{2,1,0:T(8,128)S(1)} all-to-all(f32[4,192,128]{2,1,0:T(8,128)S(1)} %shard_map.66), channel_id=1, replica_groups=mesh['y'=4,'z'=16,'x'=4,'core'=2] {'y'}, dimensions={0} | all-to-all | bytes 786432 | tf_op jit(solution)/shard_map/all_to_all | solution.py:326
  135.1 0.7 shard_map.67
  (4 shorter events, 0.0 us)
Async XLA Ops:
  13.5 40.2 %copy-start = (bf16[512,384]{1,0:T(8,128)(2,1)S(1)}, bf16[512,384]{1,0:T(8,128)(2,1)}, u32[]{:S(2)}) copy-start(bf16[512,384]{1,0:T(8,128)(2,1)} %constant.24.clone.place) | copy-start | bytes 1179652
  13.5 40.2 %all-to-all-start.1 = ((bf16[8,576,128]{2,1,0:T(8,128)(2,1)}), bf16[8,576,128]{2,1,0:T(8,128)(2,1)S(1)}, u32[]{:S(2)}, u32[]{:S(2)}) async-start(bf16[8,576,128]{2,1,0:T(8,128)(2,1)} %get-tuple-element.20), calls=%async_computation.1 | async-start | bytes 2359296 | tf_op jit(solution)/shard_map/all_to_all | solution.py:263
  56.1 10.3 %all-to-all-start.2 = ((f32[8,16,128]{2,1,0:T(8,128)}), f32[8,16,128]{2,1,0:T(8,128)S(1)}, u32[]{:S(2)}, u32[]{:S(2)}) async-start(f32[8,16,128]{2,1,0:T(8,128)} %get-tuple-element.26), calls=%async_computation.2 | async-start | bytes 131072 | tf_op jit(solution)/shard_map/all_to_all | solution.py:289
  66.4 21.5 %all-to-all-start.3 = ((f32[16,8,128]{2,1,0:T(8,128)}), f32[16,8,128]{2,1,0:T(8,128)S(1)}, u32[]{:S(2)}, u32[]{:S(2)}) async-start(f32[16,8,128]{2,1,0:T(8,128)} %get-tuple-element.28), calls=%async_computation.3 | async-start | bytes 131072 | tf_op jit(solution)/shard_map/all_to_all | solution.py:290
  90.2 34.9 %all-to-all-start.4 = ((bf16[16,112,128]{2,1,0:T(8,128)(2,1)}), bf16[16,112,128]{2,1,0:T(8,128)(2,1)S(1)}, u32[]{:S(2)}, u32[]{:S(2)}) async-start(bf16[16,112,128]{2,1,0:T(8,128)(2,1)} %get-tuple-element.29), calls=%async_computation.4 | async-start | bytes 917504 | tf_op jit(solution)/shard_map/all_to_all | solution.py:307
  103.4 4.7 %collective-permute-start = (f32[576,512]{1,0:T(8,128)S(1)}, f32[576,512]{1,0:T(8,128)S(1)}, u32[]{:S(2)}, u32[]{:S(2)}) collective-permute-start(f32[576,512]{1,0:T(8,128)S(1)} %shard_map.64), channel_id=1, source_target_pairs={{0,1},{1,0},{2,3},{3,2},{4,5},{5,4},{6,7},{7,6},{8,9},{9,8},{10,11... | collective-permute-start | bytes 3538952 | tf_op jit(solution)/shard_map/ppermute | solution.py:233
  109.3 12.2 %collective-permute-start.1 = (bf16[576,128]{1,0:T(8,128)(2,1)S(1)}, bf16[576,128]{1,0:T(8,128)(2,1)S(1)}, u32[]{:S(2)}, u32[]{:S(2)}) collective-permute-start(bf16[576,128]{1,0:T(8,128)(2,1)S(1)} %get-tuple-element.33), channel_id=1, source_target_pairs={{0,2},{2,4},{4,6},{6,0},{1,3},{3,5},{5,7},{7,1},{8,10},{10,12},{12... | collective-permute-start | bytes 442376 | tf_op jit(solution)/shard_map/ppermute | solution.py:233
  111.8 9.7 %collective-permute-start.2 = (bf16[576,128]{1,0:T(8,128)(2,1)S(1)}, bf16[576,128]{1,0:T(8,128)(2,1)S(1)}, u32[]{:S(2)}, u32[]{:S(2)}) collective-permute-start(bf16[576,128]{1,0:T(8,128)(2,1)S(1)} %get-tuple-element.34), channel_id=1, source_target_pairs={{0,4},{2,6},{4,0},{6,2},{1,5},{3,7},{5,1},{7,3},{8,12},{10,14},{12... | collective-permute-start | bytes 442376 | tf_op jit(solution)/shard_map/ppermute | solution.py:233
  115.8 8.2 %collective-permute-start.3 = (bf16[576,128]{1,0:T(8,128)(2,1)S(1)}, bf16[576,128]{1,0:T(8,128)(2,1)S(1)}, u32[]{:S(2)}, u32[]{:S(2)}) collective-permute-start(bf16[576,128]{1,0:T(8,128)(2,1)S(1)} %get-tuple-element.35), channel_id=1, source_target_pairs={{0,6},{2,0},{4,2},{6,4},{1,7},{3,1},{5,3},{7,5},{8,14},{10,8},{12,... | collective-permute-start | bytes 442376 | tf_op jit(solution)/shard_map/ppermute | solution.py:233

commit v7 on v6

--- a/solution.py
+++ b/solution.py
@@ -96,17 +96,22 @@
         for b in range(3):
             piece = came[y, ROWS + 16 * b : ROWS + 16 * b + 16].astype(f32)
             total[y * SLICE : (y + 1) * SLICE, b * 128 : (b + 1) * 128] = piece[:SLICE]
-        for i in range(NX * NC):
-            queries[i, y * ROWS : (y + 1) * ROWS] = came[y, :ROWS]
+        queries[y * ROWS : (y + 1) * ROWS] = came[y, :ROWS]
     part[...] = total[:, :SUB].astype(bf16)
 
 
-def tile_kernel(parts, passages, place, row_pairs, col_pairs, placed, targets, query_half, logits):
+def tile_kernel(parts, passages, place, row_pairs, col_pairs, placed, targets, query_full, logits, sems):
+    copies = [
+        pltpu.make_async_copy(parts.at[b], query_full.at[:, pl.ds(b * 128, 128)], sems.at[b])
+        for b in range(NC * NX)
+    ]
+    for copy in copies:
+        copy.start()
     for c in range(NC):
-        for x in range(NX):
-            query_half[:, x * 128 : (x + 1) * 128] = parts[c * NX + x]
+        for copy in copies[c * NX : (c + 1) * NX]:
+            copy.wait()
         placed[:, c * THIRD : (c + 1) * THIRD] = jnp.dot(
-            query_half[...], place[...], preferred_element_type=f32
+            query_full[:, c * HALF : (c + 1) * HALF], place[...], preferred_element_type=f32
         ).astype(bf16)
     pairs, col_top = [], None
     for start, size in BLOCKS:
@@ -130,7 +135,7 @@
     lines = jnp.concatenate(lines + [jnp.ones((2, 128), f32)], axis=0)
     for i in range(NZ):
         col_pairs[i] = lines
-    spare = parts[0].astype(f32)
+    spare = query_full[:, :128].astype(f32)
     target = spare[:, WIDTH : WIDTH + 1] * 128.0 + spare[:, WIDTH + 1 : WIDTH + 2]
     targets[...] = columns([(target[start : start + size],) for start, size in BLOCKS], 8)
 
@@ -256,11 +261,11 @@
     message = lax.all_to_all(message, "y", 0, 0, tiled=True)
     parts, passage_part = call(
         split_kernel,
-        [shape(bf16, NX * NC, TALL, 128), shape(bf16, NY * SLICE, SUB)],
+        [shape(bf16, TALL, 128), shape(bf16, NY * SLICE, SUB)],
         message,
         scratch=[pltpu.VMEM((NY * SLICE, 384), f32)],
     )
-    parts = lax.all_to_all(parts, ("core", "x"), 0, 0, tiled=True)
+    parts = lax.all_gather(parts, ("core", "x"))
     passage_part = lax.all_gather(passage_part, "z", axis=0, tiled=True)
 
     row_pairs, col_pairs, placed, targets = call(
@@ -274,7 +279,12 @@
         parts,
         passage_part,
         place,
-        scratch=[pltpu.VMEM((TALL, HALF), bf16), pltpu.VMEM((TALL, SUB), f32)],
+        far=(0,),
+        scratch=[
+            pltpu.VMEM((TALL, NC * HALF), bf16),
+            pltpu.VMEM((TALL, SUB), f32),
+            pltpu.SemaphoreType.DMA((NC * NX,)),
+        ],
         flops=2 * TALL * SUB * NC * HALF,
     )
     passage_part, targets = lax.optimization_barrier((passage_part, targets))

time: 137 us -> 147 us (1.073)
  between operations: 0.72 us -> 14.1 us
  starting transfers between devices: 41.9 us -> 37.4 us
    all_to_all x1 -> x0, starting transfers between devices: 4.43 us -> none  [body(): parts = lax.all_to_all(parts, ('core', 'x'), 0, 0, tiled=True)]
where the time goes in v7:
time: 147 us; the launch traced here: 146 us
  blocking collectives  68.6 us (47%)
  starting transfers between devices  37.4 us (25%)
  waiting for transfers between devices  14.2 us (10%)
  between operations  14.1 us (10%)
  Pallas kernels  11.6 us (8%)
    all_gather x1, blocking collectives, body(): passage_part = lax.all_gather(passage_part, 'z', axis=0, tiled=True)  35.7 us
    all_to_all x2, blocking collectives, body(): message = lax.all_to_all(message, 'y', 0, 0, tiled=True)  21.1 us
    all_to_all x1, starting transfers between devices, body(): terms = lax.all_to_all(terms, 'z', 0, 0, tiled=True)  12 us
    all_gather x1, blocking collectives, body(): row_pairs = lax.all_gather(merge(row_pairs), 'y')  11.9 us
    pallas_call x9, Pallas kernels, call(): pl.pallas_call(kernel, out_shape=outs, in_specs=[hbm if i in far else sme...  11.6 us
    ppermute x4, starting transfers between devices, around(): return lax.ppermute(x, axis, [(i, (i + step) % n) for i in range(n)])  11.3 us
    all_to_all x1, starting transfers between devices, body(): col_pairs = lax.all_to_all(col_pairs, 'z', 0, 0, tiled=True)  9.62 us
    ppermute x4, waiting for transfers between devices, around(): return lax.ppermute(x, axis, [(i, (i + step) % n) for i in range(n)])  8.09 us
  transfers between devices with their start and end apart: 8, of which 5 were waited for; matrix products, arithmetic and copies ran while one was open for 0% of the time, Pallas kernels for 2%

profile of v7, /device:TPU:64, one launch (start us, length us, event | category | flops | bytes accessed | tf_op | source)
XLA Modules:
  0.0 146.1 jit_solution(8244290216667684570)
XLA Ops:
  7.2 0.0 copy-start
  7.2 0.0 all-gather.4.cloned.1.call-start
  7.2 1.1 shard_map.59
  8.3 10.6 %all_to_all.25.came = bf16[4,192,128]{2,1,0:T(8,128)(2,1)S(1)} all-to-all(bf16[4,192,128]{2,1,0:T(8,128)(2,1)S(1)} %shard_map.59), channel_id=1, replica_groups=mesh['y'=4,'z'=16,'x'=4,'core'=2] {'y'}, dimensions={0} | all-to-all | bytes 393216 | tf_op jit(solution)/shard_map/all_to_all | solution.py:261
  18.9 0.7 shard_map.60
  19.6 0.0 all-gather.4.cloned.1.call-update
  19.6 35.7 %all_gather.17.passages = bf16[768,288]{1,0:T(8,128)(2,1)S(1)} all-gather(bf16[48,288]{1,0:T(8,128)(2,1)S(1)} %get-tuple-element.21), channel_id=1, replica_groups=mesh['y'=4,'z'=16,'x'=4,'core'=2] {'z'}, dimensions={0}, use_global_device_ids=true | all-gather | bytes 470016 | tf_op jit(solution)/shard_map/all_gather | solution.py:269
  55.3 0.0 copy-done
  55.3 3.8 %shard_map.61 = (f32[8,16,128]{2,1,0:T(8,128)}, f32[16,8,128]{2,1,0:T(8,128)}, bf16[576,768]{1,0:T(8,128)(2,1)S(1)}, f32[8,128]{1,0:T(8,128)S(1)}) custom-call(bf16[8,576,128]{2,1,0:T(8,128)(2,1)} %bitcast.8, bf16[768,288]{1,0:T(8,128)(2,1)S(1)} %all_gather.17.passages, bf16[512,384]{1,0:T(8,128)(2,1)S(1)} %copy-done), custom_call_target="tpu_custom_call" | custom-call | flops 339738624 | bytes 3035136 | tf_op jit(solution)/shard_map/pallas_call | solution.py:28
  59.1 4.4 %all-to-all-start.1 = ((f32[8,16,128]{2,1,0:T(8,128)}), f32[8,16,128]{2,1,0:T(8,128)S(1)}, u32[]{:S(2)}, u32[]{:S(2)}) async-start(f32[8,16,128]{2,1,0:T(8,128)} %get-tuple-element.26), calls=%async_computation.1 | async-start | bytes 131072 | tf_op jit(solution)/shard_map/all_to_all | solution.py:299
  63.5 0.6 shard_map.62.passage_full
  64.2 5.0 %all-to-all-done.1 = f32[8,16,128]{2,1,0:T(8,128)S(1)} async-done(((f32[8,16,128]{2,1,0:T(8,128)}), f32[8,16,128]{2,1,0:T(8,128)S(1)}, u32[]{:S(2)}, u32[]{:S(2)}) %all-to-all-start.1) | async-done | bytes 65568 | tf_op jit(solution)/shard_map/all_to_all | solution.py:299
  69.1 9.6 %all-to-all-start.2 = ((f32[16,8,128]{2,1,0:T(8,128)}), f32[16,8,128]{2,1,0:T(8,128)S(1)}, u32[]{:S(2)}, u32[]{:S(2)}) async-start(f32[16,8,128]{2,1,0:T(8,128)} %get-tuple-element.28), calls=%async_computation.2 | async-start | bytes 131072 | tf_op jit(solution)/shard_map/all_to_all | solution.py:300
  78.8 11.9 %all-gather.1 = f32[64,128]{1,0:T(8,128)S(1)} all-gather(f32[16,128]{1,0:T(8,128)S(1)} %pad_maximum_fusion), channel_id=3, replica_groups=mesh['y'=4,'z'=16,'x'=4,'core'=2] {'y'}, dimensions={0}, use_global_device_ids=true | all-gather | bytes 40960 | tf_op jit(solution)/shard_map/all_gather | solution.py:301
  90.7 0.0 all-to-all-done.2.col_pairs
  90.7 2.3 %shard_map.63 = (bf16[576,384]{1,0:T(8,128)(2,1)S(1)}, bf16[16,112,128]{2,1,0:T(8,128)(2,1)}) custom-call(bf16[576,768]{1,0:T(8,128)(2,1)S(1)} %get-tuple-element.22.placed, bf16[768,288]{1,0:T(8,128)(2,1)S(1)} %all_gather.17.passages, f32[8,128]{1,0:T(8,128)S(1)} %get-tuple-element.25.targets, f32[1,288]{1,0:T(1,128)S(1)} %add_convert_fusion.ids, ...), custom_call_target="tpu_custom_call" | custom-call | flops 254803968 | bytes 2331776 | tf_op jit(solution)/shard_map/pallas_call | solution.py:28
  93.0 12.0 %all-to-all-start.3 = ((bf16[16,112,128]{2,1,0:T(8,128)(2,1)}), bf16[16,112,128]{2,1,0:T(8,128)(2,1)S(1)}, u32[]{:S(2)}, u32[]{:S(2)}) async-start(bf16[16,112,128]{2,1,0:T(8,128)(2,1)} %get-tuple-element.29), calls=%async_computation.3 | async-start | bytes 917504 | tf_op jit(solution)/shard_map/all_to_all | solution.py:317
  105.1 0.1 pad_add_fusion.place
  105.2 1.0 shard_map.64
  106.2 1.9 %collective-permute-start = (f32[576,512]{1,0:T(8,128)S(1)}, f32[576,512]{1,0:T(8,128)S(1)}, u32[]{:S(2)}, u32[]{:S(2)}) collective-permute-start(f32[576,512]{1,0:T(8,128)S(1)} %shard_map.64), channel_id=1, source_target_pairs={{0,1},{1,0},{2,3},{3,2},{4,5},{5,4},{6,7},{7,6},{8,9},{9,8},{10,11... | collective-permute-start | bytes 3538952 | tf_op jit(solution)/shard_map/ppermute | solution.py:238
  108.1 2.8 %collective-permute-done.theirs = f32[576,512]{1,0:T(8,128)S(1)} collective-permute-done((f32[576,512]{1,0:T(8,128)S(1)}, f32[576,512]{1,0:T(8,128)S(1)}, u32[]{:S(2)}, u32[]{:S(2)}) %collective-permute-start) | collective-permute-done | bytes 1179680 | tf_op jit(solution)/shard_map/ppermute | solution.py:238
  110.9 1.2 shard_map.65
  112.2 2.5 %collective-permute-start.1 = (bf16[576,128]{1,0:T(8,128)(2,1)S(1)}, bf16[576,128]{1,0:T(8,128)(2,1)S(1)}, u32[]{:S(2)}, u32[]{:S(2)}) collective-permute-start(bf16[576,128]{1,0:T(8,128)(2,1)S(1)} %get-tuple-element.33), channel_id=1, source_target_pairs={{0,2},{2,4},{4,6},{6,0},{1,3},{3,5},{5,7},{7,1},{8,10},{10,12},{12... | collective-permute-start | bytes 442376 | tf_op jit(solution)/shard_map/ppermute | solution.py:238
  114.6 4.0 %collective-permute-start.2 = (bf16[576,128]{1,0:T(8,128)(2,1)S(1)}, bf16[576,128]{1,0:T(8,128)(2,1)S(1)}, u32[]{:S(2)}, u32[]{:S(2)}) collective-permute-start(bf16[576,128]{1,0:T(8,128)(2,1)S(1)} %get-tuple-element.34), channel_id=1, source_target_pairs={{0,4},{2,6},{4,0},{6,2},{1,5},{3,7},{5,1},{7,3},{8,12},{10,14},{12... | collective-permute-start | bytes 442376 | tf_op jit(solution)/shard_map/ppermute | solution.py:238
  118.6 2.9 %collective-permute-start.3 = (bf16[576,128]{1,0:T(8,128)(2,1)S(1)}, bf16[576,128]{1,0:T(8,128)(2,1)S(1)}, u32[]{:S(2)}, u32[]{:S(2)}) collective-permute-start(bf16[576,128]{1,0:T(8,128)(2,1)S(1)} %get-tuple-element.35), channel_id=1, source_target_pairs={{0,6},{2,0},{4,2},{6,4},{1,7},{3,1},{5,3},{7,5},{8,14},{10,8},{12,... | collective-permute-start | bytes 442376 | tf_op jit(solution)/shard_map/ppermute | solution.py:238
  121.5 2.8 %collective-permute-done.1.rest_0_ = bf16[576,128]{1,0:T(8,128)(2,1)S(1)} collective-permute-done((bf16[576,128]{1,0:T(8,128)(2,1)S(1)}, bf16[576,128]{1,0:T(8,128)(2,1)S(1)}, u32[]{:S(2)}, u32[]{:S(2)}) %collective-permute-start.1) | collective-permute-done | bytes 147488 | tf_op jit(solution)/shard_map/ppermute | solution.py:238
  124.3 0.0 collective-permute-done.2.rest_1_
  124.3 2.5 %collective-permute-done.3.rest_2_ = bf16[576,128]{1,0:T(8,128)(2,1)S(1)} collective-permute-done((bf16[576,128]{1,0:T(8,128)(2,1)S(1)}, bf16[576,128]{1,0:T(8,128)(2,1)S(1)}, u32[]{:S(2)}, u32[]{:S(2)}) %collective-permute-start.3) | collective-permute-done | bytes 147488 | tf_op jit(solution)/shard_map/ppermute | solution.py:238
  126.8 1.1 all-to-all-done.3.terms
  127.9 0.1 shard_map.66
  128.1 10.5 %all_to_all.26.came = f32[4,192,128]{2,1,0:T(8,128)S(1)} all-to-all(f32[4,192,128]{2,1,0:T(8,128)S(1)} %shard_map.66), channel_id=1, replica_groups=mesh['y'=4,'z'=16,'x'=4,'core'=2] {'y'}, dimensions={0} | all-to-all | bytes 786432 | tf_op jit(solution)/shard_map/all_to_all | solution.py:336
  138.5 0.7 shard_map.67
  (5 shorter events, 0.0 us)
Async XLA Ops:
  7.2 48.1 %copy-start = (bf16[512,384]{1,0:T(8,128)(2,1)S(1)}, bf16[512,384]{1,0:T(8,128)(2,1)}, u32[]{:S(2)}) copy-start(bf16[512,384]{1,0:T(8,128)(2,1)} %constant.24.clone.place) | copy-start | bytes 1179652
  7.2 48.1 %all-gather.4.cloned.1.call-start = ((), (), s32[]{:S(2)}) async-start(), calls=%async_computation.5 | async-start | bytes 1327104 | tf_op jit(solution)/shard_map/all_gather | solution.py:268
  59.1 10.1 %all-to-all-start.1 = ((f32[8,16,128]{2,1,0:T(8,128)}), f32[8,16,128]{2,1,0:T(8,128)S(1)}, u32[]{:S(2)}, u32[]{:S(2)}) async-start(f32[8,16,128]{2,1,0:T(8,128)} %get-tuple-element.26), calls=%async_computation.1 | async-start | bytes 131072 | tf_op jit(solution)/shard_map/all_to_all | solution.py:299
  69.1 21.6 %all-to-all-start.2 = ((f32[16,8,128]{2,1,0:T(8,128)}), f32[16,8,128]{2,1,0:T(8,128)S(1)}, u32[]{:S(2)}, u32[]{:S(2)}) async-start(f32[16,8,128]{2,1,0:T(8,128)} %get-tuple-element.28), calls=%async_computation.2 | async-start | bytes 131072 | tf_op jit(solution)/shard_map/all_to_all | solution.py:300
  93.0 34.9 %all-to-all-start.3 = ((bf16[16,112,128]{2,1,0:T(8,128)(2,1)}), bf16[16,112,128]{2,1,0:T(8,128)(2,1)S(1)}, u32[]{:S(2)}, u32[]{:S(2)}) async-start(bf16[16,112,128]{2,1,0:T(8,128)(2,1)} %get-tuple-element.29), calls=%async_computation.3 | async-start | bytes 917504 | tf_op jit(solution)/shard_map/all_to_all | solution.py:317
  106.2 4.7 %collective-permute-start = (f32[576,512]{1,0:T(8,128)S(1)}, f32[576,512]{1,0:T(8,128)S(1)}, u32[]{:S(2)}, u32[]{:S(2)}) collective-permute-start(f32[576,512]{1,0:T(8,128)S(1)} %shard_map.64), channel_id=1, source_target_pairs={{0,1},{1,0},{2,3},{3,2},{4,5},{5,4},{6,7},{7,6},{8,9},{9,8},{10,11... | collective-permute-start | bytes 3538952 | tf_op jit(solution)/shard_map/ppermute | solution.py:238
  112.2 12.2 %collective-permute-start.1 = (bf16[576,128]{1,0:T(8,128)(2,1)S(1)}, bf16[576,128]{1,0:T(8,128)(2,1)S(1)}, u32[]{:S(2)}, u32[]{:S(2)}) collective-permute-start(bf16[576,128]{1,0:T(8,128)(2,1)S(1)} %get-tuple-element.33), channel_id=1, source_target_pairs={{0,2},{2,4},{4,6},{6,0},{1,3},{3,5},{5,7},{7,1},{8,10},{10,12},{12... | collective-permute-start | bytes 442376 | tf_op jit(solution)/shard_map/ppermute | solution.py:238
  114.6 9.7 %collective-permute-start.2 = (bf16[576,128]{1,0:T(8,128)(2,1)S(1)}, bf16[576,128]{1,0:T(8,128)(2,1)S(1)}, u32[]{:S(2)}, u32[]{:S(2)}) collective-permute-start(bf16[576,128]{1,0:T(8,128)(2,1)S(1)} %get-tuple-element.34), channel_id=1, source_target_pairs={{0,4},{2,6},{4,0},{6,2},{1,5},{3,7},{5,1},{7,3},{8,12},{10,14},{12... | collective-permute-start | bytes 442376 | tf_op jit(solution)/shard_map/ppermute | solution.py:238
  118.6 8.2 %collective-permute-start.3 = (bf16[576,128]{1,0:T(8,128)(2,1)S(1)}, bf16[576,128]{1,0:T(8,128)(2,1)S(1)}, u32[]{:S(2)}, u32[]{:S(2)}) collective-permute-start(bf16[576,128]{1,0:T(8,128)(2,1)S(1)} %get-tuple-element.35), channel_id=1, source_target_pairs={{0,6},{2,0},{4,2},{6,4},{1,7},{3,1},{5,3},{7,5},{8,14},{10,8},{12,... | collective-permute-start | bytes 442376 | tf_op jit(solution)/shard_map/ppermute | solution.py:238
Sparse Core Ops, SparseCore 0:
  19.7 32.9 all-gather.3

commit v8 on v6

--- a/solution.py
+++ b/solution.py
@@ -17,6 +17,7 @@
 THIRD = NZ * NY * SLICE // NC
 BLOCKS = [(0, 128), (128, 128), (256, 128), (384, 128), (512, 64)]
 MSG = ROWS + 48
+QUARTER = ROWS // 4
 GROUP = 384
 NT = (((1,), (1,)), ((), ()))
 TN = (((0,), (0,)), ((), ()))
@@ -135,10 +136,10 @@
     targets[...] = columns([(target[start : start + size],) for start, size in BLOCKS], 8)
 
 
-def spread_kernel(passages, place, passage_full):
-    for c in range(NC):
-        turned = jnp.dot(place[...], passages[c * THIRD : (c + 1) * THIRD], preferred_element_type=f32)
-        passage_full[c * HALF : (c + 1) * HALF] = turned.astype(bf16)
+def spread_kernel(where, passages, place, own_half, other_half):
+    for c, half in ((where[0], own_half), (1 - where[0], other_half)):
+        rows = pl.ds(pl.multiple_of(c * THIRD, THIRD), THIRD)
+        half[...] = jnp.dot(place[...], passages[rows], preferred_element_type=f32).astype(bf16)
 
 
 def passage_kernel(placed, passages, targets, ids, row_pairs, col_pairs, dlogits, terms, tails):
@@ -176,51 +177,77 @@
             terms[first + i, 2 * high : 2 * high + 16] = tail.astype(bf16)
 
 
-def theirs_kernel(place, dlogits, passage_full, theirs):
-    core = place[0]
-    half = passage_full[pl.ds(pl.multiple_of((1 - core) * HALF, HALF), HALF)]
-    theirs[...] = logit_scale * lax.dot_general(dlogits[:, :SUB], half, NT, preferred_element_type=f32)
-
-
-def ours_kernel(place, dlogits, passage_full, theirs, own, *rest):
+def squeeze(block):
+    lane = lax.broadcasted_iota(jnp.int32, (ROWS, 128), 1)
+    tail = block[3 * ROWS :]
+    parts = []
+    for j in range(3):
+        moved = pltpu.roll(tail, WIDTH - 32 * j, 1)
+        parts.append(jnp.where(lane < WIDTH, block[j * ROWS : (j + 1) * ROWS], moved))
+    return jnp.concatenate(parts, axis=0)
+
+
+def query_kernel(where, dlogits, other_dlogits, own_half, other_half, own, *rest):
     outs, total = rest[:-1], rest[-1]
-    core, x = place[0], place[1]
-    half = passage_full[pl.ds(pl.multiple_of(core * HALF, HALF), HALF)]
-    total[...] = theirs[...] + logit_scale * lax.dot_general(
-        dlogits[:, :SUB], half, NT, preferred_element_type=f32
-    )
-    own[...] = total[:, pl.ds(pl.multiple_of(x * 128, 128), 128)]
+    total[...] = logit_scale * (
+        lax.dot_general(dlogits[:, :SUB], own_half[...], NT, preferred_element_type=f32)
+        + lax.dot_general(other_dlogits[:, :SUB], other_half[...], NT, preferred_element_type=f32)
+    )
+    own[...] = squeeze(total[:, pl.ds(pl.multiple_of(where[1] * 128, 128), 128)])
     for step, out in enumerate(outs, 1):
-        lanes = pl.ds(pl.multiple_of(lax.rem(x + step, NX) * 128, 128), 128)
-        out[...] = total[:, lanes].astype(bf16)
+        lanes = pl.ds(pl.multiple_of(lax.rem(where[1] + step, NX) * 128, 128), 128)
+        out[...] = squeeze(total[:, lanes]).astype(bf16)
 
 
 def fold_kernel(terms, own, *rest):
-    came, message, total = rest[:-2], rest[-2], rest[-1]
+    came, message, total, block = rest[:-3], rest[-3], rest[-2], rest[-1]
     high = NY * SLICE
     total[...] = jnp.sum(terms[...].astype(f32), axis=0)
+    lane = lax.broadcasted_iota(jnp.int32, (ROWS, 128), 1)
+    short = lax.broadcasted_iota(jnp.int32, (QUARTER, 128), 1)
+    last = jnp.zeros((ROWS, 128), f32)
     for y in range(NY):
-        rows = slice(y * ROWS, (y + 1) * ROWS)
-        message[y, :ROWS] = own[rows] + sum(c[rows].astype(f32) for c in came)
+        if y < 3:
+            rows = slice(y * ROWS, (y + 1) * ROWS)
+            value = own[rows] + sum(c[rows].astype(f32) for c in came)
+            moved = pltpu.roll(value, (128 + 32 * y - WIDTH) % 128, 1)
+            last = jnp.where((lane >= 32 * y) & (lane < 32 * y + 32), moved, last)
+        else:
+            value = last
+        block[...] = value
+        extra = block[3 * QUARTER :]
+        for j in range(3):
+            moved = pltpu.roll(extra, WIDTH - 32 * j, 1)
+            piece = block[j * QUARTER : (j + 1) * QUARTER]
+            message[y, j * QUARTER : (j + 1) * QUARTER] = jnp.where(short < WIDTH, piece, moved)
         tail = total[2 * high :]
         tail = tail if y == 0 else pltpu.roll(tail, 128 - 32 * y, 1)
         for b in range(3):
             piece = tail[:SLICE] if b == 2 else total[b * high + y * SLICE : b * high + (y + 1) * SLICE]
-            message[y, ROWS + b * 16 : ROWS + b * 16 + SLICE] = piece
-            message[y, ROWS + b * 16 + SLICE : ROWS + b * 16 + 16] = jnp.zeros((16 - SLICE, 128), f32)
-
-
-def final_kernel(came, query_grad, passage_grad):
-    query_grad[...] = jnp.sum(came[:, :ROWS], axis=0)[:, :WIDTH]
-    lane = lax.broadcasted_iota(jnp.int32, (16, 128), 1)
-    total = None
+            message[y, 3 * QUARTER + b * SLICE : 3 * QUARTER + (b + 1) * SLICE] = piece
+
+
+def final_kernel(came, query_grad, passage_grad, total):
+    total[...] = jnp.sum(came[:, : 3 * QUARTER], axis=0)
+    short = lax.broadcasted_iota(jnp.int32, (QUARTER, 128), 1)
+    last = jnp.zeros((QUARTER, 128), f32)
+    for j in range(3):
+        rows = slice(j * QUARTER, (j + 1) * QUARTER)
+        query_grad[rows] = total[rows, :WIDTH]
+        moved = pltpu.roll(total[rows], (128 + 32 * j - WIDTH) % 128, 1)
+        last = jnp.where((short >= 32 * j) & (short < 32 * j + 32), moved, last)
+    query_grad[3 * QUARTER :] = last[:, :WIDTH]
+    lane = lax.broadcasted_iota(jnp.int32, (SLICE, 128), 1)
+    wide = None
     for y in range(NY):
-        blocks = [came[y, ROWS + b * 16 : ROWS + b * 16 + 16] for b in range(3)]
+        first = 3 * QUARTER
+        blocks = [came[y, first + b * SLICE : first + (b + 1) * SLICE] for b in range(3)]
         blocks[2] = jnp.where(lane < SUB - 256, blocks[2], 0.0)
-        wide = jnp.concatenate(blocks + [jnp.zeros((16, COLS - 384), f32)], axis=1)
-        wide = wide if y == 0 else pltpu.roll(wide, y * SUB, 1)
-        total = wide if total is None else total + wide
-    passage_grad[...] = total[:SLICE]
+        row = jnp.concatenate(blocks + [jnp.zeros((SLICE, COLS - 384), f32)], axis=1)
+        row = jnp.concatenate([row, jnp.zeros((16 - SLICE, COLS), f32)], axis=0)
+        row = row if y == 0 else pltpu.roll(row, y * SUB, 1)
+        wide = row if wide is None else wide + row
+    passage_grad[...] = wide[:SLICE]
 
 
 def merge(pairs):
@@ -278,14 +305,17 @@
         flops=2 * TALL * SUB * NC * HALF,
     )
     passage_part, targets = lax.optimization_barrier((passage_part, targets))
-    (passage_full,) = call(
+    own_half, other_half = call(
         spread_kernel,
-        [shape(bf16, NC * HALF, SUB)],
+        [shape(bf16, HALF, SUB)] * 2,
+        where,
         passage_part,
         place,
         flops=2 * NC * HALF * THIRD * SUB,
     )
-    col_pairs, passage_full = lax.optimization_barrier((col_pairs, passage_full))
+    other_half = around(other_half, "core", NC, 1)
+    col_pairs, own_half = lax.optimization_barrier((col_pairs, own_half))
+    targets, other_half = lax.optimization_barrier((targets, other_half))
     row_pairs = lax.all_to_all(row_pairs, ("x", "core"), 0, 0, tiled=True)
     col_pairs = lax.all_to_all(col_pairs, "z", 0, 0, tiled=True)
     row_pairs = lax.all_gather(merge(row_pairs), "y")
@@ -306,25 +336,34 @@
     )
     terms = lax.all_to_all(terms, "z", 0, 0, tiled=True)
 
-    (theirs,) = call(
-        theirs_kernel, [shape(f32, TALL, HALF)], where, dlogits, passage_full, flops=2 * TALL * SUB * HALF
-    )
-    theirs = around(theirs, "core", NC, 1)
     own, *others = call(
-        ours_kernel,
-        [shape(f32, TALL, 128)] + [shape(bf16, TALL, 128)] * (NX - 1),
+        query_kernel,
+        [shape(f32, 3 * ROWS, 128)] + [shape(bf16, 3 * ROWS, 128)] * (NX - 1),
         where,
         dlogits,
-        passage_full,
-        theirs,
+        around(dlogits, "core", NC, 1),
+        own_half,
+        other_half,
         scratch=[pltpu.VMEM((TALL, HALF), f32)],
-        flops=2 * TALL * SUB * HALF,
+        flops=4 * TALL * SUB * HALF,
     )
     came = [around(other, "x", NX, step) for step, other in enumerate(others, 1)]
 
-    (message,) = call(fold_kernel, [shape(f32, NY, MSG, 128)], terms, own, *came, scratch=[pltpu.VMEM((112, 128), f32)])
+    (message,) = call(
+        fold_kernel,
+        [shape(f32, NY, ROWS, 128)],
+        terms,
+        own,
+        *came,
+        scratch=[pltpu.VMEM((112, 128), f32), pltpu.VMEM((ROWS, 128), f32)],
+    )
     message = lax.all_to_all(message, "y", 0, 0, tiled=True)
-    query_grad, passage_grad = call(final_kernel, [shape(f32, ROWS, WIDTH), shape(f32, SLICE, COLS)], message)
+    query_grad, passage_grad = call(
+        final_kernel,
+        [shape(f32, ROWS, WIDTH), shape(f32, SLICE, COLS)],
+        message,
+        scratch=[pltpu.VMEM((3 * QUARTER, 128), f32)],
+    )
     return (query_grad, passage_grad.T)
 
 

time: 137 us -> 136 us (level)
  starting transfers between devices: 41.9 us -> 44.5 us
  waiting for transfers between devices: 14.2 us -> 11.6 us
    all_to_all x1, waiting for transfers between devices: 1.11 us -> 4.48 us  [body(): terms = lax.all_to_all(terms, 'z', 0, 0, tiled=True)]
    all_to_all x1, waiting for transfers between devices: 4.97 us -> 1.93 us  [body(): row_pairs = lax.all_to_all(row_pairs, ('x', 'core'), 0, 0, tiled=True)]
    ppermute x4 -> x5, waiting for transfers between devices: 8.09 us -> 5.21 us  [around(): return lax.ppermute(x, axis, [(i, (i + step) % n) for i in range(n)])]
    ppermute x4 -> x5, starting transfers between devices: 11.3 us -> 13.9 us  [around(): return lax.ppermute(x, axis, [(i, (i + step) % n) for i in range(n)])]
    pallas_call x9 -> x8, Pallas kernels: 10.8 us -> 10.8 us  [call(): pl.pallas_call(kernel, out_shape=outs, in_specs=[hbm if i in far else sme...]
  transfers between devices with their start and end apart: 8 -> 9, of which waited for: 5 -> 5; matrix products, arithmetic and copies ran while one was open for 0% -> 0% of each run, Pallas kernels for 2% -> 2%
where the time goes in v8:
time: 136 us; the launch traced here: 135 us
  blocking collectives  67.6 us (50%)
  starting transfers between devices  44.5 us (33%)
  waiting for transfers between devices  11.6 us (9%)
  Pallas kernels  10.8 us (8%)
    all_gather x1, blocking collectives, body(): passage_part = lax.all_gather(passage_part, 'z', axis=0, tiled=True)  35.7 us
    all_to_all x2, blocking collectives, body(): message = lax.all_to_all(message, 'y', 0, 0, tiled=True)  20 us
    ppermute x5, starting transfers between devices, around(): return lax.ppermute(x, axis, [(i, (i + step) % n) for i in range(n)])  13.9 us
    all_to_all x1, starting transfers between devices, body(): terms = lax.all_to_all(terms, 'z', 0, 0, tiled=True)  12 us
    all_gather x1, blocking collectives, body(): row_pairs = lax.all_gather(merge(row_pairs), 'y')  11.9 us
    pallas_call x8, Pallas kernels, call(): pl.pallas_call(kernel, out_shape=outs, in_specs=[hbm if i in far else sme...  10.8 us
    all_to_all x1, starting transfers between devices, body(): col_pairs = lax.all_to_all(col_pairs, 'z', 0, 0, tiled=True)  9.51 us
    ppermute x5, waiting for transfers between devices, around(): return lax.ppermute(x, axis, [(i, (i + step) % n) for i in range(n)])  5.21 us
  transfers between devices with their start and end apart: 9, of which 5 were waited for; matrix products, arithmetic and copies ran while one was open for 0% of the time, Pallas kernels for 2%

profile of v8, /device:TPU:64, one launch (start us, length us, event | category | flops | bytes accessed | tf_op | source)
XLA Modules:
  0.0 135.5 jit_solution(17636585226533797633)
XLA Ops:
  0.6 1.1 shard_map.59
  1.7 10.6 %all_to_all.30.came = bf16[4,192,128]{2,1,0:T(8,128)(2,1)S(1)} all-to-all(bf16[4,192,128]{2,1,0:T(8,128)(2,1)S(1)} %shard_map.59), channel_id=1, replica_groups=mesh['y'=4,'z'=16,'x'=4,'core'=2] {'y'}, dimensions={0} | all-to-all | bytes 393216 | tf_op jit(solution)/shard_map/all_to_all | solution.py:283
  12.3 1.2 shard_map.60
  13.5 4.4 %all-to-all-start.1 = ((bf16[8,576,128]{2,1,0:T(8,128)(2,1)}), bf16[8,576,128]{2,1,0:T(8,128)(2,1)S(1)}, u32[]{:S(2)}, u32[]{:S(2)}) async-start(bf16[8,576,128]{2,1,0:T(8,128)(2,1)} %get-tuple-element.24), calls=%async_computation.1 | async-start | bytes 2359296 | tf_op jit(solution)/shard_map/all_to_all | solution.py:290
  17.9 35.7 %all_gather.9.passages = bf16[768,288]{1,0:T(8,128)(2,1)S(1)} all-gather(bf16[48,288]{1,0:T(8,128)(2,1)S(1)} %get-tuple-element.25), channel_id=1, replica_groups=mesh['y'=4,'z'=16,'x'=4,'core'=2] {'z'}, dimensions={0}, use_global_device_ids=true | all-gather | bytes 470016 | tf_op jit(solution)/shard_map/all_gather | solution.py:291
  53.7 0.0 all-to-all-done.1.parts
  53.7 0.0 copy-done
  53.7 2.5 %shard_map.61 = (f32[8,16,128]{2,1,0:T(8,128)}, f32[16,8,128]{2,1,0:T(8,128)}, bf16[576,768]{1,0:T(8,128)(2,1)S(1)}, f32[8,128]{1,0:T(8,128)S(1)}) custom-call(bf16[8,576,128]{2,1,0:T(8,128)(2,1)S(1)} %all-to-all-done.1.parts, bf16[768,288]{1,0:T(8,128)(2,1)S(1)} %all_gather.9.passages, bf16[512,384]{1,0:T(8,128)(2,1)S(1)} %copy-done), custom_call_target="tpu_custom_call" | custom-call | flops 339738624 | bytes 3035136 | tf_op jit(solution)/shard_map/pallas_call | solution.py:29
  56.2 4.6 %all-to-all-start.2 = ((f32[8,16,128]{2,1,0:T(8,128)}), f32[8,16,128]{2,1,0:T(8,128)S(1)}, u32[]{:S(2)}, u32[]{:S(2)}) async-start(f32[8,16,128]{2,1,0:T(8,128)} %get-tuple-element.32), calls=%async_computation.2 | async-start | bytes 131072 | tf_op jit(solution)/shard_map/all_to_all | solution.py:319
  60.8 0.1 pad_add_fusion.where
  60.9 1.2 shard_map.62
  62.1 2.4 %collective-permute-start = (bf16[512,288]{1,0:T(8,128)(2,1)S(1)}, bf16[512,288]{1,0:T(8,128)(2,1)S(1)}, u32[]{:S(2)}, u32[]{:S(2)}) collective-permute-start(bf16[512,288]{1,0:T(8,128)(2,1)S(1)} %get-tuple-element.30), channel_id=1, source_target_pairs={{0,1},{1,0},{2,3},{3,2},{4,5},{5,4},{6,7},{7,6},{8,9},{9,8},{10,11... | collective-permute-start | bytes 884744 | tf_op jit(solution)/shard_map/ppermute | solution.py:260
  64.5 1.9 %all-to-all-done.2 = f32[8,16,128]{2,1,0:T(8,128)S(1)} async-done(((f32[8,16,128]{2,1,0:T(8,128)}), f32[8,16,128]{2,1,0:T(8,128)S(1)}, u32[]{:S(2)}, u32[]{:S(2)}) %all-to-all-start.2) | async-done | bytes 65568 | tf_op jit(solution)/shard_map/all_to_all | solution.py:319
  66.4 9.5 %all-to-all-start.3 = ((f32[16,8,128]{2,1,0:T(8,128)}), f32[16,8,128]{2,1,0:T(8,128)S(1)}, u32[]{:S(2)}, u32[]{:S(2)}) async-start(f32[16,8,128]{2,1,0:T(8,128)} %get-tuple-element.35), calls=%async_computation.3 | async-start | bytes 131072 | tf_op jit(solution)/shard_map/all_to_all | solution.py:320
  76.0 11.9 %all-gather = f32[64,128]{1,0:T(8,128)S(1)} all-gather(f32[16,128]{1,0:T(8,128)S(1)} %pad_maximum_fusion), channel_id=2, replica_groups=mesh['y'=4,'z'=16,'x'=4,'core'=2] {'y'}, dimensions={0}, use_global_device_ids=true | all-gather | bytes 40960 | tf_op jit(solution)/shard_map/all_gather | solution.py:321
  87.9 0.0 collective-permute-done.other_half
  87.9 0.0 all-to-all-done.3.col_pairs
  87.9 2.3 %shard_map.63 = (bf16[576,384]{1,0:T(8,128)(2,1)S(1)}, bf16[16,112,128]{2,1,0:T(8,128)(2,1)}) custom-call(bf16[576,768]{1,0:T(8,128)(2,1)S(1)} %get-tuple-element.26.placed, bf16[768,288]{1,0:T(8,128)(2,1)S(1)} %all_gather.9.passages, f32[8,128]{1,0:T(8,128)S(1)} %get-tuple-element.31.targets, f32[1,288]{1,0:T(1,128)S(1)} %add_convert_fusion.ids, ...), custom_call_target="tpu_custom_call" | custom-call | flops 254803968 | bytes 2331776 | tf_op jit(solution)/shard_map/pallas_call | solution.py:29
  90.2 12.0 %all-to-all-start.4 = ((bf16[16,112,128]{2,1,0:T(8,128)(2,1)}), bf16[16,112,128]{2,1,0:T(8,128)(2,1)S(1)}, u32[]{:S(2)}, u32[]{:S(2)}) async-start(bf16[16,112,128]{2,1,0:T(8,128)(2,1)} %get-tuple-element.36), calls=%async_computation.4 | async-start | bytes 917504 | tf_op jit(solution)/shard_map/all_to_all | solution.py:337
  102.2 1.9 %collective-permute-start.1 = (bf16[576,384]{1,0:T(8,128)(2,1)S(1)}, bf16[576,384]{1,0:T(8,128)(2,1)S(1)}, u32[]{:S(2)}, u32[]{:S(2)}) collective-permute-start(bf16[576,384]{1,0:T(8,128)(2,1)S(1)} %get-tuple-element.37.dlogits), channel_id=1, source_target_pairs={{0,1},{1,0},{2,3},{3,2},{4,5},{5,4},{6,7},{7,6},{8,9},{9,8},{10,11... | collective-permute-start | bytes 1327112 | tf_op jit(solution)/shard_map/ppermute | solution.py:260
  104.2 1.8 %collective-permute-done.1.other_dlogits = bf16[576,384]{1,0:T(8,128)(2,1)S(1)} collective-permute-done((bf16[576,384]{1,0:T(8,128)(2,1)S(1)}, bf16[576,384]{1,0:T(8,128)(2,1)S(1)}, u32[]{:S(2)}, u32[]{:S(2)}) %collective-permute-start.1) | collective-permute-done | bytes 442400 | tf_op jit(solution)/shard_map/ppermute | solution.py:260
  105.9 1.6 %shard_map.64 = (f32[432,128]{1,0:T(8,128)S(1)}, bf16[432,128]{1,0:T(8,128)(2,1)S(1)}, bf16[432,128]{1,0:T(8,128)(2,1)S(1)}, bf16[432,128]{1,0:T(8,128)(2,1)S(1)}) custom-call(s32[2]{0:T(128)S(1)} %pad_add_fusion.where, bf16[576,384]{1,0:T(8,128)(2,1)S(1)} %get-tuple-element.37.dlogits, bf16[576,384]{1,0:T(8,128)(2,1)S(1)} %collective-permute-done.1.other_dlogits, ...), custom_call_target="tpu_custom_call" | custom-call | flops 339738624 | bytes 2027528 | tf_op jit(solution)/shard_map/pallas_call | solution.py:29
  107.5 2.5 %collective-permute-start.2 = (bf16[432,128]{1,0:T(8,128)(2,1)S(1)}, bf16[432,128]{1,0:T(8,128)(2,1)S(1)}, u32[]{:S(2)}, u32[]{:S(2)}) collective-permute-start(bf16[432,128]{1,0:T(8,128)(2,1)S(1)} %get-tuple-element.41), channel_id=1, source_target_pairs={{0,2},{2,4},{4,6},{6,0},{1,3},{3,5},{5,7},{7,1},{8,10},{10,12},{12... | collective-permute-start | bytes 331784 | tf_op jit(solution)/shard_map/ppermute | solution.py:260
  110.0 4.0 %collective-permute-start.3 = (bf16[432,128]{1,0:T(8,128)(2,1)S(1)}, bf16[432,128]{1,0:T(8,128)(2,1)S(1)}, u32[]{:S(2)}, u32[]{:S(2)}) collective-permute-start(bf16[432,128]{1,0:T(8,128)(2,1)S(1)} %get-tuple-element.42), channel_id=1, source_target_pairs={{0,4},{2,6},{4,0},{6,2},{1,5},{3,7},{5,1},{7,3},{8,12},{10,14},{12... | collective-permute-start | bytes 331784 | tf_op jit(solution)/shard_map/ppermute | solution.py:260
  114.0 3.2 %collective-permute-start.4 = (bf16[432,128]{1,0:T(8,128)(2,1)S(1)}, bf16[432,128]{1,0:T(8,128)(2,1)S(1)}, u32[]{:S(2)}, u32[]{:S(2)}) collective-permute-start(bf16[432,128]{1,0:T(8,128)(2,1)S(1)} %get-tuple-element.43), channel_id=1, source_target_pairs={{0,6},{2,0},{4,2},{6,4},{1,7},{3,1},{5,3},{7,5},{8,14},{10,8},{12,... | collective-permute-start | bytes 331784 | tf_op jit(solution)/shard_map/ppermute | solution.py:260
  117.1 0.0 collective-permute-done.2.rest_0_
  117.2 1.0 collective-permute-done.3.rest_1_
  118.2 2.4 %collective-permute-done.4.rest_2_ = bf16[432,128]{1,0:T(8,128)(2,1)S(1)} collective-permute-done((bf16[432,128]{1,0:T(8,128)(2,1)S(1)}, bf16[432,128]{1,0:T(8,128)(2,1)S(1)}, u32[]{:S(2)}, u32[]{:S(2)}) %collective-permute-start.4) | collective-permute-done | bytes 110624 | tf_op jit(solution)/shard_map/ppermute | solution.py:260
  120.6 4.5 %all-to-all-done.4.terms = bf16[16,112,128]{2,1,0:T(8,128)(2,1)S(1)} async-done(((bf16[16,112,128]{2,1,0:T(8,128)(2,1)}), bf16[16,112,128]{2,1,0:T(8,128)(2,1)S(1)}, u32[]{:S(2)}, u32[]{:S(2)}) %all-to-all-start.4) | async-done | bytes 458784 | tf_op jit(solution)/shard_map/all_to_all | solution.py:337
  125.1 0.3 shard_map.65
  125.3 9.4 %all_to_all.31.came = f32[4,144,128]{2,1,0:T(8,128)S(1)} all-to-all(f32[4,144,128]{2,1,0:T(8,128)S(1)} %shard_map.65), channel_id=1, replica_groups=mesh['y'=4,'z'=16,'x'=4,'core'=2] {'y'}, dimensions={0} | all-to-all | bytes 589824 | tf_op jit(solution)/shard_map/all_to_all | solution.py:360
  134.7 0.8 shard_map.66
  (5 shorter events, 0.0 us)
Async XLA Ops:
  13.5 40.2 %copy-start = (bf16[512,384]{1,0:T(8,128)(2,1)S(1)}, bf16[512,384]{1,0:T(8,128)(2,1)}, u32[]{:S(2)}) copy-start(bf16[512,384]{1,0:T(8,128)(2,1)} %constant.24.clone.place) | copy-start | bytes 1179652
  13.5 40.2 %all-to-all-start.1 = ((bf16[8,576,128]{2,1,0:T(8,128)(2,1)}), bf16[8,576,128]{2,1,0:T(8,128)(2,1)S(1)}, u32[]{:S(2)}, u32[]{:S(2)}) async-start(bf16[8,576,128]{2,1,0:T(8,128)(2,1)} %get-tuple-element.24), calls=%async_computation.1 | async-start | bytes 2359296 | tf_op jit(solution)/shard_map/all_to_all | solution.py:290
  56.2 10.2 %all-to-all-start.2 = ((f32[8,16,128]{2,1,0:T(8,128)}), f32[8,16,128]{2,1,0:T(8,128)S(1)}, u32[]{:S(2)}, u32[]{:S(2)}) async-start(f32[8,16,128]{2,1,0:T(8,128)} %get-tuple-element.32), calls=%async_computation.2 | async-start | bytes 131072 | tf_op jit(solution)/shard_map/all_to_all | solution.py:319
  62.1 25.8 %collective-permute-start = (bf16[512,288]{1,0:T(8,128)(2,1)S(1)}, bf16[512,288]{1,0:T(8,128)(2,1)S(1)}, u32[]{:S(2)}, u32[]{:S(2)}) collective-permute-start(bf16[512,288]{1,0:T(8,128)(2,1)S(1)} %get-tuple-element.30), channel_id=1, source_target_pairs={{0,1},{1,0},{2,3},{3,2},{4,5},{5,4},{6,7},{7,6},{8,9},{9,8},{10,11... | collective-permute-start | bytes 884744 | tf_op jit(solution)/shard_map/ppermute | solution.py:260
  66.4 21.5 %all-to-all-start.3 = ((f32[16,8,128]{2,1,0:T(8,128)}), f32[16,8,128]{2,1,0:T(8,128)S(1)}, u32[]{:S(2)}, u32[]{:S(2)}) async-start(f32[16,8,128]{2,1,0:T(8,128)} %get-tuple-element.35), calls=%async_computation.3 | async-start | bytes 131072 | tf_op jit(solution)/shard_map/all_to_all | solution.py:320
  90.2 34.9 %all-to-all-start.4 = ((bf16[16,112,128]{2,1,0:T(8,128)(2,1)}), bf16[16,112,128]{2,1,0:T(8,128)(2,1)S(1)}, u32[]{:S(2)}, u32[]{:S(2)}) async-start(bf16[16,112,128]{2,1,0:T(8,128)(2,1)} %get-tuple-element.36), calls=%async_computation.4 | async-start | bytes 917504 | tf_op jit(solution)/shard_map/all_to_all | solution.py:337
  102.2 3.7 %collective-permute-start.1 = (bf16[576,384]{1,0:T(8,128)(2,1)S(1)}, bf16[576,384]{1,0:T(8,128)(2,1)S(1)}, u32[]{:S(2)}, u32[]{:S(2)}) collective-permute-start(bf16[576,384]{1,0:T(8,128)(2,1)S(1)} %get-tuple-element.37.dlogits), channel_id=1, source_target_pairs={{0,1},{1,0},{2,3},{3,2},{4,5},{5,4},{6,7},{7,6},{8,9},{9,8},{10,11... | collective-permute-start | bytes 1327112 | tf_op jit(solution)/shard_map/ppermute | solution.py:260
  107.5 9.7 %collective-permute-start.2 = (bf16[432,128]{1,0:T(8,128)(2,1)S(1)}, bf16[432,128]{1,0:T(8,128)(2,1)S(1)}, u32[]{:S(2)}, u32[]{:S(2)}) collective-permute-start(bf16[432,128]{1,0:T(8,128)(2,1)S(1)} %get-tuple-element.41), channel_id=1, source_target_pairs={{0,2},{2,4},{4,6},{6,0},{1,3},{3,5},{5,7},{7,1},{8,10},{10,12},{12... | collective-permute-start | bytes 331784 | tf_op jit(solution)/shard_map/ppermute | solution.py:260
  110.0 8.2 %collective-permute-start.3 = (bf16[432,128]{1,0:T(8,128)(2,1)S(1)}, bf16[432,128]{1,0:T(8,128)(2,1)S(1)}, u32[]{:S(2)}, u32[]{:S(2)}) collective-permute-start(bf16[432,128]{1,0:T(8,128)(2,1)S(1)} %get-tuple-element.42), channel_id=1, source_target_pairs={{0,4},{2,6},{4,0},{6,2},{1,5},{3,7},{5,1},{7,3},{8,12},{10,14},{12... | collective-permute-start | bytes 331784 | tf_op jit(solution)/shard_map/ppermute | solution.py:260
  114.0 6.6 %collective-permute-start.4 = (bf16[432,128]{1,0:T(8,128)(2,1)S(1)}, bf16[432,128]{1,0:T(8,128)(2,1)S(1)}, u32[]{:S(2)}, u32[]{:S(2)}) collective-permute-start(bf16[432,128]{1,0:T(8,128)(2,1)S(1)} %get-tuple-element.43), channel_id=1, source_target_pairs={{0,6},{2,0},{4,2},{6,4},{1,7},{3,1},{5,3},{7,5},{8,14},{10,8},{12,... | collective-permute-start | bytes 331784 | tf_op jit(solution)/shard_map/ppermute | solution.py:260

commit v9 on v8

--- a/solution.py
+++ b/solution.py
@@ -23,14 +23,14 @@
 TN = (((0,), (0,)), ((), ()))
 
 
-def call(kernel, outs, *args, far=(), scratch=(), flops=0):
+def call(kernel, outs, *args, far=(), far_outs=(), scratch=(), flops=0):
     bytes_accessed = sum(int(np.prod(a.shape)) * a.dtype.itemsize for a in (*args, *outs))
     vmem, smem, hbm = (pl.BlockSpec(memory_space=m) for m in (pltpu.VMEM, pltpu.SMEM, pltpu.HBM))
     return pl.pallas_call(
         kernel,
-        out_shape=outs,
+        out_shape=[pltpu.HBM(o.shape, o.dtype) if i in far_outs else o for i, o in enumerate(outs)],
         in_specs=[hbm if i in far else smem if a.ndim == 1 else vmem for i, a in enumerate(args)],
-        out_specs=[vmem] * len(outs),
+        out_specs=[hbm if i in far_outs else vmem for i in range(len(outs))],
         scratch_shapes=list(scratch),
         compiler_params=pltpu.CompilerParams(vmem_limit_bytes=32 << 20),
         cost_estimate=pl.CostEstimate(flops=flops, bytes_accessed=bytes_accessed, transcendentals=0),
@@ -92,17 +92,51 @@
             message[y, ROWS + 16 * b : ROWS + 16 * b + 16] = piece[:, b * 128 : (b + 1) * 128].astype(bf16)
 
 
-def split_kernel(came, queries, part, total):
+def split_kernel(came, queries, part, total, sems):
+    copies = [
+        pltpu.make_async_copy(
+            came.at[y, pl.ds(0, ROWS)], queries.at[i, pl.ds(y * ROWS, ROWS)], sems.at[y * NX * NC + i]
+        )
+        for y in range(NY)
+        for i in range(NX * NC)
+    ]
+    for copy in copies:
+        copy.start()
     for y in range(NY):
         for b in range(3):
             piece = came[y, ROWS + 16 * b : ROWS + 16 * b + 16].astype(f32)
             total[y * SLICE : (y + 1) * SLICE, b * 128 : (b + 1) * 128] = piece[:SLICE]
-        for i in range(NX * NC):
-            queries[i, y * ROWS : (y + 1) * ROWS] = came[y, :ROWS]
-    part[...] = total[:, :SUB].astype(bf16)
-
-
-def tile_kernel(parts, passages, place, row_pairs, col_pairs, placed, targets, query_half, logits):
+    high = NY * SLICE
+    for b in range(2):
+        part[b * high : (b + 1) * high] = total[:, b * 128 : (b + 1) * 128].astype(bf16)
+    lane = lax.broadcasted_iota(jnp.int32, (SLICE, 128), 1)
+    tail = jnp.zeros((SLICE, 128), f32)
+    for y in range(NY):
+        piece = jnp.where(lane < SUB - 256, total[y * SLICE : (y + 1) * SLICE, 256:], 0.0)
+        tail += piece if y == 0 else pltpu.roll(piece, 32 * y, 1)
+    tail = jnp.concatenate([tail, jnp.zeros((16 - SLICE, 128), f32)], axis=0)
+    part[2 * high :] = tail.astype(bf16)
+    for copy in copies:
+        copy.wait()
+
+
+def unpack(came, passages, tails):
+    high = NY * SLICE
+    for z in range(NZ):
+        for b in range(2):
+            passages[z * high : (z + 1) * high, b * 128 : (b + 1) * 128] = came[z, b * high : (b + 1) * high]
+    packed = came[:, 2 * high :].astype(f32).reshape(NZ * 16, 128)
+    for y in range(NY):
+        moved = packed if y == 0 else pltpu.roll(packed, 128 - 32 * y, 1)
+        for z in range(NZ):
+            tails[z * high + y * SLICE : z * high + (y + 1) * SLICE] = moved[z * 16 : z * 16 + SLICE]
+    passages[:, 256:] = tails[:, : SUB - 256].astype(bf16)
+
+
+def tile_kernel(
+    parts, came, place, passages, row_pairs, col_pairs, placed, targets, query_half, logits, tails, rows, cols, sems
+):
+    unpack(came, passages, tails)
     for c in range(NC):
         for x in range(NX):
             query_half[:, x * 128 : (x + 1) * 128] = parts[c * NX + x]
@@ -119,21 +153,25 @@
         pairs.append((top, jnp.sum(jnp.exp(scores - top), axis=1, keepdims=True)))
         peak = jnp.max(scores, axis=0, keepdims=True)
         col_top = peak if col_top is None else jnp.maximum(col_top, peak)
-    turned = columns(pairs, 16)
-    for i in range(NX * NC):
-        row_pairs[i] = turned
+    rows[...] = columns(pairs, 16)
+    copies = [pltpu.make_async_copy(rows, row_pairs.at[i], sems.at[i]) for i in range(NX * NC)]
+    for copy in copies:
+        copy.start()
     col_sum = jnp.zeros((1, SUB), f32)
     for start, size in BLOCKS:
         col_sum += jnp.sum(jnp.exp(logits[start : start + size] - col_top), axis=0, keepdims=True)
     fill = jnp.ones((1, 384 - SUB), f32)
     both = [jnp.concatenate([v, fill], axis=1) for v in (col_top, col_sum)]
     lines = [v[:, b * 128 : (b + 1) * 128] for v in both for b in range(3)]
-    lines = jnp.concatenate(lines + [jnp.ones((2, 128), f32)], axis=0)
+    cols[...] = jnp.concatenate(lines + [jnp.ones((2, 128), f32)], axis=0)
     for i in range(NZ):
-        col_pairs[i] = lines
+        copies.append(pltpu.make_async_copy(cols, col_pairs.at[i], sems.at[NX * NC + i]))
+        copies[-1].start()
     spare = parts[0].astype(f32)
     target = spare[:, WIDTH : WIDTH + 1] * 128.0 + spare[:, WIDTH + 1 : WIDTH + 2]
     targets[...] = columns([(target[start : start + size],) for start, size in BLOCKS], 8)
+    for copy in copies:
+        copy.wait()
 
 
 def spread_kernel(where, passages, place, own_half, other_half):
@@ -142,7 +180,7 @@
         half[...] = jnp.dot(place[...], passages[rows], preferred_element_type=f32).astype(bf16)
 
 
-def passage_kernel(placed, passages, targets, ids, row_pairs, col_pairs, dlogits, terms, tails):
+def passage_kernel(placed, passages, targets, ids, row_pairs, col_pairs, dlogits, out, tails, terms, sems):
     top, total = row_pairs[:, :8], row_pairs[:, 8:]
     peak = jnp.max(top, axis=0)
     row_lse = upright(peak + jnp.log(jnp.sum(total * jnp.exp(top - peak[None]), axis=0)))
@@ -159,6 +197,7 @@
         hit = jnp.where(target[:size, j : j + 1] == ids[...], 2.0, 0.0)
         dlogits[start : start + size, :SUB] = (slope - hit).astype(bf16)
     high = NY * SLICE
+    copies = []
     for first in range(0, NZ, 4):
         if first * high % GROUP == 0:
             whole = logit_scale * lax.dot_general(
@@ -175,6 +214,11 @@
             tail = sum(tails[a, i * high + a * SLICE : i * high + (a + 1) * SLICE] for a in range(NY))
             tail = jnp.concatenate([tail, jnp.zeros((16 - SLICE, 128), f32)], axis=0)
             terms[first + i, 2 * high : 2 * high + 16] = tail.astype(bf16)
+        group = pl.ds(first, 4)
+        copies.append(pltpu.make_async_copy(terms.at[group], out.at[group], sems.at[first // 4]))
+        copies[-1].start()
+    for copy in copies:
+        copy.wait()
 
 
 def squeeze(block):
@@ -283,16 +327,18 @@
     message = lax.all_to_all(message, "y", 0, 0, tiled=True)
     parts, passage_part = call(
         split_kernel,
-        [shape(bf16, NX * NC, TALL, 128), shape(bf16, NY * SLICE, SUB)],
+        [shape(bf16, NX * NC, TALL, 128), shape(bf16, 112, 128)],
         message,
-        scratch=[pltpu.VMEM((NY * SLICE, 384), f32)],
+        far_outs=(0,),
+        scratch=[pltpu.VMEM((NY * SLICE, 384), f32), pltpu.SemaphoreType.DMA((NY * NX * NC,))],
     )
     parts = lax.all_to_all(parts, ("core", "x"), 0, 0, tiled=True)
-    passage_part = lax.all_gather(passage_part, "z", axis=0, tiled=True)
-
-    row_pairs, col_pairs, placed, targets = call(
+    passage_part = lax.all_gather(passage_part, "z")
+
+    passage_part, row_pairs, col_pairs, placed, targets = call(
         tile_kernel,
         [
+            shape(bf16, NC * THIRD, SUB),
             shape(f32, NX * NC, 16, 128),
             shape(f32, NZ, 8, 128),
             shape(bf16, TALL, NC * THIRD),
@@ -301,10 +347,17 @@
         parts,
         passage_part,
         place,
-        scratch=[pltpu.VMEM((TALL, HALF), bf16), pltpu.VMEM((TALL, SUB), f32)],
+        scratch=[
+            pltpu.VMEM((TALL, HALF), bf16),
+            pltpu.VMEM((TALL, SUB), f32),
+            pltpu.VMEM((NC * THIRD, 128), f32),
+            pltpu.VMEM((16, 128), f32),
+            pltpu.VMEM((8, 128), f32),
+            pltpu.SemaphoreType.DMA((NX * NC + NZ,)),
+        ],
+        far_outs=(1, 2),
         flops=2 * TALL * SUB * NC * HALF,
     )
-    passage_part, targets = lax.optimization_barrier((passage_part, targets))
     own_half, other_half = call(
         spread_kernel,
         [shape(bf16, HALF, SUB)] * 2,
@@ -331,7 +384,12 @@
         ids,
         row_pairs,
         col_pairs,
-        scratch=[pltpu.VMEM((NY, 4 * NY * SLICE, 128), f32)],
+        far_outs=(1,),
+        scratch=[
+            pltpu.VMEM((NY, 4 * NY * SLICE, 128), f32),
+            pltpu.VMEM((NZ, 112, 128), bf16),
+            pltpu.SemaphoreType.DMA((NZ // 4,)),
+        ],
         flops=2 * TALL * SUB * NC * THIRD,
     )
     terms = lax.all_to_all(terms, "z", 0, 0, tiled=True)

time: 136 us -> 136 us (level)
  no operation moved by 1% of the time
where the time goes in v9:
time: 136 us; the launch traced here: 135 us
  blocking collectives  66.9 us (49%)
  starting transfers between devices  44.4 us (33%)
  waiting for transfers between devices  11.6 us (9%)
  Pallas kernels  11.2 us (8%)
    all_gather x1, blocking collectives, body(): passage_part = lax.all_gather(passage_part, 'z')  35 us
    all_to_all x2, blocking collectives, body(): message = lax.all_to_all(message, 'y', 0, 0, tiled=True)  20 us
    ppermute x5, starting transfers between devices, around(): return lax.ppermute(x, axis, [(i, (i + step) % n) for i in range(n)])  14 us
    all_to_all x1, starting transfers between devices, body(): terms = lax.all_to_all(terms, 'z', 0, 0, tiled=True)  12 us
    all_gather x1, blocking collectives, body(): row_pairs = lax.all_gather(merge(row_pairs), 'y')  11.9 us
    pallas_call x8, Pallas kernels, call(): pl.pallas_call(kernel, out_shape=[pltpu.HBM(o.shape, o.dtype) if i in far...  11.2 us
    all_to_all x1, starting transfers between devices, body(): col_pairs = lax.all_to_all(col_pairs, 'z', 0, 0, tiled=True)  9.37 us
    ppermute x5, waiting for transfers between devices, around(): return lax.ppermute(x, axis, [(i, (i + step) % n) for i in range(n)])  5.21 us
  transfers between devices with their start and end apart: 9, of which 5 were waited for; matrix products, arithmetic and copies ran while one was open for 0% of the time, Pallas kernels for 2%

profile of v9, /device:TPU:64, one launch (start us, length us, event | category | flops | bytes accessed | tf_op | source)
XLA Modules:
  0.0 135.0 jit_solution(17266223892777067738)
XLA Ops:
  0.6 1.1 shard_map.59
  1.7 10.6 %all_to_all.30.came = bf16[4,192,128]{2,1,0:T(8,128)(2,1)S(1)} all-to-all(bf16[4,192,128]{2,1,0:T(8,128)(2,1)S(1)} %shard_map.59), channel_id=1, replica_groups=mesh['y'=4,'z'=16,'x'=4,'core'=2] {'y'}, dimensions={0} | all-to-all | bytes 393216 | tf_op jit(solution)/shard_map/all_to_all | solution.py:327
  12.3 1.3 shard_map.60
  13.6 0.0 copy-start
  13.6 4.4 %all-to-all-start.1 = ((bf16[8,576,128]{2,1,0:T(8,128)(2,1)}), bf16[8,576,128]{2,1,0:T(8,128)(2,1)S(1)}, u32[]{:S(2)}, u32[]{:S(2)}) async-start(bf16[8,576,128]{2,1,0:T(8,128)(2,1)} %get-tuple-element.23), calls=%async_computation.1 | async-start | bytes 2359296 | tf_op jit(solution)/shard_map/all_to_all | solution.py:335
  18.1 35.0 %all-gather = bf16[1792,128]{1,0:T(8,128)(2,1)S(1)} all-gather(bf16[112,128]{1,0:T(8,128)(2,1)S(1)} %get-tuple-element.24), channel_id=2, replica_groups=mesh['y'=4,'z'=16,'x'=4,'core'=2] {'z'}, dimensions={0}, use_global_device_ids=true | all-gather | bytes 487424 | tf_op jit(solution)/shard_map/all_gather | solution.py:336
  53.1 0.0 all-to-all-done.1.parts
  53.1 2.7 %shard_map.61 = (bf16[768,288]{1,0:T(8,128)(2,1)S(1)}, f32[8,16,128]{2,1,0:T(8,128)}, f32[16,8,128]{2,1,0:T(8,128)}, bf16[576,768]{1,0:T(8,128)(2,1)S(1)}, f32[8,128]{1,0:T(8,128)S(1)}) custom-call(bf16[8,576,128]{2,1,0:T(8,128)(2,1)S(1)} %all-to-all-done.1.parts, bf16[16,112,128]{2,1,0:T(8,128)(2,1)S(1)} %bitcast.7, bf16[512,384]{1,0:T(8,128)(2,1)S(1)} %copy-done), custom_call_target="tpu_custom_call" | custom-call | flops 339738624 | bytes 3493888 | tf_op jit(solution)/shard_map/pallas_call | solution.py:29
  55.9 4.6 %all-to-all-start.2 = ((f32[8,16,128]{2,1,0:T(8,128)}), f32[8,16,128]{2,1,0:T(8,128)S(1)}, u32[]{:S(2)}, u32[]{:S(2)}) async-start(f32[8,16,128]{2,1,0:T(8,128)} %get-tuple-element.30), calls=%async_computation.2 | async-start | bytes 131072 | tf_op jit(solution)/shard_map/all_to_all | solution.py:372
  60.4 0.1 pad_add_fusion.where
  60.5 1.2 shard_map.62
  61.7 2.4 %collective-permute-start = (bf16[512,288]{1,0:T(8,128)(2,1)S(1)}, bf16[512,288]{1,0:T(8,128)(2,1)S(1)}, u32[]{:S(2)}, u32[]{:S(2)}) collective-permute-start(bf16[512,288]{1,0:T(8,128)(2,1)S(1)} %get-tuple-element.28), channel_id=1, source_target_pairs={{0,1},{1,0},{2,3},{3,2},{4,5},{5,4},{6,7},{7,6},{8,9},{9,8},{10,11... | collective-permute-start | bytes 884744 | tf_op jit(solution)/shard_map/ppermute | solution.py:304
  64.1 1.9 %all-to-all-done.2 = f32[8,16,128]{2,1,0:T(8,128)S(1)} async-done(((f32[8,16,128]{2,1,0:T(8,128)}), f32[8,16,128]{2,1,0:T(8,128)S(1)}, u32[]{:S(2)}, u32[]{:S(2)}) %all-to-all-start.2) | async-done | bytes 65568 | tf_op jit(solution)/shard_map/all_to_all | solution.py:372
  66.1 9.4 %all-to-all-start.3 = ((f32[16,8,128]{2,1,0:T(8,128)}), f32[16,8,128]{2,1,0:T(8,128)S(1)}, u32[]{:S(2)}, u32[]{:S(2)}) async-start(f32[16,8,128]{2,1,0:T(8,128)} %get-tuple-element.33), calls=%async_computation.3 | async-start | bytes 131072 | tf_op jit(solution)/shard_map/all_to_all | solution.py:373
  75.5 11.9 %all-gather.1 = f32[64,128]{1,0:T(8,128)S(1)} all-gather(f32[16,128]{1,0:T(8,128)S(1)} %pad_maximum_fusion), channel_id=3, replica_groups=mesh['y'=4,'z'=16,'x'=4,'core'=2] {'y'}, dimensions={0}, use_global_device_ids=true | all-gather | bytes 40960 | tf_op jit(solution)/shard_map/all_gather | solution.py:374
  87.4 0.0 collective-permute-done.other_half
  87.4 0.0 all-to-all-done.3.col_pairs
  87.4 2.3 %shard_map.63 = (bf16[576,384]{1,0:T(8,128)(2,1)S(1)}, bf16[16,112,128]{2,1,0:T(8,128)(2,1)}) custom-call(bf16[576,768]{1,0:T(8,128)(2,1)S(1)} %get-tuple-element.25.placed, bf16[768,288]{1,0:T(8,128)(2,1)S(1)} %get-tuple-element.26.passages, f32[8,128]{1,0:T(8,128)S(1)} %get-tuple-element.29.targets, f32[1,288]{1,0:T(1,128)S(1)} %add_convert_fusion.ids, ...), custom_call_target="tpu_custom_call" | custom-call | flops 254803968 | bytes 2331776 | tf_op jit(solution)/shard_map/pallas_call | solution.py:29
  89.7 12.0 %all-to-all-start.4 = ((bf16[16,112,128]{2,1,0:T(8,128)(2,1)}), bf16[16,112,128]{2,1,0:T(8,128)(2,1)S(1)}, u32[]{:S(2)}, u32[]{:S(2)}) async-start(bf16[16,112,128]{2,1,0:T(8,128)(2,1)} %get-tuple-element.34), calls=%async_computation.4 | async-start | bytes 917504 | tf_op jit(solution)/shard_map/all_to_all | solution.py:395
  101.8 1.9 %collective-permute-start.1 = (bf16[576,384]{1,0:T(8,128)(2,1)S(1)}, bf16[576,384]{1,0:T(8,128)(2,1)S(1)}, u32[]{:S(2)}, u32[]{:S(2)}) collective-permute-start(bf16[576,384]{1,0:T(8,128)(2,1)S(1)} %get-tuple-element.35.dlogits), channel_id=1, source_target_pairs={{0,1},{1,0},{2,3},{3,2},{4,5},{5,4},{6,7},{7,6},{8,9},{9,8},{10,11... | collective-permute-start | bytes 1327112 | tf_op jit(solution)/shard_map/ppermute | solution.py:304
  103.7 1.8 %collective-permute-done.1.other_dlogits = bf16[576,384]{1,0:T(8,128)(2,1)S(1)} collective-permute-done((bf16[576,384]{1,0:T(8,128)(2,1)S(1)}, bf16[576,384]{1,0:T(8,128)(2,1)S(1)}, u32[]{:S(2)}, u32[]{:S(2)}) %collective-permute-start.1) | collective-permute-done | bytes 442400 | tf_op jit(solution)/shard_map/ppermute | solution.py:304
  105.5 1.6 %shard_map.64 = (f32[432,128]{1,0:T(8,128)S(1)}, bf16[432,128]{1,0:T(8,128)(2,1)S(1)}, bf16[432,128]{1,0:T(8,128)(2,1)S(1)}, bf16[432,128]{1,0:T(8,128)(2,1)S(1)}) custom-call(s32[2]{0:T(128)S(1)} %pad_add_fusion.where, bf16[576,384]{1,0:T(8,128)(2,1)S(1)} %get-tuple-element.35.dlogits, bf16[576,384]{1,0:T(8,128)(2,1)S(1)} %collective-permute-done.1.other_dlogits, ...), custom_call_target="tpu_custom_call" | custom-call | flops 339738624 | bytes 2027528 | tf_op jit(solution)/shard_map/pallas_call | solution.py:29
  107.0 2.5 %collective-permute-start.2 = (bf16[432,128]{1,0:T(8,128)(2,1)S(1)}, bf16[432,128]{1,0:T(8,128)(2,1)S(1)}, u32[]{:S(2)}, u32[]{:S(2)}) collective-permute-start(bf16[432,128]{1,0:T(8,128)(2,1)S(1)} %get-tuple-element.39), channel_id=1, source_target_pairs={{0,2},{2,4},{4,6},{6,0},{1,3},{3,5},{5,7},{7,1},{8,10},{10,12},{12... | collective-permute-start | bytes 331784 | tf_op jit(solution)/shard_map/ppermute | solution.py:304
  109.5 4.0 %collective-permute-start.3 = (bf16[432,128]{1,0:T(8,128)(2,1)S(1)}, bf16[432,128]{1,0:T(8,128)(2,1)S(1)}, u32[]{:S(2)}, u32[]{:S(2)}) collective-permute-start(bf16[432,128]{1,0:T(8,128)(2,1)S(1)} %get-tuple-element.40), channel_id=1, source_target_pairs={{0,4},{2,6},{4,0},{6,2},{1,5},{3,7},{5,1},{7,3},{8,12},{10,14},{12... | collective-permute-start | bytes 331784 | tf_op jit(solution)/shard_map/ppermute | solution.py:304
  113.5 3.2 %collective-permute-start.4 = (bf16[432,128]{1,0:T(8,128)(2,1)S(1)}, bf16[432,128]{1,0:T(8,128)(2,1)S(1)}, u32[]{:S(2)}, u32[]{:S(2)}) collective-permute-start(bf16[432,128]{1,0:T(8,128)(2,1)S(1)} %get-tuple-element.41), channel_id=1, source_target_pairs={{0,6},{2,0},{4,2},{6,4},{1,7},{3,1},{5,3},{7,5},{8,14},{10,8},{12,... | collective-permute-start | bytes 331784 | tf_op jit(solution)/shard_map/ppermute | solution.py:304
  116.7 0.0 collective-permute-done.2.rest_0_
  116.7 1.0 collective-permute-done.3.rest_1_
  117.7 2.4 %collective-permute-done.4.rest_2_ = bf16[432,128]{1,0:T(8,128)(2,1)S(1)} collective-permute-done((bf16[432,128]{1,0:T(8,128)(2,1)S(1)}, bf16[432,128]{1,0:T(8,128)(2,1)S(1)}, u32[]{:S(2)}, u32[]{:S(2)}) %collective-permute-start.4) | collective-permute-done | bytes 110624 | tf_op jit(solution)/shard_map/ppermute | solution.py:304
  120.2 4.5 %all-to-all-done.4.terms = bf16[16,112,128]{2,1,0:T(8,128)(2,1)S(1)} async-done(((bf16[16,112,128]{2,1,0:T(8,128)(2,1)}), bf16[16,112,128]{2,1,0:T(8,128)(2,1)S(1)}, u32[]{:S(2)}, u32[]{:S(2)}) %all-to-all-start.4) | async-done | bytes 458784 | tf_op jit(solution)/shard_map/all_to_all | solution.py:395
  124.6 0.3 shard_map.65
  124.9 9.4 %all_to_all.31.came = f32[4,144,128]{2,1,0:T(8,128)S(1)} all-to-all(f32[4,144,128]{2,1,0:T(8,128)S(1)} %shard_map.65), channel_id=1, replica_groups=mesh['y'=4,'z'=16,'x'=4,'core'=2] {'y'}, dimensions={0} | all-to-all | bytes 589824 | tf_op jit(solution)/shard_map/all_to_all | solution.py:418
  134.3 0.8 shard_map.66
  (5 shorter events, 0.0 us)
Async XLA Ops:
  13.6 39.5 %copy-start = (bf16[512,384]{1,0:T(8,128)(2,1)S(1)}, bf16[512,384]{1,0:T(8,128)(2,1)}, u32[]{:S(2)}) copy-start(bf16[512,384]{1,0:T(8,128)(2,1)} %constant.24.clone.place) | copy-start | bytes 1179652
  13.6 39.5 %all-to-all-start.1 = ((bf16[8,576,128]{2,1,0:T(8,128)(2,1)}), bf16[8,576,128]{2,1,0:T(8,128)(2,1)S(1)}, u32[]{:S(2)}, u32[]{:S(2)}) async-start(bf16[8,576,128]{2,1,0:T(8,128)(2,1)} %get-tuple-element.23), calls=%async_computation.1 | async-start | bytes 2359296 | tf_op jit(solution)/shard_map/all_to_all | solution.py:335
  55.9 10.2 %all-to-all-start.2 = ((f32[8,16,128]{2,1,0:T(8,128)}), f32[8,16,128]{2,1,0:T(8,128)S(1)}, u32[]{:S(2)}, u32[]{:S(2)}) async-start(f32[8,16,128]{2,1,0:T(8,128)} %get-tuple-element.30), calls=%async_computation.2 | async-start | bytes 131072 | tf_op jit(solution)/shard_map/all_to_all | solution.py:372
  61.7 25.7 %collective-permute-start = (bf16[512,288]{1,0:T(8,128)(2,1)S(1)}, bf16[512,288]{1,0:T(8,128)(2,1)S(1)}, u32[]{:S(2)}, u32[]{:S(2)}) collective-permute-start(bf16[512,288]{1,0:T(8,128)(2,1)S(1)} %get-tuple-element.28), channel_id=1, source_target_pairs={{0,1},{1,0},{2,3},{3,2},{4,5},{5,4},{6,7},{7,6},{8,9},{9,8},{10,11... | collective-permute-start | bytes 884744 | tf_op jit(solution)/shard_map/ppermute | solution.py:304
  66.1 21.3 %all-to-all-start.3 = ((f32[16,8,128]{2,1,0:T(8,128)}), f32[16,8,128]{2,1,0:T(8,128)S(1)}, u32[]{:S(2)}, u32[]{:S(2)}) async-start(f32[16,8,128]{2,1,0:T(8,128)} %get-tuple-element.33), calls=%async_computation.3 | async-start | bytes 131072 | tf_op jit(solution)/shard_map/all_to_all | solution.py:373
  89.7 34.9 %all-to-all-start.4 = ((bf16[16,112,128]{2,1,0:T(8,128)(2,1)}), bf16[16,112,128]{2,1,0:T(8,128)(2,1)S(1)}, u32[]{:S(2)}, u32[]{:S(2)}) async-start(bf16[16,112,128]{2,1,0:T(8,128)(2,1)} %get-tuple-element.34), calls=%async_computation.4 | async-start | bytes 917504 | tf_op jit(solution)/shard_map/all_to_all | solution.py:395
  101.8 3.7 %collective-permute-start.1 = (bf16[576,384]{1,0:T(8,128)(2,1)S(1)}, bf16[576,384]{1,0:T(8,128)(2,1)S(1)}, u32[]{:S(2)}, u32[]{:S(2)}) collective-permute-start(bf16[576,384]{1,0:T(8,128)(2,1)S(1)} %get-tuple-element.35.dlogits), channel_id=1, source_target_pairs={{0,1},{1,0},{2,3},{3,2},{4,5},{5,4},{6,7},{7,6},{8,9},{9,8},{10,11... | collective-permute-start | bytes 1327112 | tf_op jit(solution)/shard_map/ppermute | solution.py:304
  107.0 9.7 %collective-permute-start.2 = (bf16[432,128]{1,0:T(8,128)(2,1)S(1)}, bf16[432,128]{1,0:T(8,128)(2,1)S(1)}, u32[]{:S(2)}, u32[]{:S(2)}) collective-permute-start(bf16[432,128]{1,0:T(8,128)(2,1)S(1)} %get-tuple-element.39), channel_id=1, source_target_pairs={{0,2},{2,4},{4,6},{6,0},{1,3},{3,5},{5,7},{7,1},{8,10},{10,12},{12... | collective-permute-start | bytes 331784 | tf_op jit(solution)/shard_map/ppermute | solution.py:304
  109.5 8.2 %collective-permute-start.3 = (bf16[432,128]{1,0:T(8,128)(2,1)S(1)}, bf16[432,128]{1,0:T(8,128)(2,1)S(1)}, u32[]{:S(2)}, u32[]{:S(2)}) collective-permute-start(bf16[432,128]{1,0:T(8,128)(2,1)S(1)} %get-tuple-element.40), channel_id=1, source_target_pairs={{0,4},{2,6},{4,0},{6,2},{1,5},{3,7},{5,1},{7,3},{8,12},{10,14},{12... | collective-permute-start | bytes 331784 | tf_op jit(solution)/shard_map/ppermute | solution.py:304
  113.5 6.6 %collective-permute-start.4 = (bf16[432,128]{1,0:T(8,128)(2,1)S(1)}, bf16[432,128]{1,0:T(8,128)(2,1)S(1)}, u32[]{:S(2)}, u32[]{:S(2)}) collective-permute-start(bf16[432,128]{1,0:T(8,128)(2,1)S(1)} %get-tuple-element.41), channel_id=1, source_target_pairs={{0,6},{2,0},{4,2},{6,4},{1,7},{3,1},{5,3},{7,5},{8,14},{10,8},{12,... | collective-permute-start | bytes 331784 | tf_op jit(solution)/shard_map/ppermute | solution.py:304

commit v10 on v9

--- a/solution.py
+++ b/solution.py
@@ -92,14 +92,10 @@
             message[y, ROWS + 16 * b : ROWS + 16 * b + 16] = piece[:, b * 128 : (b + 1) * 128].astype(bf16)
 
 
-def split_kernel(came, queries, part, total, sems):
-    copies = [
-        pltpu.make_async_copy(
-            came.at[y, pl.ds(0, ROWS)], queries.at[i, pl.ds(y * ROWS, ROWS)], sems.at[y * NX * NC + i]
-        )
-        for y in range(NY)
-        for i in range(NX * NC)
-    ]
+def split_kernel(came, queries, part, staged, total, sems):
+    for y in range(NY):
+        staged[y * ROWS : (y + 1) * ROWS] = came[y, :ROWS]
+    copies = [pltpu.make_async_copy(staged, queries.at[i], sems.at[i]) for i in range(NX * NC)]
     for copy in copies:
         copy.start()
     for y in range(NY):
@@ -205,14 +201,16 @@
             )
         offset = first * high % GROUP
         part = whole[offset : offset + 4 * high]
-        for a in range(NY):
-            tails[a] = part[:, 256:] if a == 0 else pltpu.roll(part[:, 256:], 32 * a, 1)
+        tails[...] = part[:, 256:]
         for i in range(4):
             for b in range(2):
                 piece = part[i * high : (i + 1) * high, b * 128 : (b + 1) * 128]
                 terms[first + i, b * high : (b + 1) * high] = piece.astype(bf16)
-            tail = sum(tails[a, i * high + a * SLICE : i * high + (a + 1) * SLICE] for a in range(NY))
-            tail = jnp.concatenate([tail, jnp.zeros((16 - SLICE, 128), f32)], axis=0)
+            tail = jnp.zeros((16, 128), f32)
+            for a in range(NY):
+                first_row = i * high + a * SLICE
+                piece = jnp.concatenate([tails[first_row : first_row + SLICE], jnp.zeros((16 - SLICE, 128), f32)], axis=0)
+                tail += piece if a == 0 else pltpu.roll(piece, 32 * a, 1)
             terms[first + i, 2 * high : 2 * high + 16] = tail.astype(bf16)
         group = pl.ds(first, 4)
         copies.append(pltpu.make_async_copy(terms.at[group], out.at[group], sems.at[first // 4]))
@@ -330,7 +328,11 @@
         [shape(bf16, NX * NC, TALL, 128), shape(bf16, 112, 128)],
         message,
         far_outs=(0,),
-        scratch=[pltpu.VMEM((NY * SLICE, 384), f32), pltpu.SemaphoreType.DMA((NY * NX * NC,))],
+        scratch=[
+            pltpu.VMEM((TALL, 128), bf16),
+            pltpu.VMEM((NY * SLICE, 384), f32),
+            pltpu.SemaphoreType.DMA((NX * NC,)),
+        ],
     )
     parts = lax.all_to_all(parts, ("core", "x"), 0, 0, tiled=True)
     passage_part = lax.all_gather(passage_part, "z")
@@ -386,7 +388,7 @@
         col_pairs,
         far_outs=(1,),
         scratch=[
-            pltpu.VMEM((NY, 4 * NY * SLICE, 128), f32),
+            pltpu.VMEM((4 * NY * SLICE, 128), f32),
             pltpu.VMEM((NZ, 112, 128), bf16),
             pltpu.SemaphoreType.DMA((NZ // 4,)),
         ],

time: 136 us -> 135 us (level)
  no operation moved by 1% of the time
where the time goes in v10:
time: 135 us
  blocking collectives  66.9 us (50%)
  starting transfers between devices  44.4 us (33%)
  waiting for transfers between devices  11.6 us (9%)
  Pallas kernels  11 us (8%)
    all_gather x1, blocking collectives, body(): passage_part = lax.all_gather(passage_part, 'z')  35 us
    all_to_all x2, blocking collectives, body(): message = lax.all_to_all(message, 'y', 0, 0, tiled=True)  20 us
    ppermute x5, starting transfers between devices, around(): return lax.ppermute(x, axis, [(i, (i + step) % n) for i in range(n)])  14 us
    all_to_all x1, starting transfers between devices, body(): terms = lax.all_to_all(terms, 'z', 0, 0, tiled=True)  12 us
    all_gather x1, blocking collectives, body(): row_pairs = lax.all_gather(merge(row_pairs), 'y')  11.9 us
    pallas_call x8, Pallas kernels, call(): pl.pallas_call(kernel, out_shape=[pltpu.HBM(o.shape, o.dtype) if i in far...  11 us
    all_to_all x1, starting transfers between devices, body(): col_pairs = lax.all_to_all(col_pairs, 'z', 0, 0, tiled=True)  9.37 us
    ppermute x5, waiting for transfers between devices, around(): return lax.ppermute(x, axis, [(i, (i + step) % n) for i in range(n)])  5.2 us
  transfers between devices with their start and end apart: 9, of which 5 were waited for; matrix products, arithmetic and copies ran while one was open for 0% of the time, Pallas kernels for 2%

profile of v10, /device:TPU:64, one launch (start us, length us, event | category | flops | bytes accessed | tf_op | source)
XLA Modules:
  0.0 134.8 jit_solution(16012305878875857354)
XLA Ops:
  0.6 1.1 shard_map.59
  1.7 10.6 %all_to_all.30.came = bf16[4,192,128]{2,1,0:T(8,128)(2,1)S(1)} all-to-all(bf16[4,192,128]{2,1,0:T(8,128)(2,1)S(1)} %shard_map.59), channel_id=1, replica_groups=mesh['y'=4,'z'=16,'x'=4,'core'=2] {'y'}, dimensions={0} | all-to-all | bytes 393216 | tf_op jit(solution)/shard_map/all_to_all | solution.py:325
  12.3 1.1 shard_map.60
  13.4 0.0 copy-start
  13.4 4.4 %all-to-all-start.1 = ((bf16[8,576,128]{2,1,0:T(8,128)(2,1)}), bf16[8,576,128]{2,1,0:T(8,128)(2,1)S(1)}, u32[]{:S(2)}, u32[]{:S(2)}) async-start(bf16[8,576,128]{2,1,0:T(8,128)(2,1)} %get-tuple-element.23), calls=%async_computation.1 | async-start | bytes 2359296 | tf_op jit(solution)/shard_map/all_to_all | solution.py:337
  17.9 35.0 %all-gather = bf16[1792,128]{1,0:T(8,128)(2,1)S(1)} all-gather(bf16[112,128]{1,0:T(8,128)(2,1)S(1)} %get-tuple-element.24), channel_id=2, replica_groups=mesh['y'=4,'z'=16,'x'=4,'core'=2] {'z'}, dimensions={0}, use_global_device_ids=true | all-gather | bytes 487424 | tf_op jit(solution)/shard_map/all_gather | solution.py:338
  52.9 0.0 all-to-all-done.1.parts
  52.9 2.7 %shard_map.61 = (bf16[768,288]{1,0:T(8,128)(2,1)S(1)}, f32[8,16,128]{2,1,0:T(8,128)}, f32[16,8,128]{2,1,0:T(8,128)}, bf16[576,768]{1,0:T(8,128)(2,1)S(1)}, f32[8,128]{1,0:T(8,128)S(1)}) custom-call(bf16[8,576,128]{2,1,0:T(8,128)(2,1)S(1)} %all-to-all-done.1.parts, bf16[16,112,128]{2,1,0:T(8,128)(2,1)S(1)} %bitcast.7, bf16[512,384]{1,0:T(8,128)(2,1)S(1)} %copy-done), custom_call_target="tpu_custom_call" | custom-call | flops 339738624 | bytes 3493888 | tf_op jit(solution)/shard_map/pallas_call | solution.py:29
  55.7 4.6 %all-to-all-start.2 = ((f32[8,16,128]{2,1,0:T(8,128)}), f32[8,16,128]{2,1,0:T(8,128)S(1)}, u32[]{:S(2)}, u32[]{:S(2)}) async-start(f32[8,16,128]{2,1,0:T(8,128)} %get-tuple-element.30), calls=%async_computation.2 | async-start | bytes 131072 | tf_op jit(solution)/shard_map/all_to_all | solution.py:374
  60.3 0.1 pad_add_fusion.where
  60.3 1.2 shard_map.62
  61.5 2.4 %collective-permute-start = (bf16[512,288]{1,0:T(8,128)(2,1)S(1)}, bf16[512,288]{1,0:T(8,128)(2,1)S(1)}, u32[]{:S(2)}, u32[]{:S(2)}) collective-permute-start(bf16[512,288]{1,0:T(8,128)(2,1)S(1)} %get-tuple-element.28), channel_id=1, source_target_pairs={{0,1},{1,0},{2,3},{3,2},{4,5},{5,4},{6,7},{7,6},{8,9},{9,8},{10,11... | collective-permute-start | bytes 884744 | tf_op jit(solution)/shard_map/ppermute | solution.py:302
  64.0 1.9 %all-to-all-done.2 = f32[8,16,128]{2,1,0:T(8,128)S(1)} async-done(((f32[8,16,128]{2,1,0:T(8,128)}), f32[8,16,128]{2,1,0:T(8,128)S(1)}, u32[]{:S(2)}, u32[]{:S(2)}) %all-to-all-start.2) | async-done | bytes 65568 | tf_op jit(solution)/shard_map/all_to_all | solution.py:374
  65.9 9.4 %all-to-all-start.3 = ((f32[16,8,128]{2,1,0:T(8,128)}), f32[16,8,128]{2,1,0:T(8,128)S(1)}, u32[]{:S(2)}, u32[]{:S(2)}) async-start(f32[16,8,128]{2,1,0:T(8,128)} %get-tuple-element.33), calls=%async_computation.3 | async-start | bytes 131072 | tf_op jit(solution)/shard_map/all_to_all | solution.py:375
  75.3 11.9 %all-gather.1 = f32[64,128]{1,0:T(8,128)S(1)} all-gather(f32[16,128]{1,0:T(8,128)S(1)} %pad_maximum_fusion), channel_id=3, replica_groups=mesh['y'=4,'z'=16,'x'=4,'core'=2] {'y'}, dimensions={0}, use_global_device_ids=true | all-gather | bytes 40960 | tf_op jit(solution)/shard_map/all_gather | solution.py:376
  87.2 0.0 collective-permute-done.other_half
  87.2 0.0 all-to-all-done.3.col_pairs
  87.2 2.3 %shard_map.63 = (bf16[576,384]{1,0:T(8,128)(2,1)S(1)}, bf16[16,112,128]{2,1,0:T(8,128)(2,1)}) custom-call(bf16[576,768]{1,0:T(8,128)(2,1)S(1)} %get-tuple-element.25.placed, bf16[768,288]{1,0:T(8,128)(2,1)S(1)} %get-tuple-element.26.passages, f32[8,128]{1,0:T(8,128)S(1)} %get-tuple-element.29.targets, f32[1,288]{1,0:T(1,128)S(1)} %add_convert_fusion.ids, ...), custom_call_target="tpu_custom_call" | custom-call | flops 254803968 | bytes 2331776 | tf_op jit(solution)/shard_map/pallas_call | solution.py:29
  89.5 12.0 %all-to-all-start.4 = ((bf16[16,112,128]{2,1,0:T(8,128)(2,1)}), bf16[16,112,128]{2,1,0:T(8,128)(2,1)S(1)}, u32[]{:S(2)}, u32[]{:S(2)}) async-start(bf16[16,112,128]{2,1,0:T(8,128)(2,1)} %get-tuple-element.34), calls=%async_computation.4 | async-start | bytes 917504 | tf_op jit(solution)/shard_map/all_to_all | solution.py:397
  101.5 1.9 %collective-permute-start.1 = (bf16[576,384]{1,0:T(8,128)(2,1)S(1)}, bf16[576,384]{1,0:T(8,128)(2,1)S(1)}, u32[]{:S(2)}, u32[]{:S(2)}) collective-permute-start(bf16[576,384]{1,0:T(8,128)(2,1)S(1)} %get-tuple-element.35.dlogits), channel_id=1, source_target_pairs={{0,1},{1,0},{2,3},{3,2},{4,5},{5,4},{6,7},{7,6},{8,9},{9,8},{10,11... | collective-permute-start | bytes 1327112 | tf_op jit(solution)/shard_map/ppermute | solution.py:302
  103.4 1.8 %collective-permute-done.1.other_dlogits = bf16[576,384]{1,0:T(8,128)(2,1)S(1)} collective-permute-done((bf16[576,384]{1,0:T(8,128)(2,1)S(1)}, bf16[576,384]{1,0:T(8,128)(2,1)S(1)}, u32[]{:S(2)}, u32[]{:S(2)}) %collective-permute-start.1) | collective-permute-done | bytes 442400 | tf_op jit(solution)/shard_map/ppermute | solution.py:302
  105.2 1.6 %shard_map.64 = (f32[432,128]{1,0:T(8,128)S(1)}, bf16[432,128]{1,0:T(8,128)(2,1)S(1)}, bf16[432,128]{1,0:T(8,128)(2,1)S(1)}, bf16[432,128]{1,0:T(8,128)(2,1)S(1)}) custom-call(s32[2]{0:T(128)S(1)} %pad_add_fusion.where, bf16[576,384]{1,0:T(8,128)(2,1)S(1)} %get-tuple-element.35.dlogits, bf16[576,384]{1,0:T(8,128)(2,1)S(1)} %collective-permute-done.1.other_dlogits, ...), custom_call_target="tpu_custom_call" | custom-call | flops 339738624 | bytes 2027528 | tf_op jit(solution)/shard_map/pallas_call | solution.py:29
  106.8 2.5 %collective-permute-start.2 = (bf16[432,128]{1,0:T(8,128)(2,1)S(1)}, bf16[432,128]{1,0:T(8,128)(2,1)S(1)}, u32[]{:S(2)}, u32[]{:S(2)}) collective-permute-start(bf16[432,128]{1,0:T(8,128)(2,1)S(1)} %get-tuple-element.39), channel_id=1, source_target_pairs={{0,2},{2,4},{4,6},{6,0},{1,3},{3,5},{5,7},{7,1},{8,10},{10,12},{12... | collective-permute-start | bytes 331784 | tf_op jit(solution)/shard_map/ppermute | solution.py:302
  109.3 4.0 %collective-permute-start.3 = (bf16[432,128]{1,0:T(8,128)(2,1)S(1)}, bf16[432,128]{1,0:T(8,128)(2,1)S(1)}, u32[]{:S(2)}, u32[]{:S(2)}) collective-permute-start(bf16[432,128]{1,0:T(8,128)(2,1)S(1)} %get-tuple-element.40), channel_id=1, source_target_pairs={{0,4},{2,6},{4,0},{6,2},{1,5},{3,7},{5,1},{7,3},{8,12},{10,14},{12... | collective-permute-start | bytes 331784 | tf_op jit(solution)/shard_map/ppermute | solution.py:302
  113.2 3.2 %collective-permute-start.4 = (bf16[432,128]{1,0:T(8,128)(2,1)S(1)}, bf16[432,128]{1,0:T(8,128)(2,1)S(1)}, u32[]{:S(2)}, u32[]{:S(2)}) collective-permute-start(bf16[432,128]{1,0:T(8,128)(2,1)S(1)} %get-tuple-element.41), channel_id=1, source_target_pairs={{0,6},{2,0},{4,2},{6,4},{1,7},{3,1},{5,3},{7,5},{8,14},{10,8},{12,... | collective-permute-start | bytes 331784 | tf_op jit(solution)/shard_map/ppermute | solution.py:302
  116.4 0.0 collective-permute-done.2.rest_0_
  116.5 1.0 collective-permute-done.3.rest_1_
  117.5 2.4 %collective-permute-done.4.rest_2_ = bf16[432,128]{1,0:T(8,128)(2,1)S(1)} collective-permute-done((bf16[432,128]{1,0:T(8,128)(2,1)S(1)}, bf16[432,128]{1,0:T(8,128)(2,1)S(1)}, u32[]{:S(2)}, u32[]{:S(2)}) %collective-permute-start.4) | collective-permute-done | bytes 110624 | tf_op jit(solution)/shard_map/ppermute | solution.py:302
  119.9 4.5 %all-to-all-done.4.terms = bf16[16,112,128]{2,1,0:T(8,128)(2,1)S(1)} async-done(((bf16[16,112,128]{2,1,0:T(8,128)(2,1)}), bf16[16,112,128]{2,1,0:T(8,128)(2,1)S(1)}, u32[]{:S(2)}, u32[]{:S(2)}) %all-to-all-start.4) | async-done | bytes 458784 | tf_op jit(solution)/shard_map/all_to_all | solution.py:397
  124.4 0.3 shard_map.65
  124.6 9.4 %all_to_all.31.came = f32[4,144,128]{2,1,0:T(8,128)S(1)} all-to-all(f32[4,144,128]{2,1,0:T(8,128)S(1)} %shard_map.65), channel_id=1, replica_groups=mesh['y'=4,'z'=16,'x'=4,'core'=2] {'y'}, dimensions={0} | all-to-all | bytes 589824 | tf_op jit(solution)/shard_map/all_to_all | solution.py:420
  134.0 0.8 shard_map.66
  (5 shorter events, 0.0 us)
Async XLA Ops:
  13.4 39.5 %copy-start = (bf16[512,384]{1,0:T(8,128)(2,1)S(1)}, bf16[512,384]{1,0:T(8,128)(2,1)}, u32[]{:S(2)}) copy-start(bf16[512,384]{1,0:T(8,128)(2,1)} %constant.24.clone.place) | copy-start | bytes 1179652
  13.4 39.5 %all-to-all-start.1 = ((bf16[8,576,128]{2,1,0:T(8,128)(2,1)}), bf16[8,576,128]{2,1,0:T(8,128)(2,1)S(1)}, u32[]{:S(2)}, u32[]{:S(2)}) async-start(bf16[8,576,128]{2,1,0:T(8,128)(2,1)} %get-tuple-element.23), calls=%async_computation.1 | async-start | bytes 2359296 | tf_op jit(solution)/shard_map/all_to_all | solution.py:337
  55.7 10.2 %all-to-all-start.2 = ((f32[8,16,128]{2,1,0:T(8,128)}), f32[8,16,128]{2,1,0:T(8,128)S(1)}, u32[]{:S(2)}, u32[]{:S(2)}) async-start(f32[8,16,128]{2,1,0:T(8,128)} %get-tuple-element.30), calls=%async_computation.2 | async-start | bytes 131072 | tf_op jit(solution)/shard_map/all_to_all | solution.py:374
  61.5 25.7 %collective-permute-start = (bf16[512,288]{1,0:T(8,128)(2,1)S(1)}, bf16[512,288]{1,0:T(8,128)(2,1)S(1)}, u32[]{:S(2)}, u32[]{:S(2)}) collective-permute-start(bf16[512,288]{1,0:T(8,128)(2,1)S(1)} %get-tuple-element.28), channel_id=1, source_target_pairs={{0,1},{1,0},{2,3},{3,2},{4,5},{5,4},{6,7},{7,6},{8,9},{9,8},{10,11... | collective-permute-start | bytes 884744 | tf_op jit(solution)/shard_map/ppermute | solution.py:302
  65.9 21.3 %all-to-all-start.3 = ((f32[16,8,128]{2,1,0:T(8,128)}), f32[16,8,128]{2,1,0:T(8,128)S(1)}, u32[]{:S(2)}, u32[]{:S(2)}) async-start(f32[16,8,128]{2,1,0:T(8,128)} %get-tuple-element.33), calls=%async_computation.3 | async-start | bytes 131072 | tf_op jit(solution)/shard_map/all_to_all | solution.py:375
  89.5 34.9 %all-to-all-start.4 = ((bf16[16,112,128]{2,1,0:T(8,128)(2,1)}), bf16[16,112,128]{2,1,0:T(8,128)(2,1)S(1)}, u32[]{:S(2)}, u32[]{:S(2)}) async-start(bf16[16,112,128]{2,1,0:T(8,128)(2,1)} %get-tuple-element.34), calls=%async_computation.4 | async-start | bytes 917504 | tf_op jit(solution)/shard_map/all_to_all | solution.py:397
  101.5 3.7 %collective-permute-start.1 = (bf16[576,384]{1,0:T(8,128)(2,1)S(1)}, bf16[576,384]{1,0:T(8,128)(2,1)S(1)}, u32[]{:S(2)}, u32[]{:S(2)}) collective-permute-start(bf16[576,384]{1,0:T(8,128)(2,1)S(1)} %get-tuple-element.35.dlogits), channel_id=1, source_target_pairs={{0,1},{1,0},{2,3},{3,2},{4,5},{5,4},{6,7},{7,6},{8,9},{9,8},{10,11... | collective-permute-start | bytes 1327112 | tf_op jit(solution)/shard_map/ppermute | solution.py:302
  106.8 9.7 %collective-permute-start.2 = (bf16[432,128]{1,0:T(8,128)(2,1)S(1)}, bf16[432,128]{1,0:T(8,128)(2,1)S(1)}, u32[]{:S(2)}, u32[]{:S(2)}) collective-permute-start(bf16[432,128]{1,0:T(8,128)(2,1)S(1)} %get-tuple-element.39), channel_id=1, source_target_pairs={{0,2},{2,4},{4,6},{6,0},{1,3},{3,5},{5,7},{7,1},{8,10},{10,12},{12... | collective-permute-start | bytes 331784 | tf_op jit(solution)/shard_map/ppermute | solution.py:302
  109.3 8.2 %collective-permute-start.3 = (bf16[432,128]{1,0:T(8,128)(2,1)S(1)}, bf16[432,128]{1,0:T(8,128)(2,1)S(1)}, u32[]{:S(2)}, u32[]{:S(2)}) collective-permute-start(bf16[432,128]{1,0:T(8,128)(2,1)S(1)} %get-tuple-element.40), channel_id=1, source_target_pairs={{0,4},{2,6},{4,0},{6,2},{1,5},{3,7},{5,1},{7,3},{8,12},{10,14},{12... | collective-permute-start | bytes 331784 | tf_op jit(solution)/shard_map/ppermute | solution.py:302
  113.2 6.6 %collective-permute-start.4 = (bf16[432,128]{1,0:T(8,128)(2,1)S(1)}, bf16[432,128]{1,0:T(8,128)(2,1)S(1)}, u32[]{:S(2)}, u32[]{:S(2)}) collective-permute-start(bf16[432,128]{1,0:T(8,128)(2,1)S(1)} %get-tuple-element.41), channel_id=1, source_target_pairs={{0,6},{2,0},{4,2},{6,4},{1,7},{3,1},{5,3},{7,5},{8,14},{10,8},{12,... | collective-permute-start | bytes 331784 | tf_op jit(solution)/shard_map/ppermute | solution.py:302

commit v11 on v10

--- a/solution.py
+++ b/solution.py
@@ -130,7 +130,7 @@
 
 
 def tile_kernel(
-    parts, came, place, passages, row_pairs, col_pairs, placed, targets, query_half, logits, tails, rows, cols, sems
+    parts, came, place, passages, row_pairs, col_pairs, placed, targets, query_half, logits, tails, cols, sems
 ):
     unpack(came, passages, tails)
     for c in range(NC):
@@ -149,10 +149,7 @@
         pairs.append((top, jnp.sum(jnp.exp(scores - top), axis=1, keepdims=True)))
         peak = jnp.max(scores, axis=0, keepdims=True)
         col_top = peak if col_top is None else jnp.maximum(col_top, peak)
-    rows[...] = columns(pairs, 16)
-    copies = [pltpu.make_async_copy(rows, row_pairs.at[i], sems.at[i]) for i in range(NX * NC)]
-    for copy in copies:
-        copy.start()
+    row_pairs[...] = columns(pairs, 16)
     col_sum = jnp.zeros((1, SUB), f32)
     for start, size in BLOCKS:
         col_sum += jnp.sum(jnp.exp(logits[start : start + size] - col_top), axis=0, keepdims=True)
@@ -160,9 +157,9 @@
     both = [jnp.concatenate([v, fill], axis=1) for v in (col_top, col_sum)]
     lines = [v[:, b * 128 : (b + 1) * 128] for v in both for b in range(3)]
     cols[...] = jnp.concatenate(lines + [jnp.ones((2, 128), f32)], axis=0)
-    for i in range(NZ):
-        copies.append(pltpu.make_async_copy(cols, col_pairs.at[i], sems.at[NX * NC + i]))
-        copies[-1].start()
+    copies = [pltpu.make_async_copy(cols, col_pairs.at[i], sems.at[i]) for i in range(NZ)]
+    for copy in copies:
+        copy.start()
     spare = parts[0].astype(f32)
     target = spare[:, WIDTH : WIDTH + 1] * 128.0 + spare[:, WIDTH + 1 : WIDTH + 2]
     targets[...] = columns([(target[start : start + size],) for start, size in BLOCKS], 8)
@@ -170,10 +167,14 @@
         copy.wait()
 
 
-def spread_kernel(where, passages, place, own_half, other_half):
-    for c, half in ((where[0], own_half), (1 - where[0], other_half)):
+def spread_kernel(where, passages, place, own_half, other_out, other_half, sem):
+    for c, half in ((1 - where[0], other_half), (where[0], own_half)):
         rows = pl.ds(pl.multiple_of(c * THIRD, THIRD), THIRD)
         half[...] = jnp.dot(place[...], passages[rows], preferred_element_type=f32).astype(bf16)
+        if half is other_half:
+            copy = pltpu.make_async_copy(other_half, other_out, sem)
+            copy.start()
+    copy.wait()
 
 
 def passage_kernel(placed, passages, targets, ids, row_pairs, col_pairs, dlogits, out, tails, terms, sems):
@@ -341,7 +342,7 @@
         tile_kernel,
         [
             shape(bf16, NC * THIRD, SUB),
-            shape(f32, NX * NC, 16, 128),
+            shape(f32, 16, 128),
             shape(f32, NZ, 8, 128),
             shape(bf16, TALL, NC * THIRD),
             shape(f32, 8, 128),
@@ -353,27 +354,28 @@
             pltpu.VMEM((TALL, HALF), bf16),
             pltpu.VMEM((TALL, SUB), f32),
             pltpu.VMEM((NC * THIRD, 128), f32),
-            pltpu.VMEM((16, 128), f32),
             pltpu.VMEM((8, 128), f32),
-            pltpu.SemaphoreType.DMA((NX * NC + NZ,)),
+            pltpu.SemaphoreType.DMA((NZ,)),
         ],
-        far_outs=(1, 2),
+        far_outs=(2,),
         flops=2 * TALL * SUB * NC * HALF,
     )
+    col_pairs = lax.all_to_all(col_pairs, "z", 0, 0, tiled=True)
     own_half, other_half = call(
         spread_kernel,
         [shape(bf16, HALF, SUB)] * 2,
         where,
         passage_part,
         place,
+        far_outs=(1,),
+        scratch=[pltpu.VMEM((HALF, SUB), bf16), pltpu.SemaphoreType.DMA],
         flops=2 * NC * HALF * THIRD * SUB,
     )
-    other_half = around(other_half, "core", NC, 1)
-    col_pairs, own_half = lax.optimization_barrier((col_pairs, own_half))
-    targets, other_half = lax.optimization_barrier((targets, other_half))
+    row_pairs, own_half = lax.optimization_barrier((row_pairs, own_half))
+    row_pairs = merge(lax.all_gather(row_pairs, "y"))
+    row_pairs, col_pairs = lax.optimization_barrier((row_pairs, col_pairs))
+    row_pairs = jnp.broadcast_to(row_pairs[None], (NX * NC, 16, 128))
     row_pairs = lax.all_to_all(row_pairs, ("x", "core"), 0, 0, tiled=True)
-    col_pairs = lax.all_to_all(col_pairs, "z", 0, 0, tiled=True)
-    row_pairs = lax.all_gather(merge(row_pairs), "y")
 
     block = (lax.axis_index("x") * NC + lax.axis_index("core")) * NY + lax.axis_index("y")
     ids = (block * SUB + jnp.arange(SUB, dtype=jnp.int32)).astype(f32)[None]
@@ -395,6 +397,8 @@
         flops=2 * TALL * SUB * NC * THIRD,
     )
     terms = lax.all_to_all(terms, "z", 0, 0, tiled=True)
+    dlogits, other_half = lax.optimization_barrier((dlogits, other_half))
+    other_half = around(other_half, "core", NC, 1)
 
     own, *others = call(
         query_kernel,

time: 135 us -> 141 us (1.044)
  the two profiles are of different devices: /device:TPU:64 before, /device:TPU:2 now
where the time goes in v11:
time: 141 us; the launch traced here: 140 us
  blocking collectives  67.1 us (48%)
  starting transfers between devices  45.4 us (32%)
  waiting for transfers between devices  14.8 us (10%)
  Pallas kernels  11.1 us (8%)
    all_gather x1, blocking collectives, body(): passage_part = lax.all_gather(passage_part, 'z')  35.2 us
    all_to_all x2, blocking collectives, body(): message = lax.all_to_all(message, 'y', 0, 0, tiled=True)  20 us
    ppermute x5, starting transfers between devices, around(): return lax.ppermute(x, axis, [(i, (i + step) % n) for i in range(n)])  14.2 us
    all_to_all x1, starting transfers between devices, body(): terms = lax.all_to_all(terms, 'z', 0, 0, tiled=True)  12 us
    all_gather x1, blocking collectives, body(): row_pairs = merge(lax.all_gather(row_pairs, 'y'))  11.9 us
    pallas_call x8, Pallas kernels, call(): pl.pallas_call(kernel, out_shape=[pltpu.HBM(o.shape, o.dtype) if i in far...  11.1 us
    all_to_all x1, starting transfers between devices, body(): parts = lax.all_to_all(parts, ('core', 'x'), 0, 0, tiled=True)  7.62 us
    all_to_all x1, starting transfers between devices, body(): col_pairs = lax.all_to_all(col_pairs, 'z', 0, 0, tiled=True)  7.15 us
  transfers between devices with their start and end apart: 9, of which 5 were waited for; matrix products, arithmetic and copies ran while one was open for 0% of the time, Pallas kernels for 2%

profile of v11, /device:TPU:2, one launch (start us, length us, event | category | flops | bytes accessed | tf_op | source)
XLA Modules:
  0.0 140.0 jit_solution(10368646602252089461)
XLA Ops:
  0.6 1.1 shard_map.59
  1.7 10.6 %all_to_all.30.came = bf16[4,192,128]{2,1,0:T(8,128)(2,1)S(1)} all-to-all(bf16[4,192,128]{2,1,0:T(8,128)(2,1)S(1)} %shard_map.59), channel_id=1, replica_groups=mesh['y'=4,'z'=16,'x'=4,'core'=2] {'y'}, dimensions={0} | all-to-all | bytes 393216 | tf_op jit(solution)/shard_map/all_to_all | solution.py:326
  12.3 1.1 shard_map.60
  13.4 0.0 copy-start
  13.4 7.6 %all-to-all-start.1 = ((bf16[8,576,128]{2,1,0:T(8,128)(2,1)}), bf16[8,576,128]{2,1,0:T(8,128)(2,1)S(1)}, u32[]{:S(2)}, u32[]{:S(2)}) async-start(bf16[8,576,128]{2,1,0:T(8,128)(2,1)} %get-tuple-element.25), calls=%async_computation.1 | async-start | bytes 2359296 | tf_op jit(solution)/shard_map/all_to_all | solution.py:338
  21.0 0.1 pad_add_fusion.where
  21.1 35.2 %all-gather = bf16[1792,128]{1,0:T(8,128)(2,1)S(1)} all-gather(bf16[112,128]{1,0:T(8,128)(2,1)S(1)} %get-tuple-element.26), channel_id=2, replica_groups=mesh['y'=4,'z'=16,'x'=4,'core'=2] {'z'}, dimensions={0}, use_global_device_ids=true | all-gather | bytes 487424 | tf_op jit(solution)/shard_map/all_gather | solution.py:339
  56.3 0.0 all-to-all-done.1.parts
  56.3 2.5 %shard_map.61 = (bf16[768,288]{1,0:T(8,128)(2,1)S(1)}, f32[16,128]{1,0:T(8,128)S(1)}, f32[16,8,128]{2,1,0:T(8,128)}, bf16[576,768]{1,0:T(8,128)(2,1)S(1)}, f32[8,128]{1,0:T(8,128)S(1)}) custom-call(bf16[8,576,128]{2,1,0:T(8,128)(2,1)S(1)} %all-to-all-done.1.parts, bf16[16,112,128]{2,1,0:T(8,128)(2,1)S(1)} %bitcast.7, bf16[512,384]{1,0:T(8,128)(2,1)S(1)} %copy-done), custom_call_target="tpu_custom_call" | custom-call | flops 339738624 | bytes 3436544 | tf_op jit(solution)/shard_map/pallas_call | solution.py:29
  58.8 7.1 %all-to-all-start.2 = ((f32[16,8,128]{2,1,0:T(8,128)}), f32[16,8,128]{2,1,0:T(8,128)S(1)}, u32[]{:S(2)}, u32[]{:S(2)}) async-start(f32[16,8,128]{2,1,0:T(8,128)} %get-tuple-element.33), calls=%async_computation.2 | async-start | bytes 131072 | tf_op jit(solution)/shard_map/all_to_all | solution.py:363
  65.9 1.7 %shard_map.62 = (bf16[512,288]{1,0:T(8,128)(2,1)S(1)}, bf16[512,288]{1,0:T(8,128)(2,1)}) custom-call(s32[2]{0:T(128)S(1)} %pad_add_fusion.where, bf16[768,288]{1,0:T(8,128)(2,1)S(1)} %get-tuple-element.28.passages, bf16[512,384]{1,0:T(8,128)(2,1)S(1)} %copy-done), custom_call_target="tpu_custom_call" | custom-call | flops 226492416 | bytes 1425416 | tf_op jit(solution)/shard_map/pallas_call | solution.py:29
  67.7 11.9 %all-gather.1 = f32[64,128]{1,0:T(8,128)S(1)} all-gather(f32[16,128]{1,0:T(8,128)S(1)} %get-tuple-element.32), channel_id=3, replica_groups=mesh['y'=4,'z'=16,'x'=4,'core'=2] {'y'}, dimensions={0}, use_global_device_ids=true | all-gather | bytes 40960 | tf_op jit(solution)/shard_map/all_gather | solution.py:375
  79.6 0.0 all-to-all-done.2.col_pairs
  79.6 0.6 broadcast_in_dim.5
  80.3 4.4 %all-to-all-start.3 = ((f32[8,16,128]{2,1,0:T(8,128)}), f32[8,16,128]{2,1,0:T(8,128)S(1)}, u32[]{:S(2)}, u32[]{:S(2)}) async-start(f32[8,16,128]{2,1,0:T(8,128)} %broadcast_in_dim.5), calls=%async_computation.3 | async-start | bytes 131072 | tf_op jit(solution)/shard_map/all_to_all | solution.py:378
  84.7 4.2 %all-to-all-done.3.row_pairs = f32[8,16,128]{2,1,0:T(8,128)S(1)} async-done(((f32[8,16,128]{2,1,0:T(8,128)}), f32[8,16,128]{2,1,0:T(8,128)S(1)}, u32[]{:S(2)}, u32[]{:S(2)}) %all-to-all-start.3) | async-done | bytes 65568 | tf_op jit(solution)/shard_map/all_to_all | solution.py:378
  88.9 2.2 %shard_map.63 = (bf16[576,384]{1,0:T(8,128)(2,1)S(1)}, bf16[16,112,128]{2,1,0:T(8,128)(2,1)}) custom-call(bf16[576,768]{1,0:T(8,128)(2,1)S(1)} %get-tuple-element.27.placed, bf16[768,288]{1,0:T(8,128)(2,1)S(1)} %get-tuple-element.28.passages, f32[8,128]{1,0:T(8,128)S(1)} %get-tuple-element.29.targets, f32[1,288]{1,0:T(1,128)S(1)} %add_convert_fusion.ids, ...), custom_call_target="tpu_custom_call" | custom-call | flops 254803968 | bytes 2364544 | tf_op jit(solution)/shard_map/pallas_call | solution.py:29
  91.1 12.0 %all-to-all-start.4 = ((bf16[16,112,128]{2,1,0:T(8,128)(2,1)}), bf16[16,112,128]{2,1,0:T(8,128)(2,1)S(1)}, u32[]{:S(2)}, u32[]{:S(2)}) async-start(bf16[16,112,128]{2,1,0:T(8,128)(2,1)} %get-tuple-element.36), calls=%async_computation.4 | async-start | bytes 917504 | tf_op jit(solution)/shard_map/all_to_all | solution.py:399
  103.1 1.9 %collective-permute-start = (bf16[576,384]{1,0:T(8,128)(2,1)S(1)}, bf16[576,384]{1,0:T(8,128)(2,1)S(1)}, u32[]{:S(2)}, u32[]{:S(2)}) collective-permute-start(bf16[576,384]{1,0:T(8,128)(2,1)S(1)} %get-tuple-element.39.dlogits), channel_id=1, source_target_pairs={{0,1},{1,0},{2,3},{3,2},{4,5},{5,4},{6,7},{7,6},{8,9},{9,8},{10,11... | collective-permute-start | bytes 1327112 | tf_op jit(solution)/shard_map/ppermute | solution.py:303
  105.0 2.4 %collective-permute-start.1 = (bf16[512,288]{1,0:T(8,128)(2,1)S(1)}, bf16[512,288]{1,0:T(8,128)(2,1)S(1)}, u32[]{:S(2)}, u32[]{:S(2)}) collective-permute-start(bf16[512,288]{1,0:T(8,128)(2,1)S(1)} %copy-done.1), channel_id=1, source_target_pairs={{0,1},{1,0},{2,3},{3,2},{4,5},{5,4},{6,7},{7,6},{8,9},{9,8},{10,11... | collective-permute-start | bytes 884744 | tf_op jit(solution)/shard_map/ppermute | solution.py:303
  107.4 1.3 collective-permute-done.1.other_half
  108.8 0.0 collective-permute-done.other_dlogits
  108.8 1.6 %shard_map.64 = (f32[432,128]{1,0:T(8,128)S(1)}, bf16[432,128]{1,0:T(8,128)(2,1)S(1)}, bf16[432,128]{1,0:T(8,128)(2,1)S(1)}, bf16[432,128]{1,0:T(8,128)(2,1)S(1)}) custom-call(s32[2]{0:T(128)S(1)} %pad_add_fusion.where, bf16[576,384]{1,0:T(8,128)(2,1)S(1)} %get-tuple-element.39.dlogits, bf16[576,384]{1,0:T(8,128)(2,1)S(1)} %collective-permute-done.other_dlogits, ...), custom_call_target="tpu_custom_call" | custom-call | flops 339738624 | bytes 2027528 | tf_op jit(solution)/shard_map/pallas_call | solution.py:29
  110.4 2.3 %collective-permute-start.2 = (bf16[432,128]{1,0:T(8,128)(2,1)S(1)}, bf16[432,128]{1,0:T(8,128)(2,1)S(1)}, u32[]{:S(2)}, u32[]{:S(2)}) collective-permute-start(bf16[432,128]{1,0:T(8,128)(2,1)S(1)} %get-tuple-element.43), channel_id=1, source_target_pairs={{0,2},{2,4},{4,6},{6,0},{1,3},{3,5},{5,7},{7,1},{8,10},{10,12},{12... | collective-permute-start | bytes 331784 | tf_op jit(solution)/shard_map/ppermute | solution.py:303
  112.7 5.1 %collective-permute-start.3 = (bf16[432,128]{1,0:T(8,128)(2,1)S(1)}, bf16[432,128]{1,0:T(8,128)(2,1)S(1)}, u32[]{:S(2)}, u32[]{:S(2)}) collective-permute-start(bf16[432,128]{1,0:T(8,128)(2,1)S(1)} %get-tuple-element.44), channel_id=1, source_target_pairs={{0,4},{2,6},{4,0},{6,2},{1,5},{3,7},{5,1},{7,3},{8,12},{10,14},{12... | collective-permute-start | bytes 331784 | tf_op jit(solution)/shard_map/ppermute | solution.py:303
  117.7 2.5 %collective-permute-start.4 = (bf16[432,128]{1,0:T(8,128)(2,1)S(1)}, bf16[432,128]{1,0:T(8,128)(2,1)S(1)}, u32[]{:S(2)}, u32[]{:S(2)}) collective-permute-start(bf16[432,128]{1,0:T(8,128)(2,1)S(1)} %get-tuple-element.45), channel_id=1, source_target_pairs={{0,6},{2,0},{4,2},{6,4},{1,7},{3,1},{5,3},{7,5},{8,14},{10,8},{12,... | collective-permute-start | bytes 331784 | tf_op jit(solution)/shard_map/ppermute | solution.py:303
  120.2 0.9 collective-permute-done.3.rest_1_
  121.1 3.3 %collective-permute-done.4.rest_2_ = bf16[432,128]{1,0:T(8,128)(2,1)S(1)} collective-permute-done((bf16[432,128]{1,0:T(8,128)(2,1)S(1)}, bf16[432,128]{1,0:T(8,128)(2,1)S(1)}, u32[]{:S(2)}, u32[]{:S(2)}) %collective-permute-start.4) | collective-permute-done | bytes 110624 | tf_op jit(solution)/shard_map/ppermute | solution.py:303
  124.4 5.2 %all-to-all-done.4.terms = bf16[16,112,128]{2,1,0:T(8,128)(2,1)S(1)} async-done(((bf16[16,112,128]{2,1,0:T(8,128)(2,1)}), bf16[16,112,128]{2,1,0:T(8,128)(2,1)S(1)}, u32[]{:S(2)}, u32[]{:S(2)}) %all-to-all-start.4) | async-done | bytes 458784 | tf_op jit(solution)/shard_map/all_to_all | solution.py:399
  129.6 0.3 shard_map.65
  129.8 9.4 %all_to_all.31.came = f32[4,144,128]{2,1,0:T(8,128)S(1)} all-to-all(f32[4,144,128]{2,1,0:T(8,128)S(1)} %shard_map.65), channel_id=1, replica_groups=mesh['y'=4,'z'=16,'x'=4,'core'=2] {'y'}, dimensions={0} | all-to-all | bytes 589824 | tf_op jit(solution)/shard_map/all_to_all | solution.py:424
  139.2 0.8 shard_map.66
  (8 shorter events, 0.0 us)
Async XLA Ops:
  13.4 42.9 %copy-start = (bf16[512,384]{1,0:T(8,128)(2,1)S(1)}, bf16[512,384]{1,0:T(8,128)(2,1)}, u32[]{:S(2)}) copy-start(bf16[512,384]{1,0:T(8,128)(2,1)} %constant.24.clone.place) | copy-start | bytes 1179652
  13.4 42.9 %all-to-all-start.1 = ((bf16[8,576,128]{2,1,0:T(8,128)(2,1)}), bf16[8,576,128]{2,1,0:T(8,128)(2,1)S(1)}, u32[]{:S(2)}, u32[]{:S(2)}) async-start(bf16[8,576,128]{2,1,0:T(8,128)(2,1)} %get-tuple-element.25), calls=%async_computation.1 | async-start | bytes 2359296 | tf_op jit(solution)/shard_map/all_to_all | solution.py:338
  58.8 20.8 %all-to-all-start.2 = ((f32[16,8,128]{2,1,0:T(8,128)}), f32[16,8,128]{2,1,0:T(8,128)S(1)}, u32[]{:S(2)}, u32[]{:S(2)}) async-start(f32[16,8,128]{2,1,0:T(8,128)} %get-tuple-element.33), calls=%async_computation.2 | async-start | bytes 131072 | tf_op jit(solution)/shard_map/all_to_all | solution.py:363
  80.3 8.6 %all-to-all-start.3 = ((f32[8,16,128]{2,1,0:T(8,128)}), f32[8,16,128]{2,1,0:T(8,128)S(1)}, u32[]{:S(2)}, u32[]{:S(2)}) async-start(f32[8,16,128]{2,1,0:T(8,128)} %broadcast_in_dim.5), calls=%async_computation.3 | async-start | bytes 131072 | tf_op jit(solution)/shard_map/all_to_all | solution.py:378
  88.9 16.1 %copy-start.1 = (bf16[512,288]{1,0:T(8,128)(2,1)S(1)}, bf16[512,288]{1,0:T(8,128)(2,1)}, u32[]{:S(2)}) copy-start(bf16[512,288]{1,0:T(8,128)(2,1)} %get-tuple-element.41) | copy-start | bytes 884740
  91.1 38.5 %all-to-all-start.4 = ((bf16[16,112,128]{2,1,0:T(8,128)(2,1)}), bf16[16,112,128]{2,1,0:T(8,128)(2,1)S(1)}, u32[]{:S(2)}, u32[]{:S(2)}) async-start(bf16[16,112,128]{2,1,0:T(8,128)(2,1)} %get-tuple-element.36), calls=%async_computation.4 | async-start | bytes 917504 | tf_op jit(solution)/shard_map/all_to_all | solution.py:399
  103.1 5.7 %collective-permute-start = (bf16[576,384]{1,0:T(8,128)(2,1)S(1)}, bf16[576,384]{1,0:T(8,128)(2,1)S(1)}, u32[]{:S(2)}, u32[]{:S(2)}) collective-permute-start(bf16[576,384]{1,0:T(8,128)(2,1)S(1)} %get-tuple-element.39.dlogits), channel_id=1, source_target_pairs={{0,1},{1,0},{2,3},{3,2},{4,5},{5,4},{6,7},{7,6},{8,9},{9,8},{10,11... | collective-permute-start | bytes 1327112 | tf_op jit(solution)/shard_map/ppermute | solution.py:303
  105.0 3.7 %collective-permute-start.1 = (bf16[512,288]{1,0:T(8,128)(2,1)S(1)}, bf16[512,288]{1,0:T(8,128)(2,1)S(1)}, u32[]{:S(2)}, u32[]{:S(2)}) collective-permute-start(bf16[512,288]{1,0:T(8,128)(2,1)S(1)} %copy-done.1), channel_id=1, source_target_pairs={{0,1},{1,0},{2,3},{3,2},{4,5},{5,4},{6,7},{7,6},{8,9},{9,8},{10,11... | collective-permute-start | bytes 884744 | tf_op jit(solution)/shard_map/ppermute | solution.py:303
  110.4 9.9 %collective-permute-start.2 = (bf16[432,128]{1,0:T(8,128)(2,1)S(1)}, bf16[432,128]{1,0:T(8,128)(2,1)S(1)}, u32[]{:S(2)}, u32[]{:S(2)}) collective-permute-start(bf16[432,128]{1,0:T(8,128)(2,1)S(1)} %get-tuple-element.43), channel_id=1, source_target_pairs={{0,2},{2,4},{4,6},{6,0},{1,3},{3,5},{5,7},{7,1},{8,10},{10,12},{12... | collective-permute-start | bytes 331784 | tf_op jit(solution)/shard_map/ppermute | solution.py:303
  112.7 8.4 %collective-permute-start.3 = (bf16[432,128]{1,0:T(8,128)(2,1)S(1)}, bf16[432,128]{1,0:T(8,128)(2,1)S(1)}, u32[]{:S(2)}, u32[]{:S(2)}) collective-permute-start(bf16[432,128]{1,0:T(8,128)(2,1)S(1)} %get-tuple-element.44), channel_id=1, source_target_pairs={{0,4},{2,6},{4,0},{6,2},{1,5},{3,7},{5,1},{7,3},{8,12},{10,14},{12... | collective-permute-start | bytes 331784 | tf_op jit(solution)/shard_map/ppermute | solution.py:303
  117.7 6.7 %collective-permute-start.4 = (bf16[432,128]{1,0:T(8,128)(2,1)S(1)}, bf16[432,128]{1,0:T(8,128)(2,1)S(1)}, u32[]{:S(2)}, u32[]{:S(2)}) collective-permute-start(bf16[432,128]{1,0:T(8,128)(2,1)S(1)} %get-tuple-element.45), channel_id=1, source_target_pairs={{0,6},{2,0},{4,2},{6,4},{1,7},{3,1},{5,3},{7,5},{8,14},{10,8},{12,... | collective-permute-start | bytes 331784 | tf_op jit(solution)/shard_map/ppermute | solution.py:303

commit v12 on v10

--- a/solution.py
+++ b/solution.py
@@ -18,6 +18,7 @@
 BLOCKS = [(0, 128), (128, 128), (256, 128), (384, 128), (512, 64)]
 MSG = ROWS + 48
 QUARTER = ROWS // 4
+STEPS = (2, 1, 3)
 GROUP = 384
 NT = (((1,), (1,)), ((), ()))
 TN = (((0,), (0,)), ((), ()))
@@ -236,7 +237,7 @@
         + lax.dot_general(other_dlogits[:, :SUB], other_half[...], NT, preferred_element_type=f32)
     )
     own[...] = squeeze(total[:, pl.ds(pl.multiple_of(where[1] * 128, 128), 128)])
-    for step, out in enumerate(outs, 1):
+    for step, out in zip(STEPS, outs):
         lanes = pl.ds(pl.multiple_of(lax.rem(where[1] + step, NX) * 128, 128), 128)
         out[...] = squeeze(total[:, lanes]).astype(bf16)
 
@@ -407,7 +408,7 @@
         scratch=[pltpu.VMEM((TALL, HALF), f32)],
         flops=4 * TALL * SUB * HALF,
     )
-    came = [around(other, "x", NX, step) for step, other in enumerate(others, 1)]
+    came = [around(other, "x", NX, step) for step, other in zip(STEPS, others)]
 
     (message,) = call(
         fold_kernel,

time: 135 us -> 135 us (level)
  no operation moved by 1% of the time
where the time goes in v12:
time: 135 us
  blocking collectives  66.9 us (50%)
  starting transfers between devices  45 us (33%)
  Pallas kernels  11 us (8%)
  waiting for transfers between devices  11 us (8%)
    all_gather x1, blocking collectives, body(): passage_part = lax.all_gather(passage_part, 'z')  35 us
    all_to_all x2, blocking collectives, body(): message = lax.all_to_all(message, 'y', 0, 0, tiled=True)  20 us
    ppermute x5, starting transfers between devices, around(): return lax.ppermute(x, axis, [(i, (i + step) % n) for i in range(n)])  14.6 us
    all_to_all x1, starting transfers between devices, body(): terms = lax.all_to_all(terms, 'z', 0, 0, tiled=True)  12 us
    all_gather x1, blocking collectives, body(): row_pairs = lax.all_gather(merge(row_pairs), 'y')  11.9 us
    pallas_call x8, Pallas kernels, call(): pl.pallas_call(kernel, out_shape=[pltpu.HBM(o.shape, o.dtype) if i in far...  11 us
    all_to_all x1, starting transfers between devices, body(): col_pairs = lax.all_to_all(col_pairs, 'z', 0, 0, tiled=True)  9.37 us
    all_to_all x1, waiting for transfers between devices, body(): terms = lax.all_to_all(terms, 'z', 0, 0, tiled=True)  5.02 us
  transfers between devices with their start and end apart: 9, of which 5 were waited for; matrix products, arithmetic and copies ran while one was open for 0% of the time, Pallas kernels for 2%

profile of v12, /device:TPU:64, one launch (start us, length us, event | category | flops | bytes accessed | tf_op | source)
XLA Modules:
  0.0 134.8 jit_solution(12882706495771588673)
XLA Ops:
  0.6 1.1 shard_map.59
  1.7 10.6 %all_to_all.30.came = bf16[4,192,128]{2,1,0:T(8,128)(2,1)S(1)} all-to-all(bf16[4,192,128]{2,1,0:T(8,128)(2,1)S(1)} %shard_map.59), channel_id=1, replica_groups=mesh['y'=4,'z'=16,'x'=4,'core'=2] {'y'}, dimensions={0} | all-to-all | bytes 393216 | tf_op jit(solution)/shard_map/all_to_all | solution.py:326
  12.3 1.1 shard_map.60
  13.4 0.0 copy-start
  13.4 4.4 %all-to-all-start.1 = ((bf16[8,576,128]{2,1,0:T(8,128)(2,1)}), bf16[8,576,128]{2,1,0:T(8,128)(2,1)S(1)}, u32[]{:S(2)}, u32[]{:S(2)}) async-start(bf16[8,576,128]{2,1,0:T(8,128)(2,1)} %get-tuple-element.23), calls=%async_computation.1 | async-start | bytes 2359296 | tf_op jit(solution)/shard_map/all_to_all | solution.py:338
  17.9 35.0 %all-gather = bf16[1792,128]{1,0:T(8,128)(2,1)S(1)} all-gather(bf16[112,128]{1,0:T(8,128)(2,1)S(1)} %get-tuple-element.24), channel_id=2, replica_groups=mesh['y'=4,'z'=16,'x'=4,'core'=2] {'z'}, dimensions={0}, use_global_device_ids=true | all-gather | bytes 487424 | tf_op jit(solution)/shard_map/all_gather | solution.py:339
  52.9 0.0 all-to-all-done.1.parts
  52.9 2.7 %shard_map.61 = (bf16[768,288]{1,0:T(8,128)(2,1)S(1)}, f32[8,16,128]{2,1,0:T(8,128)}, f32[16,8,128]{2,1,0:T(8,128)}, bf16[576,768]{1,0:T(8,128)(2,1)S(1)}, f32[8,128]{1,0:T(8,128)S(1)}) custom-call(bf16[8,576,128]{2,1,0:T(8,128)(2,1)S(1)} %all-to-all-done.1.parts, bf16[16,112,128]{2,1,0:T(8,128)(2,1)S(1)} %bitcast.7, bf16[512,384]{1,0:T(8,128)(2,1)S(1)} %copy-done), custom_call_target="tpu_custom_call" | custom-call | flops 339738624 | bytes 3493888 | tf_op jit(solution)/shard_map/pallas_call | solution.py:30
  55.7 4.6 %all-to-all-start.2 = ((f32[8,16,128]{2,1,0:T(8,128)}), f32[8,16,128]{2,1,0:T(8,128)S(1)}, u32[]{:S(2)}, u32[]{:S(2)}) async-start(f32[8,16,128]{2,1,0:T(8,128)} %get-tuple-element.30), calls=%async_computation.2 | async-start | bytes 131072 | tf_op jit(solution)/shard_map/all_to_all | solution.py:375
  60.3 0.1 pad_add_fusion.where
  60.3 1.2 shard_map.62
  61.5 2.4 %collective-permute-start = (bf16[512,288]{1,0:T(8,128)(2,1)S(1)}, bf16[512,288]{1,0:T(8,128)(2,1)S(1)}, u32[]{:S(2)}, u32[]{:S(2)}) collective-permute-start(bf16[512,288]{1,0:T(8,128)(2,1)S(1)} %get-tuple-element.28), channel_id=1, source_target_pairs={{0,1},{1,0},{2,3},{3,2},{4,5},{5,4},{6,7},{7,6},{8,9},{9,8},{10,11... | collective-permute-start | bytes 884744 | tf_op jit(solution)/shard_map/ppermute | solution.py:303
  64.0 1.9 %all-to-all-done.2 = f32[8,16,128]{2,1,0:T(8,128)S(1)} async-done(((f32[8,16,128]{2,1,0:T(8,128)}), f32[8,16,128]{2,1,0:T(8,128)S(1)}, u32[]{:S(2)}, u32[]{:S(2)}) %all-to-all-start.2) | async-done | bytes 65568 | tf_op jit(solution)/shard_map/all_to_all | solution.py:375
  65.9 9.4 %all-to-all-start.3 = ((f32[16,8,128]{2,1,0:T(8,128)}), f32[16,8,128]{2,1,0:T(8,128)S(1)}, u32[]{:S(2)}, u32[]{:S(2)}) async-start(f32[16,8,128]{2,1,0:T(8,128)} %get-tuple-element.33), calls=%async_computation.3 | async-start | bytes 131072 | tf_op jit(solution)/shard_map/all_to_all | solution.py:376
  75.3 11.9 %all-gather.1 = f32[64,128]{1,0:T(8,128)S(1)} all-gather(f32[16,128]{1,0:T(8,128)S(1)} %pad_maximum_fusion), channel_id=3, replica_groups=mesh['y'=4,'z'=16,'x'=4,'core'=2] {'y'}, dimensions={0}, use_global_device_ids=true | all-gather | bytes 40960 | tf_op jit(solution)/shard_map/all_gather | solution.py:377
  87.2 0.0 collective-permute-done.other_half
  87.2 0.0 all-to-all-done.3.col_pairs
  87.2 2.3 %shard_map.63 = (bf16[576,384]{1,0:T(8,128)(2,1)S(1)}, bf16[16,112,128]{2,1,0:T(8,128)(2,1)}) custom-call(bf16[576,768]{1,0:T(8,128)(2,1)S(1)} %get-tuple-element.25.placed, bf16[768,288]{1,0:T(8,128)(2,1)S(1)} %get-tuple-element.26.passages, f32[8,128]{1,0:T(8,128)S(1)} %get-tuple-element.29.targets, f32[1,288]{1,0:T(1,128)S(1)} %add_convert_fusion.ids, ...), custom_call_target="tpu_custom_call" | custom-call | flops 254803968 | bytes 2331776 | tf_op jit(solution)/shard_map/pallas_call | solution.py:30
  89.5 12.0 %all-to-all-start.4 = ((bf16[16,112,128]{2,1,0:T(8,128)(2,1)}), bf16[16,112,128]{2,1,0:T(8,128)(2,1)S(1)}, u32[]{:S(2)}, u32[]{:S(2)}) async-start(bf16[16,112,128]{2,1,0:T(8,128)(2,1)} %get-tuple-element.34), calls=%async_computation.4 | async-start | bytes 917504 | tf_op jit(solution)/shard_map/all_to_all | solution.py:398
  101.5 1.9 %collective-permute-start.1 = (bf16[576,384]{1,0:T(8,128)(2,1)S(1)}, bf16[576,384]{1,0:T(8,128)(2,1)S(1)}, u32[]{:S(2)}, u32[]{:S(2)}) collective-permute-start(bf16[576,384]{1,0:T(8,128)(2,1)S(1)} %get-tuple-element.35.dlogits), channel_id=1, source_target_pairs={{0,1},{1,0},{2,3},{3,2},{4,5},{5,4},{6,7},{7,6},{8,9},{9,8},{10,11... | collective-permute-start | bytes 1327112 | tf_op jit(solution)/shard_map/ppermute | solution.py:303
  103.4 1.8 %collective-permute-done.1.other_dlogits = bf16[576,384]{1,0:T(8,128)(2,1)S(1)} collective-permute-done((bf16[576,384]{1,0:T(8,128)(2,1)S(1)}, bf16[576,384]{1,0:T(8,128)(2,1)S(1)}, u32[]{:S(2)}, u32[]{:S(2)}) %collective-permute-start.1) | collective-permute-done | bytes 442400 | tf_op jit(solution)/shard_map/ppermute | solution.py:303
  105.2 1.6 %shard_map.64 = (f32[432,128]{1,0:T(8,128)S(1)}, bf16[432,128]{1,0:T(8,128)(2,1)S(1)}, bf16[432,128]{1,0:T(8,128)(2,1)S(1)}, bf16[432,128]{1,0:T(8,128)(2,1)S(1)}) custom-call(s32[2]{0:T(128)S(1)} %pad_add_fusion.where, bf16[576,384]{1,0:T(8,128)(2,1)S(1)} %get-tuple-element.35.dlogits, bf16[576,384]{1,0:T(8,128)(2,1)S(1)} %collective-permute-done.1.other_dlogits, ...), custom_call_target="tpu_custom_call" | custom-call | flops 339738624 | bytes 2027528 | tf_op jit(solution)/shard_map/pallas_call | solution.py:30
  106.8 3.2 %collective-permute-start.2 = (bf16[432,128]{1,0:T(8,128)(2,1)S(1)}, bf16[432,128]{1,0:T(8,128)(2,1)S(1)}, u32[]{:S(2)}, u32[]{:S(2)}) collective-permute-start(bf16[432,128]{1,0:T(8,128)(2,1)S(1)} %get-tuple-element.39), channel_id=1, source_target_pairs={{0,4},{2,6},{4,0},{6,2},{1,5},{3,7},{5,1},{7,3},{8,12},{10,14},{12... | collective-permute-start | bytes 331784 | tf_op jit(solution)/shard_map/ppermute | solution.py:303
  110.0 2.7 %collective-permute-start.3 = (bf16[432,128]{1,0:T(8,128)(2,1)S(1)}, bf16[432,128]{1,0:T(8,128)(2,1)S(1)}, u32[]{:S(2)}, u32[]{:S(2)}) collective-permute-start(bf16[432,128]{1,0:T(8,128)(2,1)S(1)} %get-tuple-element.40), channel_id=1, source_target_pairs={{0,2},{2,4},{4,6},{6,0},{1,3},{3,5},{5,7},{7,1},{8,10},{10,12},{12... | collective-permute-start | bytes 331784 | tf_op jit(solution)/shard_map/ppermute | solution.py:303
  112.6 4.4 %collective-permute-start.4 = (bf16[432,128]{1,0:T(8,128)(2,1)S(1)}, bf16[432,128]{1,0:T(8,128)(2,1)S(1)}, u32[]{:S(2)}, u32[]{:S(2)}) collective-permute-start(bf16[432,128]{1,0:T(8,128)(2,1)S(1)} %get-tuple-element.41), channel_id=1, source_target_pairs={{0,6},{2,0},{4,2},{6,4},{1,7},{3,1},{5,3},{7,5},{8,14},{10,8},{12,... | collective-permute-start | bytes 331784 | tf_op jit(solution)/shard_map/ppermute | solution.py:303
  117.0 0.0 collective-permute-done.2.rest_0_
  117.1 0.8 collective-permute-done.3.rest_1_
  117.9 1.5 %collective-permute-done.4.rest_2_ = bf16[432,128]{1,0:T(8,128)(2,1)S(1)} collective-permute-done((bf16[432,128]{1,0:T(8,128)(2,1)S(1)}, bf16[432,128]{1,0:T(8,128)(2,1)S(1)}, u32[]{:S(2)}, u32[]{:S(2)}) %collective-permute-start.4) | collective-permute-done | bytes 110624 | tf_op jit(solution)/shard_map/ppermute | solution.py:303
  119.4 5.0 %all-to-all-done.4.terms = bf16[16,112,128]{2,1,0:T(8,128)(2,1)S(1)} async-done(((bf16[16,112,128]{2,1,0:T(8,128)(2,1)}), bf16[16,112,128]{2,1,0:T(8,128)(2,1)S(1)}, u32[]{:S(2)}, u32[]{:S(2)}) %all-to-all-start.4) | async-done | bytes 458784 | tf_op jit(solution)/shard_map/all_to_all | solution.py:398
  124.4 0.3 shard_map.65
  124.6 9.4 %all_to_all.31.came = f32[4,144,128]{2,1,0:T(8,128)S(1)} all-to-all(f32[4,144,128]{2,1,0:T(8,128)S(1)} %shard_map.65), channel_id=1, replica_groups=mesh['y'=4,'z'=16,'x'=4,'core'=2] {'y'}, dimensions={0} | all-to-all | bytes 589824 | tf_op jit(solution)/shard_map/all_to_all | solution.py:421
  134.0 0.8 shard_map.66
  (5 shorter events, 0.0 us)
Async XLA Ops:
  13.4 39.5 %copy-start = (bf16[512,384]{1,0:T(8,128)(2,1)S(1)}, bf16[512,384]{1,0:T(8,128)(2,1)}, u32[]{:S(2)}) copy-start(bf16[512,384]{1,0:T(8,128)(2,1)} %constant.24.clone.place) | copy-start | bytes 1179652
  13.4 39.5 %all-to-all-start.1 = ((bf16[8,576,128]{2,1,0:T(8,128)(2,1)}), bf16[8,576,128]{2,1,0:T(8,128)(2,1)S(1)}, u32[]{:S(2)}, u32[]{:S(2)}) async-start(bf16[8,576,128]{2,1,0:T(8,128)(2,1)} %get-tuple-element.23), calls=%async_computation.1 | async-start | bytes 2359296 | tf_op jit(solution)/shard_map/all_to_all | solution.py:338
  55.7 10.2 %all-to-all-start.2 = ((f32[8,16,128]{2,1,0:T(8,128)}), f32[8,16,128]{2,1,0:T(8,128)S(1)}, u32[]{:S(2)}, u32[]{:S(2)}) async-start(f32[8,16,128]{2,1,0:T(8,128)} %get-tuple-element.30), calls=%async_computation.2 | async-start | bytes 131072 | tf_op jit(solution)/shard_map/all_to_all | solution.py:375
  61.5 25.7 %collective-permute-start = (bf16[512,288]{1,0:T(8,128)(2,1)S(1)}, bf16[512,288]{1,0:T(8,128)(2,1)S(1)}, u32[]{:S(2)}, u32[]{:S(2)}) collective-permute-start(bf16[512,288]{1,0:T(8,128)(2,1)S(1)} %get-tuple-element.28), channel_id=1, source_target_pairs={{0,1},{1,0},{2,3},{3,2},{4,5},{5,4},{6,7},{7,6},{8,9},{9,8},{10,11... | collective-permute-start | bytes 884744 | tf_op jit(solution)/shard_map/ppermute | solution.py:303
  65.9 21.3 %all-to-all-start.3 = ((f32[16,8,128]{2,1,0:T(8,128)}), f32[16,8,128]{2,1,0:T(8,128)S(1)}, u32[]{:S(2)}, u32[]{:S(2)}) async-start(f32[16,8,128]{2,1,0:T(8,128)} %get-tuple-element.33), calls=%async_computation.3 | async-start | bytes 131072 | tf_op jit(solution)/shard_map/all_to_all | solution.py:376
  89.5 34.9 %all-to-all-start.4 = ((bf16[16,112,128]{2,1,0:T(8,128)(2,1)}), bf16[16,112,128]{2,1,0:T(8,128)(2,1)S(1)}, u32[]{:S(2)}, u32[]{:S(2)}) async-start(bf16[16,112,128]{2,1,0:T(8,128)(2,1)} %get-tuple-element.34), calls=%async_computation.4 | async-start | bytes 917504 | tf_op jit(solution)/shard_map/all_to_all | solution.py:398
  101.5 3.7 %collective-permute-start.1 = (bf16[576,384]{1,0:T(8,128)(2,1)S(1)}, bf16[576,384]{1,0:T(8,128)(2,1)S(1)}, u32[]{:S(2)}, u32[]{:S(2)}) collective-permute-start(bf16[576,384]{1,0:T(8,128)(2,1)S(1)} %get-tuple-element.35.dlogits), channel_id=1, source_target_pairs={{0,1},{1,0},{2,3},{3,2},{4,5},{5,4},{6,7},{7,6},{8,9},{9,8},{10,11... | collective-permute-start | bytes 1327112 | tf_op jit(solution)/shard_map/ppermute | solution.py:303
  106.8 10.3 %collective-permute-start.2 = (bf16[432,128]{1,0:T(8,128)(2,1)S(1)}, bf16[432,128]{1,0:T(8,128)(2,1)S(1)}, u32[]{:S(2)}, u32[]{:S(2)}) collective-permute-start(bf16[432,128]{1,0:T(8,128)(2,1)S(1)} %get-tuple-element.39), channel_id=1, source_target_pairs={{0,4},{2,6},{4,0},{6,2},{1,5},{3,7},{5,1},{7,3},{8,12},{10,14},{12... | collective-permute-start | bytes 331784 | tf_op jit(solution)/shard_map/ppermute | solution.py:303
  110.0 7.9 %collective-permute-start.3 = (bf16[432,128]{1,0:T(8,128)(2,1)S(1)}, bf16[432,128]{1,0:T(8,128)(2,1)S(1)}, u32[]{:S(2)}, u32[]{:S(2)}) collective-permute-start(bf16[432,128]{1,0:T(8,128)(2,1)S(1)} %get-tuple-element.40), channel_id=1, source_target_pairs={{0,2},{2,4},{4,6},{6,0},{1,3},{3,5},{5,7},{7,1},{8,10},{10,12},{12... | collective-permute-start | bytes 331784 | tf_op jit(solution)/shard_map/ppermute | solution.py:303
  112.6 6.7 %collective-permute-start.4 = (bf16[432,128]{1,0:T(8,128)(2,1)S(1)}, bf16[432,128]{1,0:T(8,128)(2,1)S(1)}, u32[]{:S(2)}, u32[]{:S(2)}) collective-permute-start(bf16[432,128]{1,0:T(8,128)(2,1)S(1)} %get-tuple-element.41), channel_id=1, source_target_pairs={{0,6},{2,0},{4,2},{6,4},{1,7},{3,1},{5,3},{7,5},{8,14},{10,8},{12,... | collective-permute-start | bytes 331784 | tf_op jit(solution)/shard_map/ppermute | solution.py:303
